TPU v7x, 32 devices: a whole 2x2x4 slice. The times are simulated.
32 devices in a mesh: dp: 4 (over y, x), expert: 8 (over z, core).
Axes of the slice: x: 2, y: 2, z: 4, core: 2. Of those that a mesh axis runs over, the one named last changes fastest.
Arguments:
- tokens: bfloat16 [2048, 2048], P('dp'), may hold values from -6 to 6
- routes: int32 [2048, 6], P('dp'), may hold values from 0 to 7, all different within a row; in each aligned block of 512 rows (0 to 511, 512 to 1023, ...) at most 512 rows name the same one
- route_weight: float32 [2048, 6], P('dp'), may hold values from 0.05 to 0.5
- w_gate: bfloat16 [32, 352, 2048], P(('dp', 'expert')), may hold values from -0.125 to 0.125
- w_up: bfloat16 [32, 352, 2048], P(('dp', 'expert')), may hold values from -0.125 to 0.125
- w_down: bfloat16 [32, 352, 2048], P(('dp', 'expert')), may hold values from -0.15625 to 0.15625
- grad_out: bfloat16 [2048, 2048], P(('dp', 'expert')), may hold values from -6 to 6
Outputs:
- mixed: bfloat16 [2048, 2048], P(('dp', 'expert'))
- grad_tokens: bfloat16 [2048, 2048], P(('dp', 'expert'))
- grad_route_weight: float32 [2048, 6], P(('dp', 'expert'))
- grad_gate: bfloat16 [32, 352, 2048], P(('dp', 'expert'))
- grad_up: bfloat16 [32, 352, 2048], P(('dp', 'expert'))
- grad_down: bfloat16 [32, 352, 2048], P(('dp', 'expert'))
Inputs may be any that keep to these rules, and one draw needn't show every extreme that they name: `routes`: each row names 6 different experts. Within the 512 rows of one index of dp no expert is named by more than 512 rows.
All inputs are finite; a program needn't handle non-finite values.
Results may differ from a plain program's by a relative error of at most 0.023.
Values may be sent and summed in bfloat16 or wider, within the bound.
No kernel may reach another device: no remote copies, remote signals or barrier semaphores. Data moves between devices by JAX's collectives and lax.ppermute only.
A program may use at most 192 MiB of HBM per device.

v0:
```python
import jax
import jax.numpy as jnp
from jax import lax
from jax.sharding import PartitionSpec as P

SHARDS = 4


def silu_parts(gate_pre):
    sigma = jax.nn.sigmoid(gate_pre)
    return (gate_pre * sigma, sigma * (1.0 + gate_pre * (1.0 - sigma)))


def deliver(buffer):
    dp_count, slot_count, width = buffer.shape
    arrived = lax.all_to_all(buffer, "dp", split_axis=0, concat_axis=0, tiled=True)
    return arrived.reshape(dp_count * slot_count, width)


def send_back(rows, dp_count, slot_count):
    width = rows.shape[1]
    returned = lax.all_to_all(
        rows.reshape(dp_count, slot_count, width), "dp", split_axis=0, concat_axis=0, tiled=True
    )
    return (returned.reshape(dp_count * slot_count, width), jnp.zeros((), jnp.int32))


def body(tokens, routes, route_weight, w_gate, w_up, w_down, grad_out):
    dp_count = lax.axis_size("dp")
    ex_count = lax.axis_size("expert")
    groups = ex_count // SHARDS
    my_group = lax.axis_index("expert") // SHARDS
    tok_rows, top_count = routes.shape
    width = tokens.shape[1]
    expert_count = dp_count * groups
    capacity = min(tok_rows, 3 * tok_rows * top_count // (2 * expert_count))
    flat_routes = routes.reshape(-1)
    route_count = flat_routes.shape[0]
    owner_ids = jnp.arange(dp_count, dtype=jnp.int32) * groups + my_group
    hit_table = (flat_routes[:, None] == owner_ids[None, :]).astype(jnp.int32)
    is_live = jnp.sum(hit_table, axis=1)
    owner_dp = jnp.sum(hit_table * jnp.arange(dp_count, dtype=jnp.int32)[None, :], axis=1)
    slot_index = jnp.sum((jnp.cumsum(hit_table, axis=0) - 1) * hit_table, axis=1)
    dump_row = dp_count * capacity
    target = jnp.where(is_live == 1, owner_dp * capacity + slot_index, dump_row)
    source = (
        jnp.full((dump_row + 1,), route_count, jnp.int32)
        .at[target]
        .set(jnp.arange(route_count, dtype=jnp.int32))[:dump_row]
    )
    filled = source < route_count
    safe_source = jnp.where(filled, source, 0)
    token_of = safe_source // top_count
    weights_flat = route_weight.reshape(-1)
    send_rows = jnp.where(filled[:, None], tokens[token_of], jnp.zeros((), tokens.dtype))
    x_rows = deliver(send_rows.reshape(dp_count, capacity, width))
    gate_matrix = w_gate[0]
    up_matrix = w_up[0]
    down_matrix = w_down[0]
    gate_pre = jnp.einsum("rd,fd->rf", x_rows, gate_matrix, preferred_element_type=jnp.float32)
    up_pre = jnp.einsum("rd,fd->rf", x_rows, up_matrix, preferred_element_type=jnp.float32)
    silu_value, silu_slope = silu_parts(gate_pre)
    hidden = (silu_value * up_pre).astype(jnp.bfloat16)
    shard_part = jnp.dot(hidden, down_matrix, preferred_element_type=jnp.float32).astype(
        jnp.bfloat16
    )
    returned, offset = send_back(shard_part, dp_count, capacity)
    piece_width = returned.shape[1]
    safe_target = jnp.where(is_live == 1, target, 0)
    route_part = jnp.where(
        is_live[:, None] == 1, returned[safe_target], jnp.zeros((), returned.dtype)
    )
    weighted = weights_flat[:, None] * route_part.astype(jnp.float32)
    mixed_part = jnp.sum(weighted.reshape(tok_rows, top_count, piece_width), axis=1)
    cotangent = lax.all_gather(grad_out, "expert", axis=0, tiled=True)
    route_grad = jnp.sum(
        route_part.reshape(tok_rows, top_count, piece_width).astype(jnp.float32)
        * cotangent[:, None, :].astype(jnp.float32),
        axis=2,
    )
    weight_of = jnp.where(filled, weights_flat[safe_source], jnp.zeros((), weights_flat.dtype))
    send_cot = (weight_of[:, None] * cotangent[token_of].astype(jnp.float32)).astype(jnp.bfloat16)
    cot_rows = deliver(send_cot.reshape(dp_count, capacity, width))
    d_hidden = jnp.einsum("rd,fd->rf", cot_rows, down_matrix, preferred_element_type=jnp.float32)
    d_gate = (d_hidden * up_pre * silu_slope).astype(jnp.bfloat16)
    d_up = (d_hidden * silu_value).astype(jnp.bfloat16)
    grad_down = jnp.einsum(
        "rf,rd->fd", hidden, cot_rows, preferred_element_type=jnp.float32
    ).astype(jnp.bfloat16)[None]
    grad_gate = jnp.einsum("rf,rd->fd", d_gate, x_rows, preferred_element_type=jnp.float32).astype(
        jnp.bfloat16
    )[None]
    grad_up = jnp.einsum("rf,rd->fd", d_up, x_rows, preferred_element_type=jnp.float32).astype(
        jnp.bfloat16
    )[None]
    shard_dx = jnp.dot(d_gate, gate_matrix, preferred_element_type=jnp.float32) + jnp.dot(
        d_up, up_matrix, preferred_element_type=jnp.float32
    )
    dx_back, dx_offset = send_back(shard_dx.astype(jnp.bfloat16), dp_count, capacity)
    route_dx = jnp.where(is_live[:, None] == 1, dx_back[safe_target], jnp.zeros((), dx_back.dtype))
    dx_part = jnp.sum(
        route_dx.astype(jnp.float32).reshape(tok_rows, top_count, piece_width), axis=1
    )
    mixed, grad_tokens, grad_route = (
        lax.psum_scatter(
            mixed_part.astype(jnp.bfloat16), "expert", scatter_dimension=0, tiled=True
        ).astype(jnp.float32),
        lax.psum_scatter(
            dx_part.astype(jnp.bfloat16), "expert", scatter_dimension=0, tiled=True
        ).astype(jnp.float32),
        lax.psum_scatter(
            route_grad.astype(jnp.bfloat16), "expert", scatter_dimension=0, tiled=True
        ).astype(jnp.float32),
    )
    return (
        mixed.astype(jnp.bfloat16),
        grad_tokens.astype(jnp.bfloat16),
        grad_route,
        grad_gate,
        grad_up,
        grad_down,
    )


def solution(mesh):
    return jax.shard_map(
        body,
        mesh=mesh,
        in_specs=(
            P("dp", None),
            P("dp", None),
            P("dp", None),
            P(("dp", "expert"), None, None),
            P(("dp", "expert"), None, None),
            P(("dp", "expert"), None, None),
            P(("dp", "expert"), None),
        ),
        out_specs=(
            P(("dp", "expert"), None),
            P(("dp", "expert"), None),
            P(("dp", "expert"), None),
            P(("dp", "expert"), None, None),
            P(("dp", "expert"), None, None),
            P(("dp", "expert"), None, None),
        ),
        check_vma=False,
    )
```

profile of v0, /device:TPU:0, one launch (start us, length us, event | category | flops | bytes accessed | tf_op | source)
XLA Modules:
  0.0 625.2 jit_solution(7457490427736226353)
XLA Ops:
  7.2 0.0 copy-start
  7.2 1.0 copy.15
  8.2 0.2 eq.61
  8.4 0.2 eq.54
  8.6 0.1 compare_convert_fusion.1
  8.6 1.1 reduce-window.6
  9.8 0.2 slice_reduce_fusion
  10.0 0.2 reduce-window.9
  10.2 0.1 add_bitcast_fusion
  10.3 0.2 fusion.15
  10.5 0.6 compare_select_fusion
  11.1 11.8 %scatter_custom_fusion = s32[2049]{0:T(1024)S(1)} fusion(s32[3072]{0:T(1024)S(1)} %bitcast.65, s32[3072]{0:T(1024)S(1)} %iota.13, s32[]{:T(128)} %constant.28.clone.1), kind=kCustom, calls=%fused_computation.61 | custom fusion | bytes 8200 | tf_op jit(solution)/shard_map/scatter | solution.py:49
  23.0 11.0 %gather_fusion = bf16[2048,2048]{1,0:T(8,128)(2,1)} fusion(bf16[512,2048]{1,0:T(8,128)(2,1)S(1)} %copy-done, s32[2048]{0:T(1024)S(1)} %fusion.18), kind=kCustom, calls=%fused_computation | custom fusion | bytes 16785408 | tf_op jit(solution)/shard_map/gather | solution.py:55
  34.0 7.2 %broadcast_select_fusion = bf16[4,512,2048]{2,1,0:T(8,128)(2,1)} fusion(bf16[4,512,2048]{2,1,0:T(8,128)(2,1)} %bitcast.60, pred[4,512]{1,0:T(4,128)(4,1)S(1)} %lt.38), kind=kLoop, calls=%fused_computation.12 | loop fusion | flops 4194304 | bytes 16779264 | tf_op jit(solution)/shard_map/jit(_where)/select_n | solution.py:55
  41.3 5.8 all-to-all-start
  47.0 0.0 all-gather.2.cloned.1.call-start
  47.1 0.7 all-gather.2.cloned.1.call-update
  47.8 0.1 copy.14
  47.9 0.0 copy-start.5
  48.0 0.2 reshape.199
  48.1 11.8 %gather_fusion.2 = f32[2048]{0:T(1024)S(1)} fusion(f32[3072]{0:T(1024)S(1)} %reshape.199, s32[2048]{0:T(1024)S(1)} %get-tuple-element.15), kind=kCustom, calls=%fused_computation.2 | custom fusion | bytes 24576 | tf_op jit(solution)/shard_map/gather | solution.py:81
  60.0 21.8 %all-gather.2.cloned.1.call-done = bf16[512,2048]{1,0:T(8,128)(2,1)} async-done(((bf16[64,2048]{1,0:T(8,128)(2,1)}), bf16[512,2048]{1,0:T(8,128)(2,1)}) %all-gather.2.cloned.1.call-update) | async-done | bytes 2097168 | tf_op jit(solution)/shard_map/all_gather | solution.py:75
  81.7 18.2 %gather_fusion.3 = bf16[2048,2048]{1,0:T(8,128)(2,1)} fusion(bf16[512,2048]{1,0:T(8,128)(2,1)} %all-gather.2.cloned.1.call-done, s32[2048]{0:T(1024)S(1)} %fusion.18), kind=kCustom, calls=%fused_computation.3 | custom fusion | bytes 16785408 | tf_op jit(solution)/shard_map/gather | solution.py:82
  99.9 8.0 %fusion = bf16[4,512,2048]{2,1,0:T(8,128)(2,1)} fusion(bf16[4,512,2048]{2,1,0:T(8,128)(2,1)} %bitcast.61, f32[4,512]{1,0:T(4,128)S(1)} %broadcast_select_fusion.1), kind=kLoop, calls=%fused_computation.9 | loop fusion | flops 12582912 | bytes 16785408 | tf_op jit(solution)/shard_map/convert_element_type | solution.py:82
  108.0 32.9 %all-to-all-done = bf16[4,512,2048]{2,1,0:T(8,128)(2,1)} async-done(((bf16[4,512,2048]{2,1,0:T(8,128)(2,1)}), bf16[4,512,2048]{2,1,0:T(8,128)(2,1)}, u32[]{:S(2)}, u32[]{:S(2)}) %all-to-all-start) | async-done | bytes 8388640 | tf_op jit(solution)/shard_map/all_to_all | solution.py:16
  140.9 5.8 all-to-all-start.2
  146.7 0.0 copy-start.9
  146.8 8.3 %fusion.9 = f32[2048,352]{0,1:T(8,128)} fusion(bf16[2048,2048]{1,0:T(8,128)(2,1)} %bitcast.4, bf16[1,352,2048]{2,1,0:T(8,128)(2,1)S(1)} %copy-done.7), kind=kOutput, calls=%fused_computation.29 | convolution fusion | flops 2952790016 | bytes 12713984 | tf_op jit(solution)/shard_map/rd,fd->rf/dot_general | solution.py:61
  155.0 8.2 %fusion.13 = f32[2048,352]{0,1:T(8,128)} fusion(bf16[2048,2048]{1,0:T(8,128)(2,1)} %bitcast.4, bf16[1,352,2048]{2,1,0:T(8,128)(2,1)S(1)} %copy-done.9), kind=kOutput, calls=%fused_computation.33 | convolution fusion | flops 2952790016 | bytes 12713984 | tf_op jit(solution)/shard_map/rd,fd->rf/dot_general | solution.py:60
  163.3 75.5 %all-to-all-done.2 = bf16[4,512,2048]{2,1,0:T(8,128)(2,1)} async-done(((bf16[4,512,2048]{2,1,0:T(8,128)(2,1)}), bf16[4,512,2048]{2,1,0:T(8,128)(2,1)}, u32[]{:S(2)}, u32[]{:S(2)}) %all-to-all-start.2) | async-done | bytes 8388640 | tf_op jit(solution)/shard_map/all_to_all | solution.py:16
  238.8 9.7 %multiply_convert_fusion = (bf16[2048,352]{0,1:T(8,128)(2,1)S(1)}, bf16[2048,352]{0,1:T(8,128)(2,1)S(1)}, bf16[2048,352]{0,1:T(8,128)(2,1)S(1)}) fusion(f32[2048,352]{0,1:T(8,128)} %fusion.13, f32[2048,352]{0,1:T(8,128)} %fusion.9, bf16[2048,2048]{1,0:T(8,128)(2,1)} %bitcast.12, bf16[1,352,2048]{2,1,0:T(8,128)(2,1)} %param.12), kind=kOutput, calls=%fused_computation.14 | convolution fusion | flops 2963603456 | bytes 19922944 | tf_op jit(solution)/shard_map/rd,fd->rf/dot_general | solution.py:84
  248.5 0.0 copy-start.13
  248.5 0.0 copy-start.3
  248.5 6.9 %convolution_convert_fusion = bf16[2048,2048]{1,0:T(8,128)(2,1)} fusion(bf16[2048,352]{0,1:T(8,128)(2,1)S(1)} %get-tuple-element.19, bf16[1,352,2048]{2,1,0:T(8,128)(2,1)S(1)} %copy-done.12), kind=kOutput, calls=%fused_computation.13 | convolution fusion | flops 2956984320 | bytes 11272192 | tf_op jit(solution)/shard_map/dot_general | solution.py:64
  255.4 5.9 all-to-all-start.1
  261.2 9.6 %fusion.11 = f32[2048,2048]{1,0:T(8,128)} fusion(bf16[2048,352]{0,1:T(8,128)(2,1)S(1)} %get-tuple-element.18, bf16[1,352,2048]{2,1,0:T(8,128)(2,1)} %param.10), kind=kOutput, calls=%fused_computation.31 | convolution fusion | flops 2952790016 | bytes 19660800 | tf_op jit(solution)/shard_map/dot_general | solution.py:96
  270.8 10.2 %add_convert_fusion = bf16[2048,2048]{1,0:T(8,128)(2,1)} fusion(f32[2048,2048]{1,0:T(8,128)} %fusion.11, bf16[2048,352]{0,1:T(8,128)(2,1)S(1)} %get-tuple-element.17, bf16[1,352,2048]{2,1,0:T(8,128)(2,1)S(1)} %copy-done.8), kind=kOutput, calls=%fused_computation.11 | convolution fusion | flops 2961178624 | bytes 28049408 | tf_op jit(solution)/shard_map/dot_general | solution.py:96
  281.0 72.0 %all-to-all-done.1 = bf16[4,512,2048]{2,1,0:T(8,128)(2,1)} async-done(((bf16[4,512,2048]{2,1,0:T(8,128)(2,1)}), bf16[4,512,2048]{2,1,0:T(8,128)(2,1)}, u32[]{:S(2)}, u32[]{:S(2)}) %all-to-all-start.1) | async-done | bytes 8388640 | tf_op jit(solution)/shard_map/all_to_all | solution.py:22
  353.0 5.8 all-to-all-start.3
  358.9 0.0 reduce-scatter.8.cloned.1.call-start
  358.9 0.9 eq.59
  359.8 0.7 broadcast_clamp_fusion
  360.5 11.3 %mul.105 = f32[512,6,2048]{2,1,0:T(8,128)} broadcast(bf16[512,2048]{1,0:T(8,128)(2,1)S(1)} %copy-done.2), dimensions={0,2} | broadcast | bytes 27262976 | tf_op jit(solution)/shard_map/mul | solution.py:77
  371.8 29.5 %mul.106 = f32[3072,2048]{1,0:T(8,128)} reshape(f32[512,6,2048]{2,1,0:T(8,128)} %mul.105) | data formatting | bytes 50331648 | tf_op jit(solution)/shard_map/mul | solution.py:77
  401.3 28.3 %gather_fusion.1 = bf16[3072,2048]{1,0:T(8,128)(2,1)} fusion(bf16[2048,2048]{1,0:T(8,128)(2,1)} %bitcast.9, s32[3072]{0:T(1024)S(1)} %broadcast_clamp_fusion), kind=kCustom, calls=%fused_computation.1 | custom fusion | bytes 25178112 | tf_op jit(solution)/shard_map/gather | solution.py:71
  429.6 21.1 %all-to-all-done.3 = bf16[4,512,2048]{2,1,0:T(8,128)(2,1)} async-done(((bf16[4,512,2048]{2,1,0:T(8,128)(2,1)}), bf16[4,512,2048]{2,1,0:T(8,128)(2,1)}, u32[]{:S(2)}, u32[]{:S(2)}) %all-to-all-start.3) | async-done | bytes 8388640 | tf_op jit(solution)/shard_map/all_to_all | solution.py:22
  450.7 28.3 %gather_fusion.4 = bf16[3072,2048]{1,0:T(8,128)(2,1)} fusion(bf16[2048,2048]{1,0:T(8,128)(2,1)} %bitcast.14, s32[3072]{0:T(1024)S(1)} %broadcast_clamp_fusion), kind=kCustom, calls=%fused_computation.4 | custom fusion | bytes 25178112 | tf_op jit(solution)/shard_map/gather | solution.py:100
  479.0 20.4 %gather.31 = bf16[512,6,2048]{2,1,0:T(8,128)(2,1)} reshape(bf16[3072,2048]{1,0:T(8,128)(2,1)} %gather_fusion.4) | data formatting | bytes 25165824 | tf_op jit(solution)/shard_map/gather | solution.py:100
  499.4 13.1 %multiply_reduce_fusion.1 = bf16[3072]{0:T(1024)(128)(2,1)S(1)} fusion(f32[3072,2048]{1,0:T(8,128)} %mul.106, bf16[3072,2048]{1,0:T(8,128)(2,1)} %gather_fusion.1, pred[3072]{0:T(1024)(128)(4,1)S(1)} %broadcast_compare_fusion), kind=kLoop, calls=%fused_computation.7 | loop fusion | flops 25162752 | bytes 37757952 | tf_op jit(solution)/shard_map/reduce_sum | solution.py:76
  512.5 0.9 convert_element_type.90
  513.4 0.0 reduce-scatter.8.cloned.1.call-update
  513.4 0.3 reduce-scatter.6.cloned.1.call-start
  513.7 14.3 %select_reduce_fusion = bf16[512,2048]{1,0:T(8,128)(2,1)} fusion(bf16[512,6,2048]{2,1,0:T(8,128)(2,1)} %gather.31, pred[512,6]{1,0:T(8,128)(4,1)S(1)} %copy-done.10), kind=kLoop, calls=%fused_computation.10 | loop fusion | flops 11534336 | bytes 14683136 | tf_op jit(solution)/shard_map/reduce_sum | solution.py:101
  528.0 0.0 reduce-scatter.6.cloned.1.call-update
  528.1 0.0 copy-start.6
  528.1 0.0 reduce-scatter.4.cloned.1.call-start
  528.1 20.4 %gather.26 = bf16[512,6,2048]{2,1,0:T(8,128)(2,1)} reshape(bf16[3072,2048]{1,0:T(8,128)(2,1)} %gather_fusion.1) | data formatting | bytes 25165824 | tf_op jit(solution)/shard_map/gather | solution.py:71
  548.6 20.7 %multiply_reduce_fusion = bf16[512,2048]{1,0:T(8,128)(2,1)} fusion(bf16[512,6,2048]{2,1,0:T(8,128)(2,1)} %gather.26, f32[512,6]{1,0:T(8,128)S(1)} %copy-done.6, pred[512,6]{1,0:T(8,128)(4,1)S(1)} %copy-done.10), kind=kLoop, calls=%fused_computation.6 | loop fusion | flops 24117248 | bytes 14695424 | tf_op jit(solution)/shard_map/reduce_sum | solution.py:74
  569.3 0.0 reduce-scatter.4.cloned.1.call-update
  569.3 7.6 %fusion.4 = bf16[1,352,2048]{2,1,0:T(8,128)(2,1)} fusion(bf16[2048,352]{0,1:T(8,128)(2,1)S(1)} %copy-done.14, bf16[2048,2048]{1,0:T(8,128)(2,1)} %bitcast.12), kind=kOutput, calls=%fused_computation.24 | convolution fusion | flops 2953510912 | bytes 11272192 | tf_op jit(solution)/shard_map/rf,rd->fd/dot_general | solution.py:87
  577.0 7.8 %fusion.3 = bf16[1,352,2048]{2,1,0:T(8,128)(2,1)} fusion(bf16[2048,352]{0,1:T(8,128)(2,1)S(1)} %get-tuple-element.17, bf16[2048,2048]{1,0:T(8,128)(2,1)} %bitcast.4), kind=kOutput, calls=%fused_computation.23 | convolution fusion | flops 2953510912 | bytes 11272192 | tf_op jit(solution)/shard_map/rf,rd->fd/dot_general | solution.py:93
  584.7 7.7 %fusion.2 = bf16[1,352,2048]{2,1,0:T(8,128)(2,1)} fusion(bf16[2048,352]{0,1:T(8,128)(2,1)S(1)} %copy-done.4, bf16[2048,2048]{1,0:T(8,128)(2,1)} %bitcast.4), kind=kOutput, calls=%fused_computation.22 | convolution fusion | flops 2953510912 | bytes 11272192 | tf_op jit(solution)/shard_map/rf,rd->fd/dot_general | solution.py:90
  592.4 1.4 copy.18
  593.8 24.4 %reduce-scatter.4.cloned.1.call-done = bf16[64,2048]{1,0:T(8,128)(2,1)} async-done(((bf16[512,2048]{1,0:T(8,128)(2,1)}), bf16[64,2048]{1,0:T(8,128)(2,1)}) %reduce-scatter.4.cloned.1.call-update) | async-done | bytes 262160 | tf_op jit(solution)/shard_map/reduce_scatter | solution.py:105
  (35 shorter events, 0.1 us)
Async XLA Ops:
  7.2 15.8 %copy-start = (bf16[512,2048]{1,0:T(8,128)(2,1)S(1)}, bf16[512,2048]{1,0:T(8,128)(2,1)}, u32[]{:S(2)}) copy-start(bf16[512,2048]{1,0:T(8,128)(2,1)} %param.7) | copy-start | bytes 6291460
  41.3 6.5 %copy-start.11 = (f32[512,6]{0,1:T(8,128)S(1)}, f32[512,6]{0,1:T(8,128)}, u32[]{:S(2)}) copy-start(f32[512,6]{0,1:T(8,128)} %param.9) | copy-start | bytes 36868
  41.3 99.6 %all-to-all-start = ((bf16[4,512,2048]{2,1,0:T(8,128)(2,1)}), bf16[4,512,2048]{2,1,0:T(8,128)(2,1)}, u32[]{:S(2)}, u32[]{:S(2)}) async-start(bf16[4,512,2048]{2,1,0:T(8,128)(2,1)} %broadcast_select_fusion), calls=%async_computation | async-start | bytes 16777216 | tf_op jit(solution)/shard_map/all_to_all | solution.py:16
  47.0 34.7 %all-gather.2.cloned.1.call-start = ((), (), s32[]{:S(2)}) async-start(), calls=%async_computation.8 | async-start | bytes 2359296 | tf_op jit(solution)/shard_map/all_gather | solution.py:75
  47.9 12.0 %copy-start.5 = (f32[512,6]{1,0:T(8,128)}, f32[512,6]{1,0:T(8,128)S(1)}, u32[]{:S(2)}) copy-start(f32[512,6]{1,0:T(8,128)S(1)} %copy.14) | copy-start | bytes 36868
  108.0 38.8 %copy-start.7 = (bf16[1,352,2048]{2,1,0:T(8,128)(2,1)S(1)}, bf16[1,352,2048]{2,1,0:T(8,128)(2,1)}, u32[]{:S(2)}) copy-start(bf16[1,352,2048]{2,1,0:T(8,128)(2,1)} %param.11) | copy-start | bytes 4325380
  140.9 97.9 %all-to-all-start.2 = ((bf16[4,512,2048]{2,1,0:T(8,128)(2,1)}), bf16[4,512,2048]{2,1,0:T(8,128)(2,1)}, u32[]{:S(2)}, u32[]{:S(2)}) async-start(bf16[4,512,2048]{2,1,0:T(8,128)(2,1)} %fusion), calls=%async_computation.3 | async-start | bytes 16777216 | tf_op jit(solution)/shard_map/all_to_all | solution.py:16
  146.7 8.3 %copy-start.9 = (bf16[1,352,2048]{2,1,0:T(8,128)(2,1)S(1)}, bf16[1,352,2048]{2,1,0:T(8,128)(2,1)}, u32[]{:S(2)}) copy-start(bf16[1,352,2048]{2,1,0:T(8,128)(2,1)} %param.10) | copy-start | bytes 4325380
  238.8 9.7 %copy-start.12 = (bf16[1,352,2048]{2,1,0:T(8,128)(2,1)S(1)}, bf16[1,352,2048]{2,1,0:T(8,128)(2,1)}, u32[]{:S(2)}) copy-start(bf16[1,352,2048]{2,1,0:T(8,128)(2,1)} %param.12) | copy-start | bytes 4325380
  248.5 6.9 %copy-start.13 = (bf16[2048,352]{0,1:T(8,128)(2,1)}, bf16[2048,352]{0,1:T(8,128)(2,1)S(1)}, u32[]{:S(2)}) copy-start(bf16[2048,352]{0,1:T(8,128)(2,1)S(1)} %get-tuple-element.19) | copy-start | bytes 4325380
  248.5 12.7 %copy-start.3 = (bf16[2048,352]{0,1:T(8,128)(2,1)}, bf16[2048,352]{0,1:T(8,128)(2,1)S(1)}, u32[]{:S(2)}) copy-start(bf16[2048,352]{0,1:T(8,128)(2,1)S(1)} %get-tuple-element.18) | copy-start | bytes 4325380
  255.4 97.7 %all-to-all-start.1 = ((bf16[4,512,2048]{2,1,0:T(8,128)(2,1)}), bf16[4,512,2048]{2,1,0:T(8,128)(2,1)}, u32[]{:S(2)}, u32[]{:S(2)}) async-start(bf16[4,512,2048]{2,1,0:T(8,128)(2,1)} %bitcast.62), calls=%async_computation.1 | async-start | bytes 16777216 | tf_op jit(solution)/shard_map/all_to_all | solution.py:22
  261.2 9.6 %copy-start.8 = (bf16[1,352,2048]{2,1,0:T(8,128)(2,1)S(1)}, bf16[1,352,2048]{2,1,0:T(8,128)(2,1)}, u32[]{:S(2)}) copy-start(bf16[1,352,2048]{2,1,0:T(8,128)(2,1)} %param.11) | copy-start | bytes 4325380
  353.0 7.5 %copy-start.2 = (bf16[512,2048]{1,0:T(8,128)(2,1)S(1)}, bf16[512,2048]{1,0:T(8,128)(2,1)}, u32[]{:S(2)}) copy-start(bf16[512,2048]{1,0:T(8,128)(2,1)} %all-gather.2.cloned.1.call-done) | copy-start | bytes 6291460
  353.0 97.7 %all-to-all-start.3 = ((bf16[4,512,2048]{2,1,0:T(8,128)(2,1)}), bf16[4,512,2048]{2,1,0:T(8,128)(2,1)}, u32[]{:S(2)}, u32[]{:S(2)}) async-start(bf16[4,512,2048]{2,1,0:T(8,128)(2,1)} %bitcast.59), calls=%async_computation.4 | async-start | bytes 16777216 | tf_op jit(solution)/shard_map/all_to_all | solution.py:22
  358.9 233.6 %reduce-scatter.8.cloned.1.call-start = ((), (), s32[]{:S(2)}) async-start(), calls=%async_computation.10 | async-start | bytes 147456 | tf_op jit(solution)/shard_map/reduce_scatter | solution.py:111
  499.4 14.4 %copy-start.10 = (pred[512,6]{1,0:T(8,128)(4,1)S(1)}, pred[512,6]{1,0:T(8,128)(4,1)}, u32[]{:S(2)}) copy-start(pred[512,6]{1,0:T(8,128)(4,1)} %eq.59) | copy-start | bytes 9220
  513.4 80.4 %reduce-scatter.6.cloned.1.call-start = ((), (), s32[]{:S(2)}) async-start(), calls=%async_computation.9 | async-start | bytes 2359296 | tf_op jit(solution)/shard_map/reduce_scatter | solution.py:108
  528.1 20.5 %copy-start.6 = (f32[512,6]{1,0:T(8,128)S(1)}, f32[512,6]{1,0:T(8,128)}, u32[]{:S(2)}) copy-start(f32[512,6]{1,0:T(8,128)} %copy-done.5) | copy-start | bytes 36868
  528.1 90.1 %reduce-scatter.4.cloned.1.call-start = ((), (), s32[]{:S(2)}) async-start(), calls=%async_computation.7 | async-start | bytes 2359296 | tf_op jit(solution)/shard_map/reduce_scatter | solution.py:105
  548.6 20.8 %copy-start.14 = (bf16[2048,352]{0,1:T(8,128)(2,1)S(1)}, bf16[2048,352]{0,1:T(8,128)(2,1)}, u32[]{:S(2)}) copy-start(bf16[2048,352]{0,1:T(8,128)(2,1)} %copy-done.13) | copy-start | bytes 4325380
  577.0 7.8 %copy-start.4 = (bf16[2048,352]{0,1:T(8,128)(2,1)S(1)}, bf16[2048,352]{0,1:T(8,128)(2,1)}, u32[]{:S(2)}) copy-start(bf16[2048,352]{0,1:T(8,128)(2,1)} %copy-done.3) | copy-start | bytes 4325380
  584.7 33.5 %copy-start.1 = (bf16[512,2048]{1,0:T(8,128)(2,1)S(1)}, bf16[512,2048]{1,0:T(8,128)(2,1)}, u32[]{:S(2)}) copy-start(bf16[512,2048]{1,0:T(8,128)(2,1)} %param.7) | copy-start | bytes 6291460
Sparse Core Ops, SparseCore 0:
  49.5 32.2 all-gather.1
  513.6 30.4 reduce-scatter.7
  547.0 33.9 reduce-scatter.5
  583.9 34.2 reduce-scatter.3
where the time goes:
time: 633 us; the launch traced here: 625 us
  waiting for transfers between devices  248 us (39%)
  local copies, waits for them, and re-layouts  196 us (31%)
  matrix products  75.9 us (12%)
  other arithmetic  66.5 us (11%)
  starting transfers between devices  23.7 us (4%)
  between operations  14.5 us (2%)
    all_to_all x2, waiting for transfers between devices, deliver(): lax.all_to_all(buffer, 'dp', split_axis=0, concat_axis=0, tiled=True)  108 us
    all_to_all x2, waiting for transfers between devices, send_back(): lax.all_to_all(rows.reshape(dp_count, slot_count, width), 'dp', split_axi...  93.1 us
    gather x2, local copies, waits for them, and re-layouts, body(): returned[safe_target]  48.7 us
    gather x2, local copies, waits for them, and re-layouts, body(): dx_back[safe_target]  48.7 us
    mul x2, local copies, waits for them, and re-layouts, body(): route_part.reshape(tok_rows, top_count, piece_width).astype(jnp.float32)  40.8 us
    reduce_scatter x1, waiting for transfers between devices, body(): lax.psum_scatter(mixed_part.astype(jnp.bfloat16), 'expert', scatter_dimen...  24.4 us
    all_gather x1, waiting for transfers between devices, body(): cotangent = lax.all_gather(grad_out, 'expert', axis=0, tiled=True)  21.8 us
    reduce_sum x1, other arithmetic, body(): jnp.sum(weighted.reshape(tok_rows, top_count, piece_width), axis=1)  20.7 us
  transfers between devices with their start and end apart: 8, of which 6 were waited for; matrix products, arithmetic and copies ran while one was open for 36% of the time, Pallas kernels for 0%

commit v1 on v0

--- a/solution.py
+++ b/solution.py
@@ -1,9 +1,17 @@
 import jax
 import jax.numpy as jnp
 from jax import lax
+from jax.experimental import pallas as pl
+from jax.experimental.pallas import tpu as pltpu
 from jax.sharding import PartitionSpec as P
 
 SHARDS = 4
+CORES = 2
+LANES = 128
+LEVEL_STEPS = (0, 2, 1, 3)
+PACKED_ROWS = 16
+VMEM_LIMIT = 32 * 1024 * 1024
+GRADS_VMEM = 56 * 1024 * 1024
 
 
 def silu_parts(gate_pre):
@@ -25,7 +33,7 @@
     return (returned.reshape(dp_count * slot_count, width), jnp.zeros((), jnp.int32))
 
 
-def body(tokens, routes, route_weight, w_gate, w_up, w_down, grad_out):
+def padded_body(tokens, routes, route_weight, w_gate, w_up, w_down, grad_out):
     dp_count = lax.axis_size("dp")
     ex_count = lax.axis_size("expert")
     groups = ex_count // SHARDS
@@ -120,6 +128,386 @@
         grad_up,
         grad_down,
     )
+
+
+FLOPS = 5_000_000_000
+BYTES = 20_000_000
+
+
+def dot_rows(left, right):
+    return lax.dot_general(
+        left, right, (((1,), (1,)), ((), ())), preferred_element_type=jnp.float32
+    )
+
+
+def dot_over_rows(left, right):
+    return lax.dot_general(
+        left, right, (((0,), (0,)), ((), ())), preferred_element_type=jnp.float32
+    )
+
+
+def padded(hidden_rows):
+    return -(-hidden_rows // LANES) * LANES
+
+
+def load_weights(refs, pre_buf, down_buf, sems):
+    h = refs[0].shape[1]
+    step = padded(h)
+    copies = []
+    for position, ref in enumerate(refs):
+        buf, first = (pre_buf, position * step) if position < 4 else (down_buf, (position - 4) * step)
+        copies.append(
+            pltpu.make_async_copy(ref.at[0], buf.at[pl.ds(first, h)], sems.at[position])
+        )
+        if step > h:
+            buf[first + h : first + step, :] = jnp.zeros((step - h, buf.shape[1]), buf.dtype)
+    return copies
+
+
+def load_rows(refs, buf, sems):
+    rows = buf.shape[0] // len(refs)
+    return [
+        pltpu.make_async_copy(
+            ref.at[pl.ds(0, rows)], buf.at[pl.ds(position * rows, rows)], sems.at[position]
+        )
+        for position, ref in enumerate(refs)
+    ]
+
+
+def forward_kernel(
+    gate, gate_other, up, up_other, down, down_other, x_first, x_second, weight,
+    mixed_out, hidden_out, weighted_out, to_gate_out, to_up_out,
+    row_buf, pre_buf, down_buf, row_sems, sems,
+):
+    both = down_buf.shape[0]
+    loads = load_weights(
+        (gate, gate_other, up, up_other, down, down_other), pre_buf, down_buf, sems
+    )
+    loads += load_rows((x_first, x_second), row_buf, row_sems)
+    for load in loads:
+        load.start()
+    for load in loads:
+        load.wait()
+    gate_pre = dot_rows(row_buf[...], pre_buf[:both])
+    up_pre = dot_rows(row_buf[...], pre_buf[both:])
+    silu_value, silu_slope = silu_parts(gate_pre)
+    hidden = silu_value * up_pre
+    weighted = (hidden * weight[...]).astype(jnp.bfloat16)
+    hidden_out[...] = hidden.astype(jnp.bfloat16)
+    weighted_out[...] = weighted
+    to_gate_out[...] = up_pre * silu_slope
+    to_up_out[...] = silu_value
+    mixed_out[...] = jnp.dot(
+        weighted, down_buf[...], preferred_element_type=jnp.float32
+    ).astype(jnp.bfloat16)
+
+
+def backward_kernel(
+    gate, gate_other, up, up_other, down, down_other, cot_first, cot_second, weight,
+    hidden, to_gate, to_up,
+    dx_left, dx_right, route_out, d_gate_out, d_up_out,
+    row_buf, pre_buf, down_buf, row_sems, sems,
+):
+    both = down_buf.shape[0]
+    loads = load_weights(
+        (gate, gate_other, up, up_other, down, down_other), pre_buf, down_buf, sems
+    )
+    first = load_rows((cot_first, cot_second), row_buf, row_sems) + loads[4:]
+    for load in first + loads[:4]:
+        load.start()
+    for load in first:
+        load.wait()
+    plain = dot_rows(row_buf[...], down_buf[...])
+    route_out[...] = jnp.sum(plain * hidden[...].astype(jnp.float32), axis=1, keepdims=True)
+    d_hidden = plain * weight[...]
+    d_gate = (d_hidden * to_gate[...]).astype(jnp.bfloat16)
+    d_up = (d_hidden * to_up[...]).astype(jnp.bfloat16)
+    d_gate_out[...] = d_gate
+    d_up_out[...] = d_up
+    for load in loads[:4]:
+        load.wait()
+    dx = jnp.dot(d_gate, pre_buf[:both], preferred_element_type=jnp.float32)
+    dx = dx + jnp.dot(d_up, pre_buf[both:], preferred_element_type=jnp.float32)
+    columns = dx_left.shape[1]
+    dx_left[...] = dx[:, :columns].astype(jnp.bfloat16)
+    dx_right[...] = dx[:, columns:].astype(jnp.bfloat16)
+
+
+WIDE, NARROW = 8, 6
+
+
+def weight_products(refs, first, count):
+    xs, gs, narrow = refs[:4], refs[4:WIDE], refs[WIDE : WIDE + NARROW]
+    rows = narrow[0].shape[0] // 2
+    there = pl.ds(first, count)
+
+    def product(pair, parts):
+        total = None
+        for position, part in enumerate(parts):
+            here = pl.ds(position % 2 * rows, rows)
+            term = dot_over_rows(pair[position // 2][here, there], part[...])
+            total = term if total is None else total + term
+        return total
+
+    return product(narrow[0:2], xs), product(narrow[2:4], xs), product(narrow[4:6], gs)
+
+
+def other_grads_kernel(*refs):
+    out = refs[-1]
+    count = refs[WIDE].shape[1] // 2
+    h = out.shape[1]
+    for position, product in enumerate(weight_products(refs, count, count)):
+        out[position] = product[:h].astype(jnp.bfloat16)
+
+
+def own_grads_kernel(*refs):
+    received, outs = refs[WIDE + NARROW], refs[WIDE + NARROW + 1 :]
+    count = refs[WIDE].shape[1] // 2
+    h = received.shape[1]
+    for position, product in enumerate(weight_products(refs, 0, count)):
+        total = product[:h] + received[position].astype(jnp.float32)
+        outs[position][0] = total.astype(jnp.bfloat16)
+
+
+def cost():
+    return pl.CostEstimate(flops=FLOPS, bytes_accessed=BYTES, transcendentals=0)
+
+
+def specs(space, count):
+    return [pl.BlockSpec(memory_space=space)] * count
+
+
+def row_kernel(kernel, name, matrices, pair, operands, outs):
+    _, h, width = matrices[0].shape
+    step = padded(h)
+    rows = operands[0].shape[0]
+    return pl.pallas_call(
+        kernel,
+        out_shape=outs,
+        in_specs=specs(pl.ANY, len(matrices) + 2) + specs(pltpu.VMEM, len(operands)),
+        out_specs=specs(pltpu.VMEM, len(outs)),
+        scratch_shapes=[
+            pltpu.VMEM((rows, width), jnp.bfloat16),
+            pltpu.VMEM((4 * step, width), jnp.bfloat16),
+            pltpu.VMEM((2 * step, width), jnp.bfloat16),
+            pltpu.SemaphoreType.DMA((2,)),
+            pltpu.SemaphoreType.DMA((6,)),
+        ],
+        compiler_params=pltpu.CompilerParams(vmem_limit_bytes=VMEM_LIMIT),
+        cost_estimate=cost(),
+        name=name,
+    )(*matrices, *pair, *operands)
+
+
+def forward(matrices, pair, weight):
+    rows, width = weight.shape[0], pair[0].shape[1]
+    units = 2 * padded(matrices[0].shape[1])
+    f32, bf16 = jnp.float32, jnp.bfloat16
+    outs = [jax.ShapeDtypeStruct((rows, width), bf16)]
+    outs += [jax.ShapeDtypeStruct((rows, units), kind) for kind in (bf16, bf16, f32, f32)]
+    return row_kernel(forward_kernel, "forward", matrices, pair, (weight,), outs)
+
+
+def backward(matrices, pair, weight, hidden, to_gate, to_up):
+    rows, width = weight.shape[0], pair[0].shape[1]
+    units = 2 * padded(matrices[0].shape[1])
+    f32, bf16 = jnp.float32, jnp.bfloat16
+    outs = [jax.ShapeDtypeStruct((rows, width // 2), bf16)] * 2
+    outs += [jax.ShapeDtypeStruct((rows, 1), f32)]
+    outs += [jax.ShapeDtypeStruct((rows, units), bf16)] * 2
+    operands = (weight, hidden, to_gate, to_up)
+    return row_kernel(backward_kernel, "backward", matrices, pair, operands, outs)
+
+
+def weight_grads(wide, narrow, h, received=None):
+    rows, width = narrow[0].shape[0] // 2, wide[0].shape[1]
+    tile = min(512, width)
+    tall = pl.BlockSpec((rows, tile), lambda n: (0, n))
+    whole = pl.BlockSpec(narrow[0].shape, lambda n: (0, 0), pipeline_mode=pl.Buffered(1))
+    three = pl.BlockSpec((3, h, tile), lambda n: (0, 0, n))
+    in_specs = [tall] * len(wide) + [whole] * len(narrow)
+    if received is None:
+        kernel, more, name = other_grads_kernel, (), "other_grads"
+        outs = jax.ShapeDtypeStruct((3, h, width), jnp.bfloat16)
+        out_specs = three
+    else:
+        kernel, more, name = own_grads_kernel, (received,), "own_grads"
+        outs = [jax.ShapeDtypeStruct((1, h, width), jnp.bfloat16)] * 3
+        out_specs = [pl.BlockSpec((1, h, tile), lambda n: (0, 0, n))] * 3
+        in_specs = in_specs + [three]
+    return pl.pallas_call(
+        kernel,
+        out_shape=outs,
+        grid=(width // tile,),
+        in_specs=in_specs,
+        out_specs=out_specs,
+        compiler_params=pltpu.CompilerParams(vmem_limit_bytes=GRADS_VMEM),
+        cost_estimate=cost(),
+        name=name,
+    )(*wide, *narrow, *more)
+
+
+def all_slots_body(tokens, routes, route_weight, w_gate, w_up, w_down, grad_out):
+    f32 = jnp.float32
+    dp_count = lax.axis_size("dp")
+    ex_count = lax.axis_size("expert")
+    levels = ex_count // CORES
+    groups = ex_count // SHARDS
+    width = tokens.shape[1]
+    block = grad_out.shape[0]
+    half = levels * block
+    dp_index = lax.axis_index("dp")
+    ex_index = lax.axis_index("expert")
+    level, core = ex_index // CORES, ex_index % CORES
+
+    def pieces(values):
+        rest, parts = values.reshape(-1), []
+        for _ in range(3):
+            part = lax.reduce_precision(rest, 8, 7)
+            parts.append(part.astype(jnp.bfloat16))
+            rest = rest - part
+        row = jnp.concatenate(parts)
+        row = jnp.pad(row, (0, PACKED_ROWS * width - row.shape[0]))
+        return row.reshape(PACKED_ROWS, width)
+
+    def whole(message, position):
+        row = message[half : half + PACKED_ROWS].reshape(-1)[: 9 * half]
+        parts = row.reshape(3, 3, half)[:, position].astype(f32)
+        return (parts[0] + parts[1]) + parts[2]
+
+    def exchange(value, partner):
+        pairs = []
+        for d in range(dp_count):
+            for e in range(ex_count):
+                other_d, other_e = partner(d, e // CORES, e % CORES)
+                pairs.append((d * ex_count + e, other_d * ex_count + other_e))
+        return lax.ppermute(value, ("dp", "expert"), pairs)
+
+    def to_near(value):
+        return exchange(value, lambda d, z, c: (d ^ (1 + c), z * CORES + c))
+
+    def to_far(value):
+        return exchange(value, lambda d, z, c: (d ^ (2 - c), z * CORES + c))
+
+    def to_core(value):
+        return exchange(value, lambda d, z, c: (d, z * CORES + 1 - c))
+
+    def to_level(value, step):
+        return exchange(value, lambda d, z, c: (d, (z ^ step) * CORES + c))
+
+    def add(*terms):
+        total = terms[0].astype(f32)
+        for term in terms[1:]:
+            total = total + term.astype(f32)
+        return total.astype(terms[0].dtype)
+
+    def after(value, *others):
+        return lax.optimization_barrier((value, *others))[0]
+
+    def by_halving(blocks):
+        pair = add(blocks[:2], to_level(blocks[2:], 1))
+        return add(pair[0], to_level(pair[1], 2))
+
+    level_order = jnp.array(LEVEL_STEPS, jnp.int32) ^ level
+    block_order = level_order * CORES + core
+    near, far = dp_index ^ (1 + core), dp_index ^ (2 - core)
+    group_dp = (dp_index, near, far, dp_index ^ 3)
+
+    group_experts = jnp.arange(dp_count, dtype=jnp.int32) * groups + ex_index // SHARDS
+    table = jnp.sum(
+        jnp.where(routes[None] == group_experts[:, None, None], route_weight[None], 0.0), axis=2
+    )
+    table = table.reshape(dp_count, ex_count, block)[:, block_order]
+    own_table, near_table, far_table, diagonal_table = (
+        lax.dynamic_index_in_dim(table, d, axis=0).reshape(half) for d in group_dp
+    )
+
+    x_own = tokens.reshape(ex_count, block, width)[block_order].reshape(half, width)
+    x_own = jnp.concatenate(
+        [x_own, pieces(jnp.stack([near_table, far_table, diagonal_table]))], axis=0
+    )
+    x_near = to_near(x_own)
+    x_far = to_far(x_own)
+    others = [to_core(matrix) for matrix in (w_gate, w_up, w_down)]
+    matrices = (w_gate, others[0], w_up, others[1], w_down, others[2])
+    g_pair = jnp.concatenate([grad_out, to_level(grad_out, 2)], axis=0)
+    x_last = to_far(x_near)
+    weight12 = jnp.concatenate([own_table, whole(x_near, 0)])[:, None]
+    weight34 = jnp.concatenate([whole(x_far, 1), whole(x_last, 2)])[:, None]
+
+    mixed12, hidden12, weighted12, *slopes12 = forward(matrices, (x_own, x_near), weight12)
+    x_last = after(x_last, mixed12)
+    g_own = jnp.concatenate([g_pair, to_level(g_pair, 1)], axis=0)
+    g_near = to_near(g_own)
+    g_far = to_far(g_own)
+    g_last = to_far(g_near)
+    mixed34, hidden34, weighted34, *slopes34 = forward(matrices, (x_far, x_last), weight34)
+    g_own, g_near = after((g_own, g_near), mixed34)
+    *dx12, route12, gate12, up12 = backward(
+        matrices, (g_own, g_near), weight12, hidden12, *slopes12
+    )
+    g_last = after(g_last, dx12)
+    *dx34, route34, gate34, up34 = backward(
+        matrices, (g_far, g_last), weight34, hidden34, *slopes34
+    )
+
+    mixed_sum = add(mixed12, after(to_far(after(mixed34, g_far)), dx34))
+    mixed_near = to_near(mixed_sum[half:])
+    mixed = add(mixed_sum[:half], mixed_near).reshape(levels, block, width)
+    mixed = by_halving(mixed)
+
+    h = w_gate.shape[1]
+    wide = (x_own, x_near, x_far, x_last, g_own, g_near, g_far, g_last)
+    narrow = (gate12, gate34, up12, up34, weighted12, weighted34)
+    received = to_core(weight_grads(wide, narrow, h))
+    grads = weight_grads(wide, narrow, h, received)
+
+    route12 = route12.reshape(2, half)
+    left_far = to_far(dx34[0])
+    left_sum = add(dx12[0], left_far)
+    left_near = to_near(after(left_sum[half:], mixed_near, *grads))
+    right_far, route_far = lax.optimization_barrier(
+        (to_far(after(dx34[1], left_far)), to_far(route34.reshape(2, half)))
+    )
+    right_sum = add(dx12[1], right_far)
+    right_near = to_near(after(right_sum[half:], left_near))
+    route_near = to_near(jnp.stack([route12[1], route_far[1]]))
+
+    left_near = after(left_near, right_sum)
+    left = add(left_sum[:half], left_near).reshape(levels, block, width // 2)
+    left = by_halving(left)
+    right_near, route_near, *_ = lax.optimization_barrier((right_near, route_near, mixed))
+    right = add(right_sum[:half], right_near).reshape(levels, block, width // 2)
+    right = [right[0]] + [
+        to_level(right[k], step) for k, step in enumerate(LEVEL_STEPS) if k > 0
+    ]
+    right = add(*right)
+    grad_tokens = jnp.concatenate([left, right], axis=1)
+
+    route_own = jnp.stack([route12[0], route_far[0], route_near[0], route_near[1]])
+    route_own = route_own.reshape(dp_count, levels, block)
+    route_own = route_own[:, :2] + to_level(route_own[:, 2:], 1)
+    by_group = (route_own[:, 0], to_level(route_own[:, 1], 2))
+    my_routes = lax.dynamic_slice_in_dim(routes, ex_index * block, block, axis=0)
+    my_group = ex_index // SHARDS
+    grad_route = jnp.zeros(my_routes.shape, f32)
+    for values, group in zip(by_group, (my_group, 1 - my_group)):
+        for position, d in enumerate((dp_index, far, near, dp_index ^ 3)):
+            grad_route = grad_route + jnp.where(
+                my_routes == d * groups + group, values[position][:, None], 0.0
+            )
+    return (mixed, grad_tokens, grad_route, *grads)
+
+
+def body(tokens, routes, *rest):
+    dp_count = lax.axis_size("dp")
+    ex_count = lax.axis_size("expert")
+    tok_rows, top_count = routes.shape
+    expert_count = dp_count * ex_count // SHARDS
+    every_slot = 3 * tok_rows * top_count >= 2 * expert_count * tok_rows
+    if every_slot and dp_count == 4 and ex_count == CORES * len(LEVEL_STEPS):
+        return all_slots_body(tokens, routes, *rest)
+    return padded_body(tokens, routes, *rest)
 
 
 def solution(mesh):

time: 633 us -> 216 us (0.34); the launches traced: 625 us -> 215 us
  waiting for transfers between devices: 248 us -> 75.7 us
  local copies, waits for them, and re-layouts: 196 us -> 30.1 us
  matrix products: 75.9 us -> 0 us
  Pallas kernels: 0 us -> 58.9 us
  other arithmetic: 66.5 us -> 15.6 us
  between operations: 14.5 us -> 1.2 us
  starting transfers between devices: 23.7 us -> 33.9 us
    all_to_all x4 -> x0, waiting for transfers between devices: 202 us -> none  [the longest x2 108 us: deliver(): lax.all_to_all(buffer, 'dp', split_axis=0, concat_axis=0, tiled=True)]
    gather x8 -> x2, local copies, waits for them, and re-layouts: 138 us -> 2.15 us  [the longest x1 1.58 us: all_slots_body(): tokens.reshape(ex_count, block, width)[block_order].reshape(half, width)]
    dot_general x9 -> x0, matrix products: 75.9 us -> none  [the longest x1 10.2 us: body(): jnp.dot(d_up, up_matrix, preferred_element_type=jnp.float32)]
    ppermute x0 -> x29, waiting for transfers between devices: none -> 75.7 us  [exchange(): return lax.ppermute(value, ('dp', 'expert'), pairs)]
    pallas_call x0 -> x6, Pallas kernels: none -> 58.9 us  [the longest x4 37.4 us: row_kernel(): pl.pallas_call(kernel, out_shape=outs, in_specs=specs(pl.ANY, len(matrice...]
    reduce_sum x4 -> x1, other arithmetic: 48.3 us -> 0.83 us  [all_slots_body(): jnp.sum(jnp.where(routes[None] == group_experts[:, None, None], route_wei...]
    mul x2 -> x0, local copies, waits for them, and re-layouts: 40.8 us -> none  [body(): route_part.reshape(tok_rows, top_count, piece_width).astype(jnp.float32)]
    ppermute x0 -> x29, starting transfers between devices: none -> 33.9 us  [exchange(): return lax.ppermute(value, ('dp', 'expert'), pairs)]
  transfers between devices with their start and end apart: 8 -> 29, of which waited for: 6 -> 13; matrix products, arithmetic and copies ran while one was open for 36% -> 12% of each run, Pallas kernels for 0% -> 27%
where the time goes in v1:
time: 216 us; the launch traced here: 215 us
  waiting for transfers between devices  75.7 us (35%)
  Pallas kernels  58.9 us (27%)
  starting transfers between devices  33.9 us (16%)
  local copies, waits for them, and re-layouts  30.1 us (14%)
  other arithmetic  15.6 us (7%)
    ppermute x29, waiting for transfers between devices, exchange(): return lax.ppermute(value, ('dp', 'expert'), pairs)  75.7 us
    pallas_call x4, Pallas kernels, row_kernel(): pl.pallas_call(kernel, out_shape=outs, in_specs=specs(pl.ANY, len(matrice...  37.4 us
    ppermute x29, starting transfers between devices, exchange(): return lax.ppermute(value, ('dp', 'expert'), pairs)  33.9 us
    unnamed x75, local copies, waits for them, and re-layouts  22.7 us
    pallas_call x2, Pallas kernels, weight_grads(): pl.pallas_call(kernel, out_shape=outs, grid=(width // tile,), in_specs=in...  21.4 us
    convert_element_type x11, other arithmetic, add(): return total.astype(terms[0].dtype)  8.67 us
  transfers between devices with their start and end apart: 29, of which 13 were waited for; matrix products, arithmetic and copies ran while one was open for 12% of the time, Pallas kernels for 27%

profile of v1, /device:TPU:0, one launch (start us, length us, event | category | flops | bytes accessed | tf_op | source)
XLA Modules:
  0.0 215.3 jit_solution(8464125232978598823)
XLA Ops:
  0.6 4.1 %collective-permute-start.6 = (bf16[64,2048]{1,0:T(8,128)(2,1)}, bf16[64,2048]{1,0:T(8,128)(2,1)}, u32[]{:S(2)}, u32[]{:S(2)}) collective-permute-start(bf16[64,2048]{1,0:T(8,128)(2,1)} %param.14), channel_id=1, source_target_pairs={{0,4},{1,5},{2,6},{3,7},{4,0},{5,1},{6,2},{7,3},{8,12},{9,13},{10,... | collective-permute-start | bytes 786440 | tf_op jit(solution)/shard_map/ppermute | solution.py:384
  7.3 1.6 gather_fusion
  8.9 1.3 pad_maximum_fusion.x_first.refs_0_
  10.2 1.6 collective-permute-start.3
  11.8 5.2 %collective-permute-done.6 = bf16[64,2048]{1,0:T(8,128)(2,1)} collective-permute-done((bf16[64,2048]{1,0:T(8,128)(2,1)}, bf16[64,2048]{1,0:T(8,128)(2,1)}, u32[]{:S(2)}, u32[]{:S(2)}) %collective-permute-start.6) | collective-permute-done | bytes 262176 | tf_op jit(solution)/shard_map/ppermute | solution.py:384
  17.0 1.8 pad_maximum_fusion.1
  19.5 1.5 collective-permute-start.4
  22.3 1.7 constant_dynamic-update-slice_fusion.1
  24.0 8.1 %collective-permute-done.7 = bf16[128,2048]{1,0:T(8,128)(2,1)S(1)} collective-permute-done((bf16[128,2048]{1,0:T(8,128)(2,1)}, bf16[128,2048]{1,0:T(8,128)(2,1)S(1)}, u32[]{:S(2)}, u32[]{:S(2)}) %collective-permute-start.7) | collective-permute-done | bytes 524320 | tf_op jit(solution)/shard_map/ppermute | solution.py:384
  33.0 1.2 collective-permute-start.10
  35.3 1.0 collective-permute-done.4.x_first.refs_2_
  36.3 1.7 collective-permute-start.5
  38.1 1.0 copy-done.8
  39.5 1.4 copy-done.10
  40.9 8.7 %forward.2 = (bf16[512,2048]{1,0:T(8,128)(2,1)S(1)}, bf16[512,768]{1,0:T(8,128)(2,1)S(1)}, bf16[512,768]{1,0:T(8,128)(2,1)S(1)}, f32[512,768]{1,0:T(8,128)S(1)}, f32[512,768]{1,0:T(8,128)S(1)}) custom-call(bf16[1,352,2048]{2,1,0:T(8,128)(2,1)} %gate.7, bf16[1,352,2048]{2,1,0:T(8,128)(2,1)} %collective-permute-done.gate_other, bf16[1,352,2048]{2,1,0:T(8,128)(2,1)} %up.7, ...), custom_call_target="tpu_custom_call" | custom-call | flops 5000000000 | bytes 20000000 | tf_op jit(solution)/shard_map/forward/pallas_call | solution.py:284
  49.6 0.9 copy-done.14
  50.5 1.2 copy-done.20
  51.7 1.2 copy-done.22
  52.8 0.9 copy-done.24
  53.7 2.6 %collective-permute-done.10.cot_second.refs_5_ = bf16[256,2048]{1,0:T(8,128)(2,1)} collective-permute-done((bf16[256,2048]{1,0:T(8,128)(2,1)}, bf16[256,2048]{1,0:T(8,128)(2,1)}, u32[]{:S(2)}, u32[]{:S(2)}) %collective-permute-start.10) | collective-permute-done | bytes 1048608 | tf_op jit(solution)/shard_map/ppermute | solution.py:384
  56.3 1.3 collective-permute-start.11
  57.6 2.0 collective-permute-done.5.x_second.refs_3_
  60.7 1.2 copy-done.9
  61.9 1.4 copy-done.11
  63.3 10.2 %forward.3 = (bf16[512,2048]{1,0:T(8,128)(2,1)}, bf16[512,768]{1,0:T(8,128)(2,1)S(1)}, bf16[512,768]{1,0:T(8,128)(2,1)S(1)}, f32[512,768]{1,0:T(8,128)S(1)}, f32[512,768]{1,0:T(8,128)S(1)}) custom-call(bf16[1,352,2048]{2,1,0:T(8,128)(2,1)} %gate.7, bf16[1,352,2048]{2,1,0:T(8,128)(2,1)} %collective-permute-done.gate_other, bf16[1,352,2048]{2,1,0:T(8,128)(2,1)} %up.7, ...), custom_call_target="tpu_custom_call" | custom-call | flops 5000000000 | bytes 20000000 | tf_op jit(solution)/shard_map/forward/pallas_call | solution.py:284
  73.5 0.9 copy-done.15
  74.4 1.5 collective-permute-start.9
  76.0 9.2 %backward.2 = (bf16[512,1024]{1,0:T(8,128)(2,1)S(1)}, bf16[512,1024]{1,0:T(8,128)(2,1)S(1)}, f32[512,1]{1,0:T(8,128)S(1)}, bf16[512,768]{1,0:T(8,128)(2,1)S(1)}, bf16[512,768]{1,0:T(8,128)(2,1)S(1)}) custom-call(bf16[1,352,2048]{2,1,0:T(8,128)(2,1)} %gate.7, bf16[1,352,2048]{2,1,0:T(8,128)(2,1)} %collective-permute-done.gate_other, ...), custom_call_target="tpu_custom_call" | custom-call | flops 5000000000 | bytes 20000000 | tf_op jit(solution)/shard_map/backward/pallas_call | solution.py:284
  85.2 1.0 copy-done.3
  86.9 0.9 copy-done.16
  87.8 0.9 copy-done.17
  88.7 9.3 %backward.3 = (bf16[512,1024]{1,0:T(8,128)(2,1)}, bf16[512,1024]{1,0:T(8,128)(2,1)S(1)}, f32[512,1]{1,0:T(8,128)S(1)}, bf16[512,768]{1,0:T(8,128)(2,1)S(1)}, bf16[512,768]{1,0:T(8,128)(2,1)S(1)}) custom-call(bf16[1,352,2048]{2,1,0:T(8,128)(2,1)} %gate.7, bf16[1,352,2048]{2,1,0:T(8,128)(2,1)} %collective-permute-done.gate_other, bf16[1,352,2048]{2,1,0:T(8,128)(2,1)} %up.7, ...), custom_call_target="tpu_custom_call" | custom-call | flops 5000000000 | bytes 20000000 | tf_op jit(solution)/shard_map/backward/pallas_call | solution.py:284
  98.0 1.0 copy-done.13
  99.0 0.9 copy-done.18
  99.9 0.9 copy-done.19
  100.8 10.6 %other_grads.1 = bf16[3,352,2048]{2,1,0:T(8,128)(2,1)} custom-call(bf16[272,2048]{1,0:T(8,128)(2,1)} %copy-done.2, bf16[272,2048]{1,0:T(8,128)(2,1)} %collective-permute-done.3.x_second.refs_1_, bf16[272,2048]{1,0:T(8,128)(2,1)} %copy-done.8, bf16[272,2048]{1,0:T(8,128)(2,1)} %collective-permute-done.5.x_second.refs_3_, ...), custom_call_target="tpu_custom_call" | custom-call | flops 5000000000 | bytes 20000000 | tf_op jit(solution)/shard_map/other_grads/pallas_call | solution.py:338
  111.4 1.3 collective-permute-start.16
  112.7 1.5 collective-permute-start.15
  114.2 13.6 %collective-permute-done.15 = bf16[512,1024]{1,0:T(8,128)(2,1)} collective-permute-done((bf16[512,1024]{1,0:T(8,128)(2,1)}, bf16[512,1024]{1,0:T(8,128)(2,1)}, u32[]{:S(2)}, u32[]{:S(2)}) %collective-permute-start.15) | collective-permute-done | bytes 1048608 | tf_op jit(solution)/shard_map/ppermute | solution.py:384
  127.8 1.5 collective-permute-start.18
  129.3 1.1 slice_reduce_fusion
  130.5 2.4 %add_convert_fusion = bf16[512,2048]{1,0:T(8,128)(2,1)S(1)} fusion(bf16[512,2048]{1,0:T(8,128)(2,1)} %collective-permute-done.9, bf16[512,2048]{1,0:T(8,128)(2,1)S(1)} %get-tuple-element.43), kind=kLoop, calls=%fused_computation.2 | loop fusion | flops 4194304 | bytes 6291456 | tf_op jit(solution)/shard_map/convert_element_type | solution.py:402
  132.9 1.3 copy-done.26
  134.2 1.0 slice.267
  136.5 1.6 add_convert_fusion.2
  138.2 1.0 copy-done.28
  140.0 9.4 %collective-permute-done.19 = f32[2,256]{1,0:T(2,128)S(1)} collective-permute-done((f32[2,256]{1,0:T(2,128)S(1)}, f32[2,256]{1,0:T(2,128)S(1)}, u32[]{:S(2)}, u32[]{:S(2)}) %collective-permute-start.19) | collective-permute-done | bytes 2080 | tf_op jit(solution)/shard_map/ppermute | solution.py:384
  149.6 1.6 add_convert_fusion.1
  151.2 1.2 collective-permute-done.12
  152.4 1.6 add_convert_fusion.3
  154.1 1.6 collective-permute-start.13
  155.8 10.8 %own_grads.1 = (bf16[1,352,2048]{2,1,0:T(8,128)(2,1)}, bf16[1,352,2048]{2,1,0:T(8,128)(2,1)}, bf16[1,352,2048]{2,1,0:T(8,128)(2,1)}) custom-call(bf16[272,2048]{1,0:T(8,128)(2,1)} %copy-done.2, bf16[272,2048]{1,0:T(8,128)(2,1)} %collective-permute-done.3.x_second.refs_1_, bf16[272,2048]{1,0:T(8,128)(2,1)} %copy-done.8, ...), custom_call_target="tpu_custom_call" | custom-call | flops 5000000000 | bytes 20000000 | tf_op jit(solution)/shard_map/own_grads/pallas_call | solution.py:338
  166.6 0.9 collective-permute-start.17
  167.6 0.9 collective-permute-done.13
  168.6 7.3 %collective-permute-done.17 = bf16[256,1024]{1,0:T(8,128)(2,1)S(1)} collective-permute-done((bf16[256,1024]{1,0:T(8,128)(2,1)S(1)}, bf16[256,1024]{1,0:T(8,128)(2,1)S(1)}, u32[]{:S(2)}, u32[]{:S(2)}) %collective-permute-start.17) | collective-permute-done | bytes 524320 | tf_op jit(solution)/shard_map/ppermute | solution.py:384
  176.6 2.3 %collective-permute-start.14 = (bf16[64,2048]{1,0:T(8,128)(2,1)S(1)}, bf16[64,2048]{1,0:T(8,128)(2,1)S(1)}, u32[]{:S(2)}, u32[]{:S(2)}) collective-permute-start(bf16[64,2048]{1,0:T(8,128)(2,1)S(1)} %slice_bitcast_fusion), channel_id=1, source_target_pairs={{0,4},{1,5},{2,6},{3,7},{4,0},{5,1},{6,2},{7,3},{8,12},{9,13},{10,... | collective-permute-start | bytes 786440 | tf_op jit(solution)/shard_map/ppermute | solution.py:384
  178.9 1.5 collective-permute-start.22
  180.4 9.7 %collective-permute-done.20 = bf16[2,64,1024]{2,1,0:T(8,128)(2,1)S(1)} collective-permute-done((bf16[2,64,1024]{2,1,0:T(8,128)(2,1)S(1)}, bf16[2,64,1024]{2,1,0:T(8,128)(2,1)S(1)}, u32[]{:S(2)}, u32[]{:S(2)}) %collective-permute-start.20) | collective-permute-done | bytes 262176 | tf_op jit(solution)/shard_map/ppermute | solution.py:384
  191.1 6.6 %collective-permute-done.21 = bf16[64,1024]{1,0:T(8,128)(2,1)S(1)} collective-permute-done((bf16[64,1024]{1,0:T(8,128)(2,1)S(1)}, bf16[64,1024]{1,0:T(8,128)(2,1)S(1)}, u32[]{:S(2)}, u32[]{:S(2)}) %collective-permute-start.21) | collective-permute-done | bytes 131104 | tf_op jit(solution)/shard_map/ppermute | solution.py:384
  198.1 2.7 %collective-permute-start.26 = (bf16[64,1024]{1,0:T(8,128)(2,1)S(1)}, bf16[64,1024]{1,0:T(8,128)(2,1)S(1)}, u32[]{:S(2)}, u32[]{:S(2)}) collective-permute-start(bf16[64,1024]{1,0:T(8,128)(2,1)S(1)} %get-tuple-element.91), channel_id=1, source_target_pairs={{0,6},{1,7},{2,4},{3,5},{4,2},{5,3},{6,0},{7,1},{8,14},{9,15},{10,... | collective-permute-start | bytes 393224 | tf_op jit(solution)/shard_map/ppermute | solution.py:384
  200.9 1.1 collective-permute-start.25
  202.6 2.4 %collective-permute-start.28 = (f32[4,64]{1,0:T(4,128)S(1)}, f32[4,64]{1,0:T(4,128)S(1)}, u32[]{:S(2)}, u32[]{:S(2)}) collective-permute-start(f32[4,64]{1,0:T(4,128)S(1)} %bitcast.69), channel_id=1, source_target_pairs={{0,4},{1,5},{2,6},{3,7},{4,0},{5,1},{6,2},{7,3},{8,12},{9,13},{10,... | collective-permute-start | bytes 3080 | tf_op jit(solution)/shard_map/ppermute | solution.py:384
  205.0 8.1 %collective-permute-done.28 = f32[4,64]{1,0:T(4,128)S(1)} collective-permute-done((f32[4,64]{1,0:T(4,128)S(1)}, f32[4,64]{1,0:T(4,128)S(1)}, u32[]{:S(2)}, u32[]{:S(2)}) %collective-permute-start.28) | collective-permute-done | bytes 1056 | tf_op jit(solution)/shard_map/ppermute | solution.py:384
  213.1 1.4 select_add_fusion
  (146 shorter events, 14.9 us)
Async XLA Ops:
  0.6 6.7 %copy-start = (bf16[512,2048]{1,0:T(8,128)(2,1)S(1)}, bf16[512,2048]{1,0:T(8,128)(2,1)}, u32[]{:S(2)}) copy-start(bf16[512,2048]{1,0:T(8,128)(2,1)} %param.8) | copy-start | bytes 6291460
  0.6 16.3 %collective-permute-start.6 = (bf16[64,2048]{1,0:T(8,128)(2,1)}, bf16[64,2048]{1,0:T(8,128)(2,1)}, u32[]{:S(2)}, u32[]{:S(2)}) collective-permute-start(bf16[64,2048]{1,0:T(8,128)(2,1)} %param.14), channel_id=1, source_target_pairs={{0,4},{1,5},{2,6},{3,7},{4,0},{5,1},{6,2},{7,3},{8,12},{9,13},{10,... | collective-permute-start | bytes 786440 | tf_op jit(solution)/shard_map/ppermute | solution.py:384
  7.3 9.7 %copy-start.30 = (bf16[64,2048]{1,0:T(8,128)(2,1)S(1)}, bf16[64,2048]{1,0:T(8,128)(2,1)}, u32[]{:S(2)}) copy-start(bf16[64,2048]{1,0:T(8,128)(2,1)} %param.14) | copy-start | bytes 786436
  10.2 39.4 %copy-start.2 = (bf16[272,2048]{1,0:T(8,128)(2,1)}, bf16[272,2048]{1,0:T(8,128)(2,1)S(1)}, u32[]{:S(2)}) copy-start(bf16[272,2048]{1,0:T(8,128)(2,1)S(1)} %pad_maximum_fusion.x_first.refs_0_) | copy-start | bytes 3342340
  10.2 22.7 %collective-permute-start.3 = (bf16[272,2048]{1,0:T(8,128)(2,1)S(1)}, bf16[272,2048]{1,0:T(8,128)(2,1)}, u32[]{:S(2)}, u32[]{:S(2)}) collective-permute-start(bf16[272,2048]{1,0:T(8,128)(2,1)S(1)} %pad_maximum_fusion.x_first.refs_0_), channel_id=1, source_target_pairs={{0,8},{1,17},{2,10},{3,19},{4,12},{5,21},{6,14},{7,23},{8,0},{9,25... | collective-permute-start | bytes 3342344 | tf_op jit(solution)/shard_map/ppermute | solution.py:384
  18.8 13.3 %collective-permute-start.7 = (bf16[128,2048]{1,0:T(8,128)(2,1)}, bf16[128,2048]{1,0:T(8,128)(2,1)S(1)}, u32[]{:S(2)}, u32[]{:S(2)}) collective-permute-start(bf16[128,2048]{1,0:T(8,128)(2,1)} %pad_maximum_fusion.1), channel_id=1, source_target_pairs={{0,2},{1,3},{2,0},{3,1},{4,6},{5,7},{6,4},{7,5},{8,10},{9,11},{10,... | collective-permute-start | bytes 1572872 | tf_op jit(solution)/shard_map/ppermute | solution.py:384
  19.5 16.8 %collective-permute-start.4 = (bf16[272,2048]{1,0:T(8,128)(2,1)S(1)}, bf16[272,2048]{1,0:T(8,128)(2,1)S(1)}, u32[]{:S(2)}, u32[]{:S(2)}) collective-permute-start(bf16[272,2048]{1,0:T(8,128)(2,1)S(1)} %pad_maximum_fusion.x_first.refs_0_), channel_id=1, source_target_pairs={{0,16},{1,9},{2,18},{3,11},{4,20},{5,13},{6,22},{7,15},{8,24},{9,1... | collective-permute-start | bytes 3342344 | tf_op jit(solution)/shard_map/ppermute | solution.py:384
  21.0 18.1 %collective-permute-start = (bf16[1,352,2048]{2,1,0:T(8,128)(2,1)}, bf16[1,352,2048]{2,1,0:T(8,128)(2,1)}, u32[]{:S(2)}, u32[]{:S(2)}) collective-permute-start(bf16[1,352,2048]{2,1,0:T(8,128)(2,1)} %gate.7), channel_id=1, source_target_pairs={{0,1},{1,0},{2,3},{3,2},{4,5},{5,4},{6,7},{7,6},{8,9},{9,8},{10,11... | collective-permute-start | bytes 4325384 | tf_op jit(solution)/shard_map/ppermute | solution.py:384
  21.0 18.5 %collective-permute-start.1 = (bf16[1,352,2048]{2,1,0:T(8,128)(2,1)}, bf16[1,352,2048]{2,1,0:T(8,128)(2,1)}, u32[]{:S(2)}, u32[]{:S(2)}) collective-permute-start(bf16[1,352,2048]{2,1,0:T(8,128)(2,1)} %up.7), channel_id=1, source_target_pairs={{0,1},{1,0},{2,3},{3,2},{4,5},{5,4},{6,7},{7,6},{8,9},{9,8},{10,11... | collective-permute-start | bytes 4325384 | tf_op jit(solution)/shard_map/ppermute | solution.py:384
  32.1 7.4 %collective-permute-start.2 = (bf16[1,352,2048]{2,1,0:T(8,128)(2,1)}, bf16[1,352,2048]{2,1,0:T(8,128)(2,1)}, u32[]{:S(2)}, u32[]{:S(2)}) collective-permute-start(bf16[1,352,2048]{2,1,0:T(8,128)(2,1)} %down.7), channel_id=1, source_target_pairs={{0,1},{1,0},{2,3},{3,2},{4,5},{5,4},{6,7},{7,6},{8,9},{9,8},{10,11... | collective-permute-start | bytes 4325384 | tf_op jit(solution)/shard_map/ppermute | solution.py:384
  33.0 23.3 %collective-permute-start.10 = (bf16[256,2048]{1,0:T(8,128)(2,1)}, bf16[256,2048]{1,0:T(8,128)(2,1)}, u32[]{:S(2)}, u32[]{:S(2)}) collective-permute-start(bf16[256,2048]{1,0:T(8,128)(2,1)} %constant_dynamic-update-slice_fusion.cot_first.refs_4_), channel_id=1, source_target_pairs={{0,8},{1,17},{2,10},{3,19},{4,12},{5,21},{6,14},{7,23},{8,0},{9,25... | collective-permute-start | bytes 3145736 | tf_op jit(solution)/shard_map/ppermute | solution.py:384
  36.3 23.3 %collective-permute-start.5 = (bf16[272,2048]{1,0:T(8,128)(2,1)}, bf16[272,2048]{1,0:T(8,128)(2,1)}, u32[]{:S(2)}, u32[]{:S(2)}) collective-permute-start(bf16[272,2048]{1,0:T(8,128)(2,1)} %collective-permute-done.3.x_second.refs_1_), channel_id=1, source_target_pairs={{0,16},{1,9},{2,18},{3,11},{4,20},{5,13},{6,22},{7,15},{8,24},{9,1... | collective-permute-start | bytes 3342344 | tf_op jit(solution)/shard_map/ppermute | solution.py:384
  38.1 1.0 copy-start.8
  39.1 35.3 %collective-permute-start.8 = (bf16[256,2048]{1,0:T(8,128)(2,1)}, bf16[256,2048]{1,0:T(8,128)(2,1)}, u32[]{:S(2)}, u32[]{:S(2)}) collective-permute-start(bf16[256,2048]{1,0:T(8,128)(2,1)} %constant_dynamic-update-slice_fusion.cot_first.refs_4_), channel_id=1, source_target_pairs={{0,16},{1,9},{2,18},{3,11},{4,20},{5,13},{6,22},{7,15},{8,24},{9,1... | collective-permute-start | bytes 3145736 | tf_op jit(solution)/shard_map/ppermute | solution.py:384
  39.5 1.4 copy-start.10
  49.6 0.9 copy-start.14
  50.5 1.2 copy-start.20
  51.7 1.2 copy-start.22
  52.8 0.9 copy-start.24
  56.3 32.4 %collective-permute-start.11 = (bf16[256,2048]{1,0:T(8,128)(2,1)}, bf16[256,2048]{1,0:T(8,128)(2,1)}, u32[]{:S(2)}, u32[]{:S(2)}) collective-permute-start(bf16[256,2048]{1,0:T(8,128)(2,1)} %collective-permute-done.10.cot_second.refs_5_), channel_id=1, source_target_pairs={{0,16},{1,9},{2,18},{3,11},{4,20},{5,13},{6,22},{7,15},{8,24},{9,1... | collective-permute-start | bytes 3145736 | tf_op jit(solution)/shard_map/ppermute | solution.py:384
  60.7 1.3 copy-start.9
  61.9 1.4 copy-start.11
  63.3 10.2 %copy-start.6 = (f32[512,1]{1,0:T(8,128)}, f32[512,1]{1,0:T(8,128)S(1)}, u32[]{:S(2)}) copy-start(f32[512,1]{1,0:T(8,128)S(1)} %copy.32.weight) | copy-start | bytes 6148
  63.3 12.7 %copy-start.12 = (bf16[1,352,2048]{2,1,0:T(8,128)(2,1)S(1)}, bf16[1,352,2048]{2,1,0:T(8,128)(2,1)}, u32[]{:S(2)}) copy-start(bf16[1,352,2048]{2,1,0:T(8,128)(2,1)} %down.7) | copy-start | bytes 4325380
  63.3 12.7 %copy-start.21 = (f32[512,768]{1,0:T(8,128)S(1)}, f32[512,768]{1,0:T(8,128)}, u32[]{:S(2)}) copy-start(f32[512,768]{1,0:T(8,128)} %copy-done.20) | copy-start | bytes 4718596
  63.3 12.7 %copy-start.23 = (f32[512,768]{1,0:T(8,128)S(1)}, f32[512,768]{1,0:T(8,128)}, u32[]{:S(2)}) copy-start(f32[512,768]{1,0:T(8,128)} %copy-done.22) | copy-start | bytes 4718596
  63.3 12.7 %copy-start.25 = (bf16[512,768]{1,0:T(8,128)(2,1)S(1)}, bf16[512,768]{1,0:T(8,128)(2,1)}, u32[]{:S(2)}) copy-start(bf16[512,768]{1,0:T(8,128)(2,1)} %copy-done.24) | copy-start | bytes 2359300
  73.5 0.9 copy-start.15
  74.4 56.0 %collective-permute-start.9 = (bf16[512,2048]{1,0:T(8,128)(2,1)}, bf16[512,2048]{1,0:T(8,128)(2,1)}, u32[]{:S(2)}, u32[]{:S(2)}) collective-permute-start(bf16[512,2048]{1,0:T(8,128)(2,1)} %get-tuple-element.46), channel_id=1, source_target_pairs={{0,16},{1,9},{2,18},{3,11},{4,20},{5,13},{6,22},{7,15},{8,24},{9,1... | collective-permute-start | bytes 6291464 | tf_op jit(solution)/shard_map/ppermute | solution.py:384
  76.0 12.7 %copy-start.7 = (f32[512,1]{1,0:T(8,128)S(1)}, f32[512,1]{1,0:T(8,128)}, u32[]{:S(2)}) copy-start(f32[512,1]{1,0:T(8,128)} %copy-done.6) | copy-start | bytes 6148
  85.2 1.0 copy-start.3
  86.2 0.7 copy-start.5
  86.9 0.9 copy-start.16
  87.8 0.9 copy-start.17
  98.0 1.0 copy-start.13
  99.0 0.9 copy-start.18
  99.9 0.9 copy-start.19
  111.4 44.4 %collective-permute-start.16 = (bf16[3,352,2048]{2,1,0:T(8,128)(2,1)}, bf16[3,352,2048]{2,1,0:T(8,128)(2,1)}, u32[]{:S(2)}, u32[]{:S(2)}) collective-permute-start(bf16[3,352,2048]{2,1,0:T(8,128)(2,1)} %other_grads.1), channel_id=1, source_target_pairs={{0,1},{1,0},{2,3},{3,2},{4,5},{5,4},{6,7},{7,6},{8,9},{9,8},{10,11... | collective-permute-start | bytes 12976136 | tf_op jit(solution)/shard_map/ppermute | solution.py:384
  112.7 15.1 %collective-permute-start.15 = (bf16[512,1024]{1,0:T(8,128)(2,1)}, bf16[512,1024]{1,0:T(8,128)(2,1)}, u32[]{:S(2)}, u32[]{:S(2)}) collective-permute-start(bf16[512,1024]{1,0:T(8,128)(2,1)} %get-tuple-element.58), channel_id=1, source_target_pairs={{0,16},{1,9},{2,18},{3,11},{4,20},{5,13},{6,22},{7,15},{8,24},{9,1... | collective-permute-start | bytes 3145736 | tf_op jit(solution)/shard_map/ppermute | solution.py:384
  127.8 21.7 %collective-permute-start.18 = (bf16[512,1024]{1,0:T(8,128)(2,1)}, bf16[512,1024]{1,0:T(8,128)(2,1)}, u32[]{:S(2)}, u32[]{:S(2)}) collective-permute-start(bf16[512,1024]{1,0:T(8,128)(2,1)} %copy-done.13), channel_id=1, source_target_pairs={{0,16},{1,9},{2,18},{3,11},{4,20},{5,13},{6,22},{7,15},{8,24},{9,1... | collective-permute-start | bytes 3145736 | tf_op jit(solution)/shard_map/ppermute | solution.py:384
  132.9 1.3 copy-start.26
  134.2 2.3 %copy-start.4 = (bf16[512,1024]{1,0:T(8,128)(2,1)S(1)}, bf16[512,1024]{1,0:T(8,128)(2,1)}, u32[]{:S(2)}) copy-start(bf16[512,1024]{1,0:T(8,128)(2,1)} %copy-done.3) | copy-start | bytes 3145732
  135.2 17.2 %collective-permute-start.12 = (bf16[256,2048]{1,0:T(8,128)(2,1)}, bf16[256,2048]{1,0:T(8,128)(2,1)}, u32[]{:S(2)}, u32[]{:S(2)}) collective-permute-start(bf16[256,2048]{1,0:T(8,128)(2,1)} %slice.267), channel_id=1, source_target_pairs={{0,8},{1,17},{2,10},{3,19},{4,12},{5,21},{6,14},{7,23},{8,0},{9,25... | collective-permute-start | bytes 3145736 | tf_op jit(solution)/shard_map/ppermute | solution.py:384
  135.9 13.5 %collective-permute-start.19 = (f32[2,256]{1,0:T(2,128)S(1)}, f32[2,256]{1,0:T(2,128)S(1)}, u32[]{:S(2)}, u32[]{:S(2)}) collective-permute-start(f32[2,256]{1,0:T(2,128)S(1)} %reshape.144), channel_id=1, source_target_pairs={{0,16},{1,9},{2,18},{3,11},{4,20},{5,13},{6,22},{7,15},{8,24},{9,1... | collective-permute-start | bytes 6152 | tf_op jit(solution)/shard_map/ppermute | solution.py:384
  138.1 1.0 copy-start.28
  139.1 13.3 %copy-start.27 = (bf16[512,2048]{1,0:T(8,128)(2,1)S(1)}, bf16[512,2048]{1,0:T(8,128)(2,1)}, u32[]{:S(2)}) copy-start(bf16[512,2048]{1,0:T(8,128)(2,1)} %copy-done.26) | copy-start | bytes 6291460
  149.5 48.2 %collective-permute-start.23 = (f32[2,256]{1,0:T(2,128)S(1)}, f32[2,256]{1,0:T(2,128)S(1)}, u32[]{:S(2)}, u32[]{:S(2)}) collective-permute-start(f32[2,256]{1,0:T(2,128)S(1)} %pad_maximum_fusion.6), channel_id=1, source_target_pairs={{0,8},{1,17},{2,10},{3,19},{4,12},{5,21},{6,14},{7,23},{8,0},{9,25... | collective-permute-start | bytes 6152 | tf_op jit(solution)/shard_map/ppermute | solution.py:384
  154.1 12.5 %copy-start.31 = (bf16[256,1024]{1,0:T(8,128)(2,1)S(1)}, bf16[256,1024]{1,0:T(8,128)(2,1)}, u32[]{:S(2)}) copy-start(bf16[256,1024]{1,0:T(8,128)(2,1)} %slice.273) | copy-start | bytes 1572868
  154.1 14.3 %collective-permute-start.13 = (bf16[2,64,2048]{2,1,0:T(8,128)(2,1)S(1)}, bf16[2,64,2048]{2,1,0:T(8,128)(2,1)S(1)}, u32[]{:S(2)}, u32[]{:S(2)}) collective-permute-start(bf16[2,64,2048]{2,1,0:T(8,128)(2,1)S(1)} %bitcast.58), channel_id=1, source_target_pairs={{0,2},{1,3},{2,0},{3,1},{4,6},{5,7},{6,4},{7,5},{8,10},{9,11},{10,... | collective-permute-start | bytes 1572872 | tf_op jit(solution)/shard_map/ppermute | solution.py:384
  166.6 9.3 %copy-start.29 = (bf16[512,1024]{1,0:T(8,128)(2,1)S(1)}, bf16[512,1024]{1,0:T(8,128)(2,1)}, u32[]{:S(2)}) copy-start(bf16[512,1024]{1,0:T(8,128)(2,1)} %copy-done.28) | copy-start | bytes 3145732
  166.6 9.2 %collective-permute-start.17 = (bf16[256,1024]{1,0:T(8,128)(2,1)S(1)}, bf16[256,1024]{1,0:T(8,128)(2,1)S(1)}, u32[]{:S(2)}, u32[]{:S(2)}) collective-permute-start(bf16[256,1024]{1,0:T(8,128)(2,1)S(1)} %copy-done.31), channel_id=1, source_target_pairs={{0,8},{1,17},{2,10},{3,19},{4,12},{5,21},{6,14},{7,23},{8,0},{9,25... | collective-permute-start | bytes 1572872 | tf_op jit(solution)/shard_map/ppermute | solution.py:384
  176.1 14.0 %collective-permute-start.20 = (bf16[2,64,1024]{2,1,0:T(8,128)(2,1)S(1)}, bf16[2,64,1024]{2,1,0:T(8,128)(2,1)S(1)}, u32[]{:S(2)}, u32[]{:S(2)}) collective-permute-start(bf16[2,64,1024]{2,1,0:T(8,128)(2,1)S(1)} %bitcast.59), channel_id=1, source_target_pairs={{0,2},{1,3},{2,0},{3,1},{4,6},{5,7},{6,4},{7,5},{8,10},{9,11},{10,... | collective-permute-start | bytes 786440 | tf_op jit(solution)/shard_map/ppermute | solution.py:384
  176.6 13.7 %collective-permute-start.14 = (bf16[64,2048]{1,0:T(8,128)(2,1)S(1)}, bf16[64,2048]{1,0:T(8,128)(2,1)S(1)}, u32[]{:S(2)}, u32[]{:S(2)}) collective-permute-start(bf16[64,2048]{1,0:T(8,128)(2,1)S(1)} %slice_bitcast_fusion), channel_id=1, source_target_pairs={{0,4},{1,5},{2,6},{3,7},{4,0},{5,1},{6,2},{7,3},{8,12},{9,13},{10,... | collective-permute-start | bytes 786440 | tf_op jit(solution)/shard_map/ppermute | solution.py:384
  178.9 18.8 %collective-permute-start.22 = (bf16[256,1024]{1,0:T(8,128)(2,1)S(1)}, bf16[256,1024]{1,0:T(8,128)(2,1)S(1)}, u32[]{:S(2)}, u32[]{:S(2)}) collective-permute-start(bf16[256,1024]{1,0:T(8,128)(2,1)S(1)} %slice.279), channel_id=1, source_target_pairs={{0,8},{1,17},{2,10},{3,19},{4,12},{5,21},{6,14},{7,23},{8,0},{9,25... | collective-permute-start | bytes 1572872 | tf_op jit(solution)/shard_map/ppermute | solution.py:384
  190.2 7.5 %collective-permute-start.21 = (bf16[64,1024]{1,0:T(8,128)(2,1)S(1)}, bf16[64,1024]{1,0:T(8,128)(2,1)S(1)}, u32[]{:S(2)}, u32[]{:S(2)}) collective-permute-start(bf16[64,1024]{1,0:T(8,128)(2,1)S(1)} %slice_bitcast_fusion.2), channel_id=1, source_target_pairs={{0,4},{1,5},{2,6},{3,7},{4,0},{5,1},{6,2},{7,3},{8,12},{9,13},{10,... | collective-permute-start | bytes 393224 | tf_op jit(solution)/shard_map/ppermute | solution.py:384
  190.3 25.0 %copy-start.1 = (bf16[512,2048]{1,0:T(8,128)(2,1)S(1)}, bf16[512,2048]{1,0:T(8,128)(2,1)}, u32[]{:S(2)}) copy-start(bf16[512,2048]{1,0:T(8,128)(2,1)} %param.8) | copy-start | bytes 6291460
  198.0 4.6 %collective-permute-start.27 = (f32[4,2,64]{2,1,0:T(2,128)S(1)}, f32[4,2,64]{2,1,0:T(2,128)S(1)}, u32[]{:S(2)}, u32[]{:S(2)}) collective-permute-start(f32[4,2,64]{2,1,0:T(2,128)S(1)} %slice.285), channel_id=1, source_target_pairs={{0,2},{1,3},{2,0},{3,1},{4,6},{5,7},{6,4},{7,5},{8,10},{9,11},{10,... | collective-permute-start | bytes 6152 | tf_op jit(solution)/shard_map/ppermute | solution.py:384
  198.1 16.4 %collective-permute-start.26 = (bf16[64,1024]{1,0:T(8,128)(2,1)S(1)}, bf16[64,1024]{1,0:T(8,128)(2,1)S(1)}, u32[]{:S(2)}, u32[]{:S(2)}) collective-permute-start(bf16[64,1024]{1,0:T(8,128)(2,1)S(1)} %get-tuple-element.91), channel_id=1, source_target_pairs={{0,6},{1,7},{2,4},{3,5},{4,2},{5,3},{6,0},{7,1},{8,14},{9,15},{10,... | collective-permute-start | bytes 393224 | tf_op jit(solution)/shard_map/ppermute | solution.py:384
  200.9 13.6 %collective-permute-start.25 = (bf16[64,1024]{1,0:T(8,128)(2,1)S(1)}, bf16[64,1024]{1,0:T(8,128)(2,1)S(1)}, u32[]{:S(2)}, u32[]{:S(2)}) collective-permute-start(bf16[64,1024]{1,0:T(8,128)(2,1)S(1)} %get-tuple-element.92), channel_id=1, source_target_pairs={{0,2},{1,3},{2,0},{3,1},{4,6},{5,7},{6,4},{7,5},{8,10},{9,11},{10,... | collective-permute-start | bytes 393224 | tf_op jit(solution)/shard_map/ppermute | solution.py:384
  202.0 12.5 %collective-permute-start.24 = (bf16[64,1024]{1,0:T(8,128)(2,1)S(1)}, bf16[64,1024]{1,0:T(8,128)(2,1)S(1)}, u32[]{:S(2)}, u32[]{:S(2)}) collective-permute-start(bf16[64,1024]{1,0:T(8,128)(2,1)S(1)} %get-tuple-element.90), channel_id=1, source_target_pairs={{0,4},{1,5},{2,6},{3,7},{4,0},{5,1},{6,2},{7,3},{8,12},{9,13},{10,... | collective-permute-start | bytes 393224 | tf_op jit(solution)/shard_map/ppermute | solution.py:384
  202.6 10.5 %collective-permute-start.28 = (f32[4,64]{1,0:T(4,128)S(1)}, f32[4,64]{1,0:T(4,128)S(1)}, u32[]{:S(2)}, u32[]{:S(2)}) collective-permute-start(f32[4,64]{1,0:T(4,128)S(1)} %bitcast.69), channel_id=1, source_target_pairs={{0,4},{1,5},{2,6},{3,7},{4,0},{5,1},{6,2},{7,3},{8,12},{9,13},{10,... | collective-permute-start | bytes 3080 | tf_op jit(solution)/shard_map/ppermute | solution.py:384

commit v2 on v1

--- a/solution.py
+++ b/solution.py
@@ -8,10 +8,11 @@
 SHARDS = 4
 CORES = 2
 LANES = 128
+UNIT_TILE = 256
+COLUMN_TILE = 512
 LEVEL_STEPS = (0, 2, 1, 3)
 PACKED_ROWS = 16
-VMEM_LIMIT = 32 * 1024 * 1024
-GRADS_VMEM = 56 * 1024 * 1024
+VMEM_LIMIT = 56 * 1024 * 1024
 
 
 def silu_parts(gate_pre):
@@ -164,6 +165,14 @@
     return copies
 
 
+def dot_columns(out, left, right):
+    for first in range(0, out.shape[1], COLUMN_TILE):
+        there = pl.ds(first, min(COLUMN_TILE, out.shape[1] - first))
+        out[:, there] = jnp.dot(
+            left[...], right[:, there], preferred_element_type=jnp.float32
+        ).astype(out.dtype)
+
+
 def load_rows(refs, buf, sems):
     rows = buf.shape[0] // len(refs)
     return [
@@ -174,63 +183,103 @@
     ]
 
 
+def start(copies):
+    for copy in copies:
+        copy.start()
+
+
+def wait(copies):
+    for copy in copies:
+        copy.wait()
+
+
+def copies_between(pairs, sems):
+    return [
+        pltpu.make_async_copy(source, place, sems.at[position])
+        for position, (source, place) in enumerate(pairs)
+    ]
+
+
 def forward_kernel(
     gate, gate_other, up, up_other, down, down_other, x_first, x_second, weight,
     mixed_out, hidden_out, weighted_out, to_gate_out, to_up_out,
-    row_buf, pre_buf, down_buf, row_sems, sems,
+    row_buf, pre_buf, down_buf, mixed, hidden, weighted, to_gate, to_up,
+    row_sems, sems, out_sems,
 ):
     both = down_buf.shape[0]
     loads = load_weights(
         (gate, gate_other, up, up_other, down, down_other), pre_buf, down_buf, sems
     )
-    loads += load_rows((x_first, x_second), row_buf, row_sems)
-    for load in loads:
-        load.start()
-    for load in loads:
-        load.wait()
-    gate_pre = dot_rows(row_buf[...], pre_buf[:both])
-    up_pre = dot_rows(row_buf[...], pre_buf[both:])
-    silu_value, silu_slope = silu_parts(gate_pre)
-    hidden = silu_value * up_pre
-    weighted = (hidden * weight[...]).astype(jnp.bfloat16)
-    hidden_out[...] = hidden.astype(jnp.bfloat16)
-    weighted_out[...] = weighted
-    to_gate_out[...] = up_pre * silu_slope
-    to_up_out[...] = silu_value
-    mixed_out[...] = jnp.dot(
-        weighted, down_buf[...], preferred_element_type=jnp.float32
-    ).astype(jnp.bfloat16)
+    rows = load_rows((x_first, x_second), row_buf, row_sems)
+    stores = copies_between(
+        (
+            (hidden, hidden_out),
+            (weighted, weighted_out),
+            (to_gate, to_gate_out),
+            (to_up, to_up_out),
+            (mixed, mixed_out),
+        ),
+        out_sems,
+    )
+    start(rows + loads)
+    wait(rows + loads[:4])
+    for first in range(0, both, UNIT_TILE):
+        there = pl.ds(first, UNIT_TILE)
+        gate_pre = dot_rows(row_buf[...], pre_buf[there])
+        up_pre = dot_rows(row_buf[...], pre_buf[pl.ds(both + first, UNIT_TILE)])
+        silu_value, silu_slope = silu_parts(gate_pre)
+        product = silu_value * up_pre
+        hidden[:, there] = product.astype(jnp.bfloat16)
+        weighted[:, there] = (product * weight[...]).astype(jnp.bfloat16)
+        to_gate[:, there] = up_pre * silu_slope
+        to_up[:, there] = silu_value
+    start(stores[:4])
+    wait(loads[4:])
+    dot_columns(mixed, weighted, down_buf)
+    start(stores[4:])
+    wait(stores)
 
 
 def backward_kernel(
     gate, gate_other, up, up_other, down, down_other, cot_first, cot_second, weight,
-    hidden, to_gate, to_up,
-    dx_left, dx_right, route_out, d_gate_out, d_up_out,
-    row_buf, pre_buf, down_buf, row_sems, sems,
+    hidden_in, to_gate_in, to_up_in,
+    dx_out, route_out, d_gate_out, d_up_out,
+    row_buf, pre_buf, down_buf, dx, d_pre, hidden, to_gate, to_up,
+    row_sems, sems, in_sems, out_sems,
 ):
     both = down_buf.shape[0]
     loads = load_weights(
         (gate, gate_other, up, up_other, down, down_other), pre_buf, down_buf, sems
     )
-    first = load_rows((cot_first, cot_second), row_buf, row_sems) + loads[4:]
-    for load in first + loads[:4]:
-        load.start()
-    for load in first:
-        load.wait()
-    plain = dot_rows(row_buf[...], down_buf[...])
-    route_out[...] = jnp.sum(plain * hidden[...].astype(jnp.float32), axis=1, keepdims=True)
-    d_hidden = plain * weight[...]
-    d_gate = (d_hidden * to_gate[...]).astype(jnp.bfloat16)
-    d_up = (d_hidden * to_up[...]).astype(jnp.bfloat16)
-    d_gate_out[...] = d_gate
-    d_up_out[...] = d_up
-    for load in loads[:4]:
-        load.wait()
-    dx = jnp.dot(d_gate, pre_buf[:both], preferred_element_type=jnp.float32)
-    dx = dx + jnp.dot(d_up, pre_buf[both:], preferred_element_type=jnp.float32)
-    columns = dx_left.shape[1]
-    dx_left[...] = dx[:, :columns].astype(jnp.bfloat16)
-    dx_right[...] = dx[:, columns:].astype(jnp.bfloat16)
+    rows = load_rows((cot_first, cot_second), row_buf, row_sems)
+    parts = copies_between(
+        ((hidden_in, hidden), (to_gate_in, to_gate), (to_up_in, to_up)), in_sems
+    )
+    stores = copies_between(
+        (
+            (d_pre.at[:, pl.ds(0, both)], d_gate_out),
+            (d_pre.at[:, pl.ds(both, both)], d_up_out),
+            (dx, dx_out),
+        ),
+        out_sems,
+    )
+    start(rows + loads[4:] + parts + loads[:4])
+    wait(rows + loads[4:] + parts)
+    route = None
+    for first in range(0, both, UNIT_TILE):
+        there = pl.ds(first, UNIT_TILE)
+        plain = dot_rows(row_buf[...], down_buf[there])
+        term = jnp.sum(plain * hidden[:, there].astype(jnp.float32), axis=1, keepdims=True)
+        route = term if route is None else route + term
+        d_hidden = plain * weight[...]
+        d_pre[:, there] = (d_hidden * to_gate[:, there]).astype(jnp.bfloat16)
+        d_pre[:, pl.ds(both + first, UNIT_TILE)] = (d_hidden * to_up[:, there]).astype(jnp.bfloat16)
+    route_out[...] = route
+    start(stores[:2])
+    wait(loads[:4])
+    dot_columns(dx, d_pre, pre_buf)
+    start(stores[2:])
+    wait(stores)
 
 
 WIDE, NARROW = 8, 6
@@ -277,26 +326,33 @@
     return [pl.BlockSpec(memory_space=space)] * count
 
 
-def row_kernel(kernel, name, matrices, pair, operands, outs):
+def row_kernel(kernel, name, matrices, pair, weight, parts, outs, in_vmem, buffers, copied):
     _, h, width = matrices[0].shape
     step = padded(h)
-    rows = operands[0].shape[0]
+    rows = weight.shape[0]
+    sems = [2, 6] + [len(parts)] * bool(parts) + [copied]
+    space = [pltpu.VMEM if position in in_vmem else pl.ANY for position in range(len(outs))]
     return pl.pallas_call(
         kernel,
         out_shape=outs,
-        in_specs=specs(pl.ANY, len(matrices) + 2) + specs(pltpu.VMEM, len(operands)),
-        out_specs=specs(pltpu.VMEM, len(outs)),
+        in_specs=specs(pl.ANY, len(matrices) + 2)
+        + specs(pltpu.VMEM, 1)
+        + specs(pl.ANY, len(parts)),
+        out_specs=[pl.BlockSpec(memory_space=kind) for kind in space],
         scratch_shapes=[
             pltpu.VMEM((rows, width), jnp.bfloat16),
             pltpu.VMEM((4 * step, width), jnp.bfloat16),
             pltpu.VMEM((2 * step, width), jnp.bfloat16),
-            pltpu.SemaphoreType.DMA((2,)),
-            pltpu.SemaphoreType.DMA((6,)),
+            *[
+                pltpu.VMEM(array.shape, array.dtype)
+                for array in (*buffers, *parts)
+            ],
+            *[pltpu.SemaphoreType.DMA((count,)) for count in sems],
         ],
         compiler_params=pltpu.CompilerParams(vmem_limit_bytes=VMEM_LIMIT),
         cost_estimate=cost(),
         name=name,
-    )(*matrices, *pair, *operands)
+    )(*matrices, *pair, weight, *parts)
 
 
 def forward(matrices, pair, weight):
@@ -305,18 +361,20 @@
     f32, bf16 = jnp.float32, jnp.bfloat16
     outs = [jax.ShapeDtypeStruct((rows, width), bf16)]
     outs += [jax.ShapeDtypeStruct((rows, units), kind) for kind in (bf16, bf16, f32, f32)]
-    return row_kernel(forward_kernel, "forward", matrices, pair, (weight,), outs)
+    return row_kernel(forward_kernel, "forward", matrices, pair, weight, (), outs, (), outs, 5)
 
 
 def backward(matrices, pair, weight, hidden, to_gate, to_up):
     rows, width = weight.shape[0], pair[0].shape[1]
     units = 2 * padded(matrices[0].shape[1])
     f32, bf16 = jnp.float32, jnp.bfloat16
-    outs = [jax.ShapeDtypeStruct((rows, width // 2), bf16)] * 2
-    outs += [jax.ShapeDtypeStruct((rows, 1), f32)]
+    outs = [jax.ShapeDtypeStruct((rows, width), bf16), jax.ShapeDtypeStruct((rows, 1), f32)]
     outs += [jax.ShapeDtypeStruct((rows, units), bf16)] * 2
-    operands = (weight, hidden, to_gate, to_up)
-    return row_kernel(backward_kernel, "backward", matrices, pair, operands, outs)
+    parts = (hidden, to_gate, to_up)
+    buffers = (outs[0], jax.ShapeDtypeStruct((rows, 2 * units), bf16))
+    return row_kernel(
+        backward_kernel, "backward", matrices, pair, weight, parts, outs, (1,), buffers, 3
+    )
 
 
 def weight_grads(wide, narrow, h, received=None):
@@ -341,7 +399,7 @@
         grid=(width // tile,),
         in_specs=in_specs,
         out_specs=out_specs,
-        compiler_params=pltpu.CompilerParams(vmem_limit_bytes=GRADS_VMEM),
+        compiler_params=pltpu.CompilerParams(vmem_limit_bytes=VMEM_LIMIT),
         cost_estimate=cost(),
         name=name,
     )(*wide, *narrow, *more)
@@ -404,9 +462,18 @@
     def after(value, *others):
         return lax.optimization_barrier((value, *others))[0]
 
-    def by_halving(blocks):
-        pair = add(blocks[:2], to_level(blocks[2:], 1))
-        return add(pair[0], to_level(pair[1], 2))
+    def in_blocks(terms):
+        return [term.reshape(levels, block, term.shape[-1]) for term in terms]
+
+    def by_blocks(terms, *wait_for):
+        terms = in_blocks(terms)
+        received = [
+            to_level(add(*[term[k] for term in terms]), step)
+            for k, step in enumerate(LEVEL_STEPS)
+            if k > 0
+        ]
+        own = after(terms[0][0], *wait_for)
+        return add(own, *[term[0] for term in terms[1:]], *received)
 
     level_order = jnp.array(LEVEL_STEPS, jnp.int32) ^ level
     block_order = level_order * CORES + core
@@ -430,71 +497,66 @@
     x_far = to_far(x_own)
     others = [to_core(matrix) for matrix in (w_gate, w_up, w_down)]
     matrices = (w_gate, others[0], w_up, others[1], w_down, others[2])
-    g_pair = jnp.concatenate([grad_out, to_level(grad_out, 2)], axis=0)
-    x_last = to_far(x_near)
+    cotangent = after(grad_out, x_own)
+    g_pair = jnp.concatenate([cotangent, to_level(cotangent, 2)], axis=0)
+    x_last = to_far(after(x_near, x_far))
     weight12 = jnp.concatenate([own_table, whole(x_near, 0)])[:, None]
     weight34 = jnp.concatenate([whole(x_far, 1), whole(x_last, 2)])[:, None]
 
     mixed12, hidden12, weighted12, *slopes12 = forward(matrices, (x_own, x_near), weight12)
     x_last = after(x_last, mixed12)
     g_own = jnp.concatenate([g_pair, to_level(g_pair, 1)], axis=0)
+    g_own = after(g_own, x_near, x_far)
     g_near = to_near(g_own)
-    g_far = to_far(g_own)
-    g_last = to_far(g_near)
+    g_far = to_far(after(g_own, x_last, g_near))
+    g_last = to_far(after(g_near, x_last))
+    dx12, route12, gate12, up12 = backward(
+        matrices, after((g_own, g_near), x_last), weight12, hidden12, *slopes12
+    )
+    x_far, x_last = after((x_far, x_last), dx12)
     mixed34, hidden34, weighted34, *slopes34 = forward(matrices, (x_far, x_last), weight34)
-    g_own, g_near = after((g_own, g_near), mixed34)
-    *dx12, route12, gate12, up12 = backward(
-        matrices, (g_own, g_near), weight12, hidden12, *slopes12
-    )
-    g_last = after(g_last, dx12)
-    *dx34, route34, gate34, up34 = backward(
+    g_last = after(g_last, mixed34)
+    dx34, route34, gate34, up34 = backward(
         matrices, (g_far, g_last), weight34, hidden34, *slopes34
     )
 
-    mixed_sum = add(mixed12, after(to_far(after(mixed34, g_far)), dx34))
-    mixed_near = to_near(mixed_sum[half:])
-    mixed = add(mixed_sum[:half], mixed_near).reshape(levels, block, width)
-    mixed = by_halving(mixed)
+    mixed_far = to_far(after(mixed34, g_far, g_last))
+    mixed_part = add(mixed12[half:], after(mixed_far, dx34)[half:])
+    mixed_near = to_near(mixed_part)
+
+    mixed_terms = in_blocks((mixed12[:half], mixed_far[:half], mixed_near))
+    mixed_pair = add(*[term[2:] for term in mixed_terms])
+    dx_far = to_far(dx34)
+    dx_part = add(dx12[half:], after(dx_far, mixed_pair)[half:])
+    dx_near = to_near(dx_part)
+    mixed_pair = after(to_level(mixed_pair, 1), dx_part)
+    mixed_last = to_level(add(*[term[1] for term in mixed_terms], mixed_pair[1]), 2)
 
     h = w_gate.shape[1]
     wide = (x_own, x_near, x_far, x_last, g_own, g_near, g_far, g_last)
-    narrow = (gate12, gate34, up12, up34, weighted12, weighted34)
+    narrow = after((gate12, gate34, up12, up34, weighted12, weighted34), mixed_far)
     received = to_core(weight_grads(wide, narrow, h))
     grads = weight_grads(wide, narrow, h, received)
 
-    route12 = route12.reshape(2, half)
-    left_far = to_far(dx34[0])
-    left_sum = add(dx12[0], left_far)
-    left_near = to_near(after(left_sum[half:], mixed_near, *grads))
-    right_far, route_far = lax.optimization_barrier(
-        (to_far(after(dx34[1], left_far)), to_far(route34.reshape(2, half)))
-    )
-    right_sum = add(dx12[1], right_far)
-    right_near = to_near(after(right_sum[half:], left_near))
-    route_near = to_near(jnp.stack([route12[1], route_far[1]]))
-
-    left_near = after(left_near, right_sum)
-    left = add(left_sum[:half], left_near).reshape(levels, block, width // 2)
-    left = by_halving(left)
-    right_near, route_near, *_ = lax.optimization_barrier((right_near, route_near, mixed))
-    right = add(right_sum[:half], right_near).reshape(levels, block, width // 2)
-    right = [right[0]] + [
-        to_level(right[k], step) for k, step in enumerate(LEVEL_STEPS) if k > 0
-    ]
-    right = add(*right)
-    grad_tokens = jnp.concatenate([left, right], axis=1)
-
-    route_own = jnp.stack([route12[0], route_far[0], route_near[0], route_near[1]])
-    route_own = route_own.reshape(dp_count, levels, block)
-    route_own = route_own[:, :2] + to_level(route_own[:, 2:], 1)
-    by_group = (route_own[:, 0], to_level(route_own[:, 1], 2))
+    route = jnp.concatenate([route12, route34]).reshape(dp_count, levels, block)
+    pair = after(to_level(route[:, 2:], 1), mixed_part)
+    other_group = after(to_level(route[:, 1] + pair[:, 1], 2), mixed_near)
+    route = jnp.stack([route[:, 0] + pair[:, 0], other_group], axis=1)
+    route_far = after(to_far(route[2:]), dx_near)
+    route_near = to_near(jnp.stack([route[1], route_far[1]]))
+
+    mixed_last = after(mixed_last, *grads)
+    mixed = add(*[term[0] for term in mixed_terms], mixed_pair[0], mixed_last)
+    grad_tokens = by_blocks((dx12[:half], dx_far[:half], dx_near), *grads)
+
+    route_own = jnp.stack([route[0], route_far[0], route_near[0], route_near[1]])
     my_routes = lax.dynamic_slice_in_dim(routes, ex_index * block, block, axis=0)
     my_group = ex_index // SHARDS
     grad_route = jnp.zeros(my_routes.shape, f32)
-    for values, group in zip(by_group, (my_group, 1 - my_group)):
+    for which, group in enumerate((my_group, 1 - my_group)):
         for position, d in enumerate((dp_index, far, near, dp_index ^ 3)):
             grad_route = grad_route + jnp.where(
-                my_routes == d * groups + group, values[position][:, None], 0.0
+                my_routes == d * groups + group, route_own[position, which][:, None], 0.0
             )
     return (mixed, grad_tokens, grad_route, *grads)
 

time: 216 us -> 206 us (0.954); the launches traced: 215 us -> 202 us
  local copies, waits for them, and re-layouts: 30.1 us -> 8.72 us
  Pallas kernels: 58.9 us -> 74.1 us
  other arithmetic: 15.6 us -> 12.2 us
  starting transfers between devices: 33.9 us -> 30.5 us
    unnamed x75 -> x30, local copies, waits for them, and re-layouts: 22.7 us -> 2.91 us
    pallas_call x4, Pallas kernels: 37.4 us -> 52.4 us  [row_kernel(): pl.pallas_call(kernel, out_shape=outs, in_specs=specs(pl.ANY, len(matrice...]
    ppermute x29 -> x25, starting transfers between devices: 33.9 us -> 30.5 us  [exchange(): return lax.ppermute(value, ('dp', 'expert'), pairs)]
    convert_element_type x11 -> x7, other arithmetic: 8.67 us -> 7.85 us  [add(): return total.astype(terms[0].dtype)]
    ppermute x29 -> x25, waiting for transfers between devices: 75.7 us -> 75 us  [exchange(): return lax.ppermute(value, ('dp', 'expert'), pairs)]
  transfers between devices with their start and end apart: 29 -> 25, of which waited for: 13 -> 11; matrix products, arithmetic and copies ran while one was open for 12% -> 8% of each run, Pallas kernels for 27% -> 37%
where the time goes in v2:
time: 206 us; the launch traced here: 202 us
  waiting for transfers between devices  75 us (36%)
  Pallas kernels  74.1 us (36%)
  starting transfers between devices  30.5 us (15%)
  other arithmetic  12.2 us (6%)
  local copies, waits for them, and re-layouts  8.72 us (4%)
    ppermute x25, waiting for transfers between devices, exchange(): return lax.ppermute(value, ('dp', 'expert'), pairs)  75 us
    pallas_call x4, Pallas kernels, row_kernel(): pl.pallas_call(kernel, out_shape=outs, in_specs=specs(pl.ANY, len(matrice...  52.4 us
    ppermute x25, starting transfers between devices, exchange(): return lax.ppermute(value, ('dp', 'expert'), pairs)  30.5 us
    pallas_call x2, Pallas kernels, weight_grads(): pl.pallas_call(kernel, out_shape=outs, grid=(width // tile,), in_specs=in...  21.8 us
    convert_element_type x7, other arithmetic, add(): return total.astype(terms[0].dtype)  7.85 us
  transfers between devices with their start and end apart: 25, of which 11 were waited for; matrix products, arithmetic and copies ran while one was open for 8% of the time, Pallas kernels for 37%

profile of v2, /device:TPU:0, one launch (start us, length us, event | category | flops | bytes accessed | tf_op | source)
XLA Modules:
  0.0 201.7 jit_solution(17278788335775227315)
XLA Ops:
  0.7 0.8 compare_select_fusion
  1.5 0.8 select_reduce_fusion
  2.4 0.1 reshape.153
  2.4 0.6 gather_fusion.1
  3.1 0.1 stack_reshape.11
  3.1 0.1 stack_reshape.10
  3.4 0.6 gather_fusion
  4.1 0.2 copy-done.8
  4.4 4.0 %collective-permute-start.6 = (bf16[64,2048]{1,0:T(8,128)(2,1)S(1)}, bf16[64,2048]{1,0:T(8,128)(2,1)S(1)}, u32[]{:S(2)}, u32[]{:S(2)}) collective-permute-start(bf16[64,2048]{1,0:T(8,128)(2,1)S(1)} %copy-done.8), channel_id=1, source_target_pairs={{0,4},{1,5},{2,6},{3,7},{4,0},{5,1},{6,2},{7,3},{8,12},{9,13},{10,... | collective-permute-start | bytes 786440 | tf_op jit(solution)/shard_map/ppermute | solution.py:442
  8.4 1.5 collective-permute-start.4
  9.9 1.5 collective-permute-start.3
  11.4 8.9 %collective-permute-done.6 = bf16[64,2048]{1,0:T(8,128)(2,1)S(1)} collective-permute-done((bf16[64,2048]{1,0:T(8,128)(2,1)S(1)}, bf16[64,2048]{1,0:T(8,128)(2,1)S(1)}, u32[]{:S(2)}, u32[]{:S(2)}) %collective-permute-start.6) | collective-permute-done | bytes 262176 | tf_op jit(solution)/shard_map/ppermute | solution.py:442
  20.4 0.8 collective-permute-start.7
  21.2 0.5 collective-permute-start.1
  21.7 11.9 %collective-permute-done.7 = bf16[128,2048]{1,0:T(8,128)(2,1)} collective-permute-done((bf16[128,2048]{1,0:T(8,128)(2,1)S(1)}, bf16[128,2048]{1,0:T(8,128)(2,1)}, u32[]{:S(2)}, u32[]{:S(2)}) %collective-permute-start.7) | collective-permute-done | bytes 524320 | tf_op jit(solution)/shard_map/ppermute | solution.py:442
  33.6 1.1 pad_maximum_fusion.1.cot_first.refs_4_
  34.8 1.0 collective-permute-done.4.x_first.refs_2_
  35.7 0.8 slice_bitcast_fusion.2
  36.6 1.6 collective-permute-start.5
  38.2 0.8 slice_bitcast_fusion.1
  39.1 0.9 copy.52.weight
  40.0 0.6 collective-permute-start.8
  40.7 11.2 %forward.2 = (bf16[512,2048]{1,0:T(8,128)(2,1)}, bf16[512,768]{1,0:T(8,128)(2,1)}, bf16[512,768]{1,0:T(8,128)(2,1)}, f32[512,768]{1,0:T(8,128)}, f32[512,768]{1,0:T(8,128)}) custom-call(bf16[1,352,2048]{2,1,0:T(8,128)(2,1)} %gate.7, bf16[1,352,2048]{2,1,0:T(8,128)(2,1)} %collective-permute-done.gate_other, bf16[1,352,2048]{2,1,0:T(8,128)(2,1)} %up.7, ...), custom_call_target="tpu_custom_call" | custom-call | flops 5000000000 | bytes 20000000 | tf_op jit(solution)/shard_map/forward/pallas_call | solution.py:335
  51.8 11.4 %collective-permute-done.5.x_second.refs_3_ = bf16[272,2048]{1,0:T(8,128)(2,1)} collective-permute-done((bf16[272,2048]{1,0:T(8,128)(2,1)}, bf16[272,2048]{1,0:T(8,128)(2,1)}, u32[]{:S(2)}, u32[]{:S(2)}) %collective-permute-start.5) | collective-permute-done | bytes 1114144 | tf_op jit(solution)/shard_map/ppermute | solution.py:442
  63.2 0.8 slice_bitcast_fusion
  64.1 1.6 collective-permute-start.9
  65.7 0.5 collective-permute-start.10
  66.2 0.9 copy.54.weight
  67.1 14.9 %backward.2 = (bf16[512,2048]{1,0:T(8,128)(2,1)}, f32[512,1]{1,0:T(8,128)}, bf16[512,768]{1,0:T(8,128)(2,1)}, bf16[512,768]{1,0:T(8,128)(2,1)}) custom-call(bf16[1,352,2048]{2,1,0:T(8,128)(2,1)} %gate.7, bf16[1,352,2048]{2,1,0:T(8,128)(2,1)} %collective-permute-done.gate_other, bf16[1,352,2048]{2,1,0:T(8,128)(2,1)} %up.7, ...), custom_call_target="tpu_custom_call" | custom-call | flops 5000000000 | bytes 20000000 | tf_op jit(solution)/shard_map/backward/pallas_call | solution.py:335
  82.0 11.3 %forward.3 = (bf16[512,2048]{1,0:T(8,128)(2,1)}, bf16[512,768]{1,0:T(8,128)(2,1)}, bf16[512,768]{1,0:T(8,128)(2,1)}, f32[512,768]{1,0:T(8,128)}, f32[512,768]{1,0:T(8,128)}) custom-call(bf16[1,352,2048]{2,1,0:T(8,128)(2,1)} %gate.7, bf16[1,352,2048]{2,1,0:T(8,128)(2,1)} %collective-permute-done.gate_other, bf16[1,352,2048]{2,1,0:T(8,128)(2,1)} %up.7, ...), custom_call_target="tpu_custom_call" | custom-call | flops 5000000000 | bytes 20000000 | tf_op jit(solution)/shard_map/forward/pallas_call | solution.py:335
  93.4 1.6 collective-permute-start.11
  95.0 15.0 %backward.3 = (bf16[512,2048]{1,0:T(8,128)(2,1)}, f32[512,1]{1,0:T(8,128)}, bf16[512,768]{1,0:T(8,128)(2,1)}, bf16[512,768]{1,0:T(8,128)(2,1)}) custom-call(bf16[1,352,2048]{2,1,0:T(8,128)(2,1)} %gate.7, bf16[1,352,2048]{2,1,0:T(8,128)(2,1)} %collective-permute-done.gate_other, bf16[1,352,2048]{2,1,0:T(8,128)(2,1)} %up.7, ...), custom_call_target="tpu_custom_call" | custom-call | flops 5000000000 | bytes 20000000 | tf_op jit(solution)/shard_map/backward/pallas_call | solution.py:335
  110.0 1.1 collective-permute-start.14
  111.0 8.7 %collective-permute-done.11 = bf16[512,2048]{1,0:T(8,128)(2,1)S(1)} collective-permute-done((bf16[512,2048]{1,0:T(8,128)(2,1)}, bf16[512,2048]{1,0:T(8,128)(2,1)S(1)}, u32[]{:S(2)}, u32[]{:S(2)}) %collective-permute-start.11) | collective-permute-done | bytes 2097184 | tf_op jit(solution)/shard_map/ppermute | solution.py:442
  119.7 0.4 add_convert_fusion.1
  120.1 0.2 collective-permute-start.12
  120.3 10.8 %other_grads.1 = bf16[3,352,2048]{2,1,0:T(8,128)(2,1)} custom-call(bf16[272,2048]{1,0:T(8,128)(2,1)} %copy-done.6, bf16[272,2048]{1,0:T(8,128)(2,1)} %collective-permute-done.3.x_second.refs_1_, bf16[272,2048]{1,0:T(8,128)(2,1)} %collective-permute-done.4.x_first.refs_2_, bf16[272,2048]{1,0:T(8,128)(2,1)} %collective-permute-done.5.x_second.refs_3_, ...), custom_call_target="tpu_custom_call" | custom-call | flops 5000000000 | bytes 20000000 | tf_op jit(solution)/shard_map/other_grads/pallas_call | solution.py:396
  131.3 0.1 copy.56
  131.4 1.1 copy.57
  132.6 1.6 collective-permute-start.21
  134.2 1.1 slice.279
  135.3 0.9 collective-permute-done.21
  136.2 10.1 %collective-permute-done.12 = bf16[256,2048]{1,0:T(8,128)(2,1)} collective-permute-done((bf16[256,2048]{1,0:T(8,128)(2,1)S(1)}, bf16[256,2048]{1,0:T(8,128)(2,1)}, u32[]{:S(2)}, u32[]{:S(2)}) %collective-permute-start.12) | collective-permute-done | bytes 1048608 | tf_op jit(solution)/shard_map/ppermute | solution.py:442
  146.4 1.6 add_convert_fusion.2
  148.0 5.4 %collective-permute-done.14 = bf16[512,2048]{1,0:T(8,128)(2,1)S(1)} collective-permute-done((bf16[512,2048]{1,0:T(8,128)(2,1)}, bf16[512,2048]{1,0:T(8,128)(2,1)S(1)}, u32[]{:S(2)}, u32[]{:S(2)}) %collective-permute-start.14) | collective-permute-done | bytes 2097184 | tf_op jit(solution)/shard_map/ppermute | solution.py:442
  153.4 0.4 add_convert_fusion
  153.8 0.2 collective-permute-start.17
  154.0 3.4 %collective-permute-start.22 = (f32[4,64]{1,0:T(4,128)S(1)}, f32[4,64]{1,0:T(4,128)S(1)}, u32[]{:S(2)}, u32[]{:S(2)}) collective-permute-start(f32[4,64]{1,0:T(4,128)S(1)} %bitcast.58), channel_id=1, source_target_pairs={{0,4},{1,5},{2,6},{3,7},{4,0},{5,1},{6,2},{7,3},{8,12},{9,13},{10,... | collective-permute-start | bytes 3080 | tf_op jit(solution)/shard_map/ppermute | solution.py:442
  157.4 1.7 collective-permute-start.13
  159.2 1.6 collective-permute-start.23
  160.8 8.1 %collective-permute-done.13 = bf16[2,64,2048]{2,1,0:T(8,128)(2,1)S(1)} collective-permute-done((bf16[2,64,2048]{2,1,0:T(8,128)(2,1)S(1)}, bf16[2,64,2048]{2,1,0:T(8,128)(2,1)S(1)}, u32[]{:S(2)}, u32[]{:S(2)}) %collective-permute-start.13) | collective-permute-done | bytes 524320 | tf_op jit(solution)/shard_map/ppermute | solution.py:442
  168.9 1.2 fusion
  170.1 0.7 collective-permute-start.15
  170.9 1.2 collective-permute-start.24
  172.1 0.4 add_convert_fusion.6
  172.5 2.7 %collective-permute-start.18 = (bf16[64,2048]{1,0:T(8,128)(2,1)S(1)}, bf16[64,2048]{1,0:T(8,128)(2,1)S(1)}, u32[]{:S(2)}, u32[]{:S(2)}) collective-permute-start(bf16[64,2048]{1,0:T(8,128)(2,1)S(1)} %get-tuple-element.104), channel_id=1, source_target_pairs={{0,4},{1,5},{2,6},{3,7},{4,0},{5,1},{6,2},{7,3},{8,12},{9,13},{10,... | collective-permute-start | bytes 786440 | tf_op jit(solution)/shard_map/ppermute | solution.py:442
  175.2 1.5 collective-permute-start.20
  176.6 0.3 collective-permute-start.19
  176.9 1.4 select_add_fusion
  178.3 10.9 %own_grads.1 = (bf16[1,352,2048]{2,1,0:T(8,128)(2,1)}, bf16[1,352,2048]{2,1,0:T(8,128)(2,1)}, bf16[1,352,2048]{2,1,0:T(8,128)(2,1)}) custom-call(bf16[272,2048]{1,0:T(8,128)(2,1)} %copy-done.6, bf16[272,2048]{1,0:T(8,128)(2,1)} %collective-permute-done.3.x_second.refs_1_, bf16[272,2048]{1,0:T(8,128)(2,1)} %collective-permute-done.4.x_first.refs_2_, ...), custom_call_target="tpu_custom_call" | custom-call | flops 5000000000 | bytes 20000000 | tf_op jit(solution)/shard_map/own_grads/pallas_call | solution.py:396
  189.2 5.0 %collective-permute-done.15 = bf16[64,2048]{1,0:T(8,128)(2,1)S(1)} collective-permute-done((bf16[64,2048]{1,0:T(8,128)(2,1)S(1)}, bf16[64,2048]{1,0:T(8,128)(2,1)S(1)}, u32[]{:S(2)}, u32[]{:S(2)}) %collective-permute-start.15) | collective-permute-done | bytes 262176 | tf_op jit(solution)/shard_map/ppermute | solution.py:442
  194.2 2.0 fusion.2
  196.1 3.6 %collective-permute-done.18 = bf16[64,2048]{1,0:T(8,128)(2,1)S(1)} collective-permute-done((bf16[64,2048]{1,0:T(8,128)(2,1)S(1)}, bf16[64,2048]{1,0:T(8,128)(2,1)S(1)}, u32[]{:S(2)}, u32[]{:S(2)}) %collective-permute-start.18) | collective-permute-done | bytes 262176 | tf_op jit(solution)/shard_map/ppermute | solution.py:442
  199.8 1.9 add_convert_fusion.3
  (82 shorter events, 0.9 us)
Async XLA Ops:
  0.6 2.8 %copy-start = (bf16[512,2048]{1,0:T(8,128)(2,1)S(1)}, bf16[512,2048]{1,0:T(8,128)(2,1)}, u32[]{:S(2)}) copy-start(bf16[512,2048]{1,0:T(8,128)(2,1)} %param.8) | copy-start | bytes 6291460
  3.4 1.0 copy-start.8
  4.4 36.3 %copy-start.6 = (bf16[272,2048]{1,0:T(8,128)(2,1)}, bf16[272,2048]{1,0:T(8,128)(2,1)S(1)}, u32[]{:S(2)}) copy-start(bf16[272,2048]{1,0:T(8,128)(2,1)S(1)} %pad_maximum_fusion.x_first.refs_0_) | copy-start | bytes 3342340
  4.4 16.0 %collective-permute-start.6 = (bf16[64,2048]{1,0:T(8,128)(2,1)S(1)}, bf16[64,2048]{1,0:T(8,128)(2,1)S(1)}, u32[]{:S(2)}, u32[]{:S(2)}) collective-permute-start(bf16[64,2048]{1,0:T(8,128)(2,1)S(1)} %copy-done.8), channel_id=1, source_target_pairs={{0,4},{1,5},{2,6},{3,7},{4,0},{5,1},{6,2},{7,3},{8,12},{9,13},{10,... | collective-permute-start | bytes 786440 | tf_op jit(solution)/shard_map/ppermute | solution.py:442
  8.4 27.3 %collective-permute-start.4 = (bf16[272,2048]{1,0:T(8,128)(2,1)S(1)}, bf16[272,2048]{1,0:T(8,128)(2,1)}, u32[]{:S(2)}, u32[]{:S(2)}) collective-permute-start(bf16[272,2048]{1,0:T(8,128)(2,1)S(1)} %pad_maximum_fusion.x_first.refs_0_), channel_id=1, source_target_pairs={{0,16},{1,9},{2,18},{3,11},{4,20},{5,13},{6,22},{7,15},{8,24},{9,1... | collective-permute-start | bytes 3342344 | tf_op jit(solution)/shard_map/ppermute | solution.py:442
  9.9 25.8 %collective-permute-start.3 = (bf16[272,2048]{1,0:T(8,128)(2,1)S(1)}, bf16[272,2048]{1,0:T(8,128)(2,1)}, u32[]{:S(2)}, u32[]{:S(2)}) collective-permute-start(bf16[272,2048]{1,0:T(8,128)(2,1)S(1)} %pad_maximum_fusion.x_first.refs_0_), channel_id=1, source_target_pairs={{0,8},{1,17},{2,10},{3,19},{4,12},{5,21},{6,14},{7,23},{8,0},{9,25... | collective-permute-start | bytes 3342344 | tf_op jit(solution)/shard_map/ppermute | solution.py:442
  20.4 13.3 %collective-permute-start.7 = (bf16[128,2048]{1,0:T(8,128)(2,1)S(1)}, bf16[128,2048]{1,0:T(8,128)(2,1)}, u32[]{:S(2)}, u32[]{:S(2)}) collective-permute-start(bf16[128,2048]{1,0:T(8,128)(2,1)S(1)} %pad_maximum_fusion.2), channel_id=1, source_target_pairs={{0,2},{1,3},{2,0},{3,1},{4,6},{5,7},{6,4},{7,5},{8,10},{9,11},{10,... | collective-permute-start | bytes 1572872 | tf_op jit(solution)/shard_map/ppermute | solution.py:442
  21.1 19.5 %collective-permute-start = (bf16[1,352,2048]{2,1,0:T(8,128)(2,1)}, bf16[1,352,2048]{2,1,0:T(8,128)(2,1)}, u32[]{:S(2)}, u32[]{:S(2)}) collective-permute-start(bf16[1,352,2048]{2,1,0:T(8,128)(2,1)} %gate.7), channel_id=1, source_target_pairs={{0,1},{1,0},{2,3},{3,2},{4,5},{5,4},{6,7},{7,6},{8,9},{9,8},{10,11... | collective-permute-start | bytes 4325384 | tf_op jit(solution)/shard_map/ppermute | solution.py:442
  21.2 19.5 %collective-permute-start.1 = (bf16[1,352,2048]{2,1,0:T(8,128)(2,1)}, bf16[1,352,2048]{2,1,0:T(8,128)(2,1)}, u32[]{:S(2)}, u32[]{:S(2)}) collective-permute-start(bf16[1,352,2048]{2,1,0:T(8,128)(2,1)} %up.7), channel_id=1, source_target_pairs={{0,1},{1,0},{2,3},{3,2},{4,5},{5,4},{6,7},{7,6},{8,9},{9,8},{10,11... | collective-permute-start | bytes 4325384 | tf_op jit(solution)/shard_map/ppermute | solution.py:442
  33.6 7.0 %collective-permute-start.2 = (bf16[1,352,2048]{2,1,0:T(8,128)(2,1)}, bf16[1,352,2048]{2,1,0:T(8,128)(2,1)}, u32[]{:S(2)}, u32[]{:S(2)}) collective-permute-start(bf16[1,352,2048]{2,1,0:T(8,128)(2,1)} %down.7), channel_id=1, source_target_pairs={{0,1},{1,0},{2,3},{3,2},{4,5},{5,4},{6,7},{7,6},{8,9},{9,8},{10,11... | collective-permute-start | bytes 4325384 | tf_op jit(solution)/shard_map/ppermute | solution.py:442
  34.8 29.4 %copy-start.7 = (bf16[256,2048]{1,0:T(8,128)(2,1)}, bf16[256,2048]{1,0:T(8,128)(2,1)S(1)}, u32[]{:S(2)}) copy-start(bf16[256,2048]{1,0:T(8,128)(2,1)S(1)} %pad_maximum_fusion.1.cot_first.refs_4_) | copy-start | bytes 3145732
  36.6 26.6 %collective-permute-start.5 = (bf16[272,2048]{1,0:T(8,128)(2,1)}, bf16[272,2048]{1,0:T(8,128)(2,1)}, u32[]{:S(2)}, u32[]{:S(2)}) collective-permute-start(bf16[272,2048]{1,0:T(8,128)(2,1)} %collective-permute-done.3.x_second.refs_1_), channel_id=1, source_target_pairs={{0,16},{1,9},{2,18},{3,11},{4,20},{5,13},{6,22},{7,15},{8,24},{9,1... | collective-permute-start | bytes 3342344 | tf_op jit(solution)/shard_map/ppermute | solution.py:442
  40.0 24.1 %collective-permute-start.8 = (bf16[256,2048]{1,0:T(8,128)(2,1)S(1)}, bf16[256,2048]{1,0:T(8,128)(2,1)}, u32[]{:S(2)}, u32[]{:S(2)}) collective-permute-start(bf16[256,2048]{1,0:T(8,128)(2,1)S(1)} %pad_maximum_fusion.1.cot_first.refs_4_), channel_id=1, source_target_pairs={{0,8},{1,17},{2,10},{3,19},{4,12},{5,21},{6,14},{7,23},{8,0},{9,25... | collective-permute-start | bytes 3145736 | tf_op jit(solution)/shard_map/ppermute | solution.py:442
  64.1 29.2 %collective-permute-start.9 = (bf16[256,2048]{1,0:T(8,128)(2,1)S(1)}, bf16[256,2048]{1,0:T(8,128)(2,1)S(1)}, u32[]{:S(2)}, u32[]{:S(2)}) collective-permute-start(bf16[256,2048]{1,0:T(8,128)(2,1)S(1)} %pad_maximum_fusion.1.cot_first.refs_4_), channel_id=1, source_target_pairs={{0,16},{1,9},{2,18},{3,11},{4,20},{5,13},{6,22},{7,15},{8,24},{9,1... | collective-permute-start | bytes 3145736 | tf_op jit(solution)/shard_map/ppermute | solution.py:442
  65.7 27.6 %collective-permute-start.10 = (bf16[256,2048]{1,0:T(8,128)(2,1)}, bf16[256,2048]{1,0:T(8,128)(2,1)}, u32[]{:S(2)}, u32[]{:S(2)}) collective-permute-start(bf16[256,2048]{1,0:T(8,128)(2,1)} %collective-permute-done.8.cot_second.refs_5_), channel_id=1, source_target_pairs={{0,16},{1,9},{2,18},{3,11},{4,20},{5,13},{6,22},{7,15},{8,24},{9,1... | collective-permute-start | bytes 3145736 | tf_op jit(solution)/shard_map/ppermute | solution.py:442
  93.4 1.6 copy-start.10
  93.4 26.3 %collective-permute-start.11 = (bf16[512,2048]{1,0:T(8,128)(2,1)}, bf16[512,2048]{1,0:T(8,128)(2,1)S(1)}, u32[]{:S(2)}, u32[]{:S(2)}) collective-permute-start(bf16[512,2048]{1,0:T(8,128)(2,1)} %get-tuple-element.70), channel_id=1, source_target_pairs={{0,16},{1,9},{2,18},{3,11},{4,20},{5,13},{6,22},{7,15},{8,24},{9,1... | collective-permute-start | bytes 6291464 | tf_op jit(solution)/shard_map/ppermute | solution.py:442
  95.0 24.7 %copy-start.4 = (bf16[512,2048]{1,0:T(8,128)(2,1)S(1)}, bf16[512,2048]{1,0:T(8,128)(2,1)}, u32[]{:S(2)}) copy-start(bf16[512,2048]{1,0:T(8,128)(2,1)} %get-tuple-element.53) | copy-start | bytes 6291460
  110.0 43.4 %collective-permute-start.14 = (bf16[512,2048]{1,0:T(8,128)(2,1)}, bf16[512,2048]{1,0:T(8,128)(2,1)S(1)}, u32[]{:S(2)}, u32[]{:S(2)}) collective-permute-start(bf16[512,2048]{1,0:T(8,128)(2,1)} %get-tuple-element.74), channel_id=1, source_target_pairs={{0,16},{1,9},{2,18},{3,11},{4,20},{5,13},{6,22},{7,15},{8,24},{9,1... | collective-permute-start | bytes 6291464 | tf_op jit(solution)/shard_map/ppermute | solution.py:442
  119.7 11.5 %copy-start.5 = (bf16[512,2048]{1,0:T(8,128)(2,1)}, bf16[512,2048]{1,0:T(8,128)(2,1)S(1)}, u32[]{:S(2)}) copy-start(bf16[512,2048]{1,0:T(8,128)(2,1)S(1)} %collective-permute-done.11) | copy-start | bytes 6291460
  120.1 11.2 %copy-start.9 = (f32[512,1]{1,0:T(8,128)S(1)}, f32[512,1]{1,0:T(8,128)}, u32[]{:S(2)}) copy-start(f32[512,1]{1,0:T(8,128)} %get-tuple-element.95) | copy-start | bytes 6148
  120.1 26.3 %collective-permute-start.12 = (bf16[256,2048]{1,0:T(8,128)(2,1)S(1)}, bf16[256,2048]{1,0:T(8,128)(2,1)}, u32[]{:S(2)}, u32[]{:S(2)}) collective-permute-start(bf16[256,2048]{1,0:T(8,128)(2,1)S(1)} %add_convert_fusion.1), channel_id=1, source_target_pairs={{0,8},{1,17},{2,10},{3,19},{4,12},{5,21},{6,14},{7,23},{8,0},{9,25... | collective-permute-start | bytes 3145736 | tf_op jit(solution)/shard_map/ppermute | solution.py:442
  131.2 47.1 %collective-permute-start.16 = (bf16[3,352,2048]{2,1,0:T(8,128)(2,1)}, bf16[3,352,2048]{2,1,0:T(8,128)(2,1)}, u32[]{:S(2)}, u32[]{:S(2)}) collective-permute-start(bf16[3,352,2048]{2,1,0:T(8,128)(2,1)} %other_grads.1), channel_id=1, source_target_pairs={{0,1},{1,0},{2,3},{3,2},{4,5},{5,4},{6,7},{7,6},{8,9},{9,8},{10,11... | collective-permute-start | bytes 12976136 | tf_op jit(solution)/shard_map/ppermute | solution.py:442
  132.6 3.7 %collective-permute-start.21 = (f32[4,2,64]{2,0,1:T(4,128)S(1)}, f32[4,2,64]{2,0,1:T(4,128)S(1)}, u32[]{:S(2)}, u32[]{:S(2)}) collective-permute-start(f32[4,2,64]{2,0,1:T(4,128)S(1)} %copy.62), channel_id=1, source_target_pairs={{0,2},{1,3},{2,0},{3,1},{4,6},{5,7},{6,4},{7,5},{8,10},{9,11},{10,... | collective-permute-start | bytes 6152 | tf_op jit(solution)/shard_map/ppermute | solution.py:442
  134.2 19.2 %copy-start.3 = (bf16[512,2048]{1,0:T(8,128)(2,1)S(1)}, bf16[512,2048]{1,0:T(8,128)(2,1)}, u32[]{:S(2)}) copy-start(bf16[512,2048]{1,0:T(8,128)(2,1)} %get-tuple-element.63) | copy-start | bytes 6291460
  153.4 18.7 %copy-start.2 = (bf16[512,2048]{1,0:T(8,128)(2,1)}, bf16[512,2048]{1,0:T(8,128)(2,1)S(1)}, u32[]{:S(2)}) copy-start(bf16[512,2048]{1,0:T(8,128)(2,1)S(1)} %collective-permute-done.14) | copy-start | bytes 6291460
  153.8 17.1 %collective-permute-start.17 = (bf16[256,2048]{1,0:T(8,128)(2,1)S(1)}, bf16[256,2048]{1,0:T(8,128)(2,1)S(1)}, u32[]{:S(2)}, u32[]{:S(2)}) collective-permute-start(bf16[256,2048]{1,0:T(8,128)(2,1)S(1)} %add_convert_fusion), channel_id=1, source_target_pairs={{0,8},{1,17},{2,10},{3,19},{4,12},{5,21},{6,14},{7,23},{8,0},{9,25... | collective-permute-start | bytes 3145736 | tf_op jit(solution)/shard_map/ppermute | solution.py:442
  154.0 5.1 %collective-permute-start.22 = (f32[4,64]{1,0:T(4,128)S(1)}, f32[4,64]{1,0:T(4,128)S(1)}, u32[]{:S(2)}, u32[]{:S(2)}) collective-permute-start(f32[4,64]{1,0:T(4,128)S(1)} %bitcast.58), channel_id=1, source_target_pairs={{0,4},{1,5},{2,6},{3,7},{4,0},{5,1},{6,2},{7,3},{8,12},{9,13},{10,... | collective-permute-start | bytes 3080 | tf_op jit(solution)/shard_map/ppermute | solution.py:442
  157.4 11.4 %collective-permute-start.13 = (bf16[2,64,2048]{2,1,0:T(8,128)(2,1)S(1)}, bf16[2,64,2048]{2,1,0:T(8,128)(2,1)S(1)}, u32[]{:S(2)}, u32[]{:S(2)}) collective-permute-start(bf16[2,64,2048]{2,1,0:T(8,128)(2,1)S(1)} %bitcast.45), channel_id=1, source_target_pairs={{0,2},{1,3},{2,0},{3,1},{4,6},{5,7},{6,4},{7,5},{8,10},{9,11},{10,... | collective-permute-start | bytes 1572872 | tf_op jit(solution)/shard_map/ppermute | solution.py:442
  159.2 11.7 %collective-permute-start.23 = (f32[2,2,64]{2,0,1:T(2,128)S(1)}, f32[2,2,64]{2,0,1:T(2,128)S(1)}, u32[]{:S(2)}, u32[]{:S(2)}) collective-permute-start(f32[2,2,64]{2,0,1:T(2,128)S(1)} %fusion.10), channel_id=1, source_target_pairs={{0,16},{1,9},{2,18},{3,11},{4,20},{5,13},{6,22},{7,15},{8,24},{9,1... | collective-permute-start | bytes 3080 | tf_op jit(solution)/shard_map/ppermute | solution.py:442
  170.1 24.0 %collective-permute-start.15 = (bf16[64,2048]{1,0:T(8,128)(2,1)S(1)}, bf16[64,2048]{1,0:T(8,128)(2,1)S(1)}, u32[]{:S(2)}, u32[]{:S(2)}) collective-permute-start(bf16[64,2048]{1,0:T(8,128)(2,1)S(1)} %fusion), channel_id=1, source_target_pairs={{0,4},{1,5},{2,6},{3,7},{4,0},{5,1},{6,2},{7,3},{8,12},{9,13},{10,... | collective-permute-start | bytes 786440 | tf_op jit(solution)/shard_map/ppermute | solution.py:442
  170.9 5.8 %collective-permute-start.24 = (f32[2,2,64]{2,0,1:T(2,128)S(1)}, f32[2,2,64]{2,0,1:T(2,128)S(1)}, u32[]{:S(2)}, u32[]{:S(2)}) collective-permute-start(f32[2,2,64]{2,0,1:T(2,128)S(1)} %fusion.11), channel_id=1, source_target_pairs={{0,8},{1,17},{2,10},{3,19},{4,12},{5,21},{6,14},{7,23},{8,0},{9,25... | collective-permute-start | bytes 3080 | tf_op jit(solution)/shard_map/ppermute | solution.py:442
  172.5 27.3 %collective-permute-start.18 = (bf16[64,2048]{1,0:T(8,128)(2,1)S(1)}, bf16[64,2048]{1,0:T(8,128)(2,1)S(1)}, u32[]{:S(2)}, u32[]{:S(2)}) collective-permute-start(bf16[64,2048]{1,0:T(8,128)(2,1)S(1)} %get-tuple-element.104), channel_id=1, source_target_pairs={{0,4},{1,5},{2,6},{3,7},{4,0},{5,1},{6,2},{7,3},{8,12},{9,13},{10,... | collective-permute-start | bytes 786440 | tf_op jit(solution)/shard_map/ppermute | solution.py:442
  175.2 24.6 %collective-permute-start.20 = (bf16[64,2048]{1,0:T(8,128)(2,1)S(1)}, bf16[64,2048]{1,0:T(8,128)(2,1)S(1)}, u32[]{:S(2)}, u32[]{:S(2)}) collective-permute-start(bf16[64,2048]{1,0:T(8,128)(2,1)S(1)} %get-tuple-element.105), channel_id=1, source_target_pairs={{0,6},{1,7},{2,4},{3,5},{4,2},{5,3},{6,0},{7,1},{8,14},{9,15},{10,... | collective-permute-start | bytes 786440 | tf_op jit(solution)/shard_map/ppermute | solution.py:442
  176.6 23.1 %collective-permute-start.19 = (bf16[64,2048]{1,0:T(8,128)(2,1)S(1)}, bf16[64,2048]{1,0:T(8,128)(2,1)S(1)}, u32[]{:S(2)}, u32[]{:S(2)}) collective-permute-start(bf16[64,2048]{1,0:T(8,128)(2,1)S(1)} %get-tuple-element.106), channel_id=1, source_target_pairs={{0,2},{1,3},{2,0},{3,1},{4,6},{5,7},{6,4},{7,5},{8,10},{9,11},{10,... | collective-permute-start | bytes 786440 | tf_op jit(solution)/shard_map/ppermute | solution.py:442
  178.3 23.4 %copy-start.1 = (bf16[512,2048]{1,0:T(8,128)(2,1)S(1)}, bf16[512,2048]{1,0:T(8,128)(2,1)}, u32[]{:S(2)}) copy-start(bf16[512,2048]{1,0:T(8,128)(2,1)} %param.8) | copy-start | bytes 6291460

commit v3 on v2

--- a/solution.py
+++ b/solution.py
@@ -200,86 +200,122 @@
     ]
 
 
-def forward_kernel(
-    gate, gate_other, up, up_other, down, down_other, x_first, x_second, weight,
-    mixed_out, hidden_out, weighted_out, to_gate_out, to_up_out,
-    row_buf, pre_buf, down_buf, mixed, hidden, weighted, to_gate, to_up,
-    row_sems, sems, out_sems,
-):
-    both = down_buf.shape[0]
-    loads = load_weights(
-        (gate, gate_other, up, up_other, down, down_other), pre_buf, down_buf, sems
-    )
-    rows = load_rows((x_first, x_second), row_buf, row_sems)
-    stores = copies_between(
-        (
-            (hidden, hidden_out),
-            (weighted, weighted_out),
-            (to_gate, to_gate_out),
-            (to_up, to_up_out),
-            (mixed, mixed_out),
-        ),
-        out_sems,
-    )
-    start(rows + loads)
-    wait(rows + loads[:4])
+def forward_units(rows, weight, pre, hidden, weighted, to_gate, to_up):
+    both = hidden.shape[1]
     for first in range(0, both, UNIT_TILE):
         there = pl.ds(first, UNIT_TILE)
-        gate_pre = dot_rows(row_buf[...], pre_buf[there])
-        up_pre = dot_rows(row_buf[...], pre_buf[pl.ds(both + first, UNIT_TILE)])
+        gate_pre = dot_rows(rows[...], pre[there])
+        up_pre = dot_rows(rows[...], pre[pl.ds(both + first, UNIT_TILE)])
         silu_value, silu_slope = silu_parts(gate_pre)
         product = silu_value * up_pre
         hidden[:, there] = product.astype(jnp.bfloat16)
         weighted[:, there] = (product * weight[...]).astype(jnp.bfloat16)
         to_gate[:, there] = up_pre * silu_slope
         to_up[:, there] = silu_value
-    start(stores[:4])
-    wait(loads[4:])
-    dot_columns(mixed, weighted, down_buf)
-    start(stores[4:])
-    wait(stores)
-
-
-def backward_kernel(
-    gate, gate_other, up, up_other, down, down_other, cot_first, cot_second, weight,
-    hidden_in, to_gate_in, to_up_in,
-    dx_out, route_out, d_gate_out, d_up_out,
-    row_buf, pre_buf, down_buf, dx, d_pre, hidden, to_gate, to_up,
-    row_sems, sems, in_sems, out_sems,
-):
-    both = down_buf.shape[0]
-    loads = load_weights(
-        (gate, gate_other, up, up_other, down, down_other), pre_buf, down_buf, sems
-    )
-    rows = load_rows((cot_first, cot_second), row_buf, row_sems)
-    parts = copies_between(
-        ((hidden_in, hidden), (to_gate_in, to_gate), (to_up_in, to_up)), in_sems
-    )
-    stores = copies_between(
-        (
-            (d_pre.at[:, pl.ds(0, both)], d_gate_out),
-            (d_pre.at[:, pl.ds(both, both)], d_up_out),
-            (dx, dx_out),
-        ),
-        out_sems,
-    )
-    start(rows + loads[4:] + parts + loads[:4])
-    wait(rows + loads[4:] + parts)
+
+
+def backward_units(rows, weight, down, hidden, to_gate, to_up, d_pre, route_out):
+    both = hidden.shape[1]
     route = None
     for first in range(0, both, UNIT_TILE):
         there = pl.ds(first, UNIT_TILE)
-        plain = dot_rows(row_buf[...], down_buf[there])
+        plain = dot_rows(rows[...], down[there])
         term = jnp.sum(plain * hidden[:, there].astype(jnp.float32), axis=1, keepdims=True)
         route = term if route is None else route + term
         d_hidden = plain * weight[...]
         d_pre[:, there] = (d_hidden * to_gate[:, there]).astype(jnp.bfloat16)
         d_pre[:, pl.ds(both + first, UNIT_TILE)] = (d_hidden * to_up[:, there]).astype(jnp.bfloat16)
     route_out[...] = route
-    start(stores[:2])
+
+
+def both_halves(d_pre):
+    both = d_pre.shape[1] // 2
+    return d_pre.at[:, pl.ds(0, both)], d_pre.at[:, pl.ds(both, both)]
+
+
+def forward_kernel(
+    gate, gate_other, up, up_other, down, down_other, x_first, x_second, weight,
+    mixed_out, hidden_out, weighted_out, to_gate_out, to_up_out,
+    pre_buf, down_buf, row_buf, mixed, hidden, weighted, to_gate, to_up,
+    sems, row_sems, out_sems,
+):
+    loads = load_weights(
+        (gate, gate_other, up, up_other, down, down_other), pre_buf, down_buf, sems
+    )
+    rows = load_rows((x_first, x_second), row_buf, row_sems)
+    kept = (hidden, weighted, to_gate, to_up)
+    outs = (hidden_out, weighted_out, to_gate_out, to_up_out)
+    stores = copies_between(((mixed, mixed_out), *zip(kept, outs)), out_sems)
+    start(rows + loads)
+    wait(rows + loads[:4])
+    forward_units(row_buf, weight, pre_buf, *kept)
+    start(stores[1:])
+    wait(loads[4:])
+    dot_columns(mixed, weighted, down_buf)
+    start(stores[:1])
+    wait(stores)
+
+
+def backward_kernel(
+    gate, gate_other, up, up_other, down, down_other, cot_first, cot_second, weight,
+    hidden_in, to_gate_in, to_up_in,
+    dx_out, route_out, d_gate_out, d_up_out,
+    pre_buf, down_buf, row_buf, dx, d_pre, hidden, to_gate, to_up,
+    sems, row_sems, in_sems, out_sems,
+):
+    loads = load_weights(
+        (gate, gate_other, up, up_other, down, down_other), pre_buf, down_buf, sems
+    )
+    rows = load_rows((cot_first, cot_second), row_buf, row_sems)
+    kept = (hidden, to_gate, to_up)
+    parts = copies_between(zip((hidden_in, to_gate_in, to_up_in), kept), in_sems)
+    d_gate, d_up = both_halves(d_pre)
+    stores = copies_between(((dx, dx_out), (d_gate, d_gate_out), (d_up, d_up_out)), out_sems)
+    start(rows + loads[4:] + parts + loads[:4])
+    wait(rows + loads[4:] + parts)
+    backward_units(row_buf, weight, down_buf, *kept, d_pre, route_out)
+    start(stores[1:])
     wait(loads[:4])
     dot_columns(dx, d_pre, pre_buf)
-    start(stores[2:])
+    start(stores[:1])
     wait(stores)
+
+
+def middle_kernel(
+    gate, gate_other, up, up_other, down, down_other,
+    x_first, x_second, cot_first, cot_second, weight34, weight12,
+    hidden_in, to_gate_in, to_up_in,
+    mixed_out, hidden_out, weighted_out, to_gate_out, to_up_out,
+    dx_out, route_out, d_gate_out, d_up_out,
+    pre_buf, down_buf, row_buf, cot_buf,
+    mixed, hidden34, weighted34, to_gate34, to_up34, dx, d_pre, hidden12, to_gate12, to_up12,
+    sems, row_sems, cot_sems, in_sems, out_sems, back_sems,
+):
+    loads = load_weights(
+        (gate, gate_other, up, up_other, down, down_other), pre_buf, down_buf, sems
+    )
+    rows = load_rows((x_first, x_second), row_buf, row_sems)
+    cots = load_rows((cot_first, cot_second), cot_buf, cot_sems)
+    kept34 = (hidden34, weighted34, to_gate34, to_up34)
+    kept12 = (hidden12, to_gate12, to_up12)
+    parts = copies_between(zip((hidden_in, to_gate_in, to_up_in), kept12), in_sems)
+    outs = (hidden_out, weighted_out, to_gate_out, to_up_out)
+    stores = copies_between(((mixed, mixed_out), *zip(kept34, outs)), out_sems)
+    d_gate, d_up = both_halves(d_pre)
+    back = copies_between(((dx, dx_out), (d_gate, d_gate_out), (d_up, d_up_out)), back_sems)
+    start(rows + loads + cots + parts)
+    wait(rows + loads[:4])
+    forward_units(row_buf, weight34, pre_buf, *kept34)
+    start(stores[1:])
+    wait(loads[4:])
+    dot_columns(mixed, weighted34, down_buf)
+    start(stores[:1])
+    wait(cots + parts)
+    backward_units(cot_buf, weight12, down_buf, *kept12, d_pre, route_out)
+    start(back[1:])
+    dot_columns(dx, d_pre, pre_buf)
+    start(back[:1])
+    wait(stores + back)
 
 
 WIDE, NARROW = 8, 6
@@ -326,55 +362,72 @@
     return [pl.BlockSpec(memory_space=space)] * count
 
 
-def row_kernel(kernel, name, matrices, pair, weight, parts, outs, in_vmem, buffers, copied):
+def buffers_for(arrays):
+    return [pltpu.VMEM(array.shape, array.dtype) for array in arrays]
+
+
+def row_kernel(kernel, name, matrices, pairs, weights, parts, outs, in_vmem, buffers, counts):
     _, h, width = matrices[0].shape
     step = padded(h)
-    rows = weight.shape[0]
-    sems = [2, 6] + [len(parts)] * bool(parts) + [copied]
+    rows = weights[0].shape[0]
     space = [pltpu.VMEM if position in in_vmem else pl.ANY for position in range(len(outs))]
+    own = [jax.ShapeDtypeStruct((n, width), jnp.bfloat16) for n in (4 * step, 2 * step)]
+    own += [jax.ShapeDtypeStruct((rows, width), jnp.bfloat16)] * (len(pairs) // 2)
     return pl.pallas_call(
         kernel,
         out_shape=outs,
-        in_specs=specs(pl.ANY, len(matrices) + 2)
-        + specs(pltpu.VMEM, 1)
+        in_specs=specs(pl.ANY, len(matrices) + len(pairs))
+        + specs(pltpu.VMEM, len(weights))
         + specs(pl.ANY, len(parts)),
         out_specs=[pl.BlockSpec(memory_space=kind) for kind in space],
-        scratch_shapes=[
-            pltpu.VMEM((rows, width), jnp.bfloat16),
-            pltpu.VMEM((4 * step, width), jnp.bfloat16),
-            pltpu.VMEM((2 * step, width), jnp.bfloat16),
-            *[
-                pltpu.VMEM(array.shape, array.dtype)
-                for array in (*buffers, *parts)
-            ],
-            *[pltpu.SemaphoreType.DMA((count,)) for count in sems],
-        ],
+        scratch_shapes=buffers_for((*own, *buffers, *parts))
+        + [pltpu.SemaphoreType.DMA((count,)) for count in counts],
         compiler_params=pltpu.CompilerParams(vmem_limit_bytes=VMEM_LIMIT),
         cost_estimate=cost(),
         name=name,
-    )(*matrices, *pair, weight, *parts)
-
-
-def forward(matrices, pair, weight):
-    rows, width = weight.shape[0], pair[0].shape[1]
+    )(*matrices, *pairs, *weights, *parts)
+
+
+def forward_outs(matrices, weight):
+    rows, width = weight.shape[0], matrices[0].shape[2]
     units = 2 * padded(matrices[0].shape[1])
     f32, bf16 = jnp.float32, jnp.bfloat16
     outs = [jax.ShapeDtypeStruct((rows, width), bf16)]
-    outs += [jax.ShapeDtypeStruct((rows, units), kind) for kind in (bf16, bf16, f32, f32)]
-    return row_kernel(forward_kernel, "forward", matrices, pair, weight, (), outs, (), outs, 5)
-
-
-def backward(matrices, pair, weight, hidden, to_gate, to_up):
-    rows, width = weight.shape[0], pair[0].shape[1]
+    return outs + [jax.ShapeDtypeStruct((rows, units), kind) for kind in (bf16, bf16, f32, f32)]
+
+
+def backward_outs(matrices, weight):
+    rows, width = weight.shape[0], matrices[0].shape[2]
     units = 2 * padded(matrices[0].shape[1])
     f32, bf16 = jnp.float32, jnp.bfloat16
     outs = [jax.ShapeDtypeStruct((rows, width), bf16), jax.ShapeDtypeStruct((rows, 1), f32)]
     outs += [jax.ShapeDtypeStruct((rows, units), bf16)] * 2
-    parts = (hidden, to_gate, to_up)
-    buffers = (outs[0], jax.ShapeDtypeStruct((rows, 2 * units), bf16))
+    return outs, [outs[0], jax.ShapeDtypeStruct((rows, 2 * units), bf16)]
+
+
+def forward(matrices, pair, weight):
+    outs = forward_outs(matrices, weight)
     return row_kernel(
-        backward_kernel, "backward", matrices, pair, weight, parts, outs, (1,), buffers, 3
-    )
+        forward_kernel, "forward", matrices, pair, (weight,), (), outs, (), outs, (6, 2, 5)
+    )
+
+
+def backward(matrices, pair, weight, parts):
+    outs, buffers = backward_outs(matrices, weight)
+    return row_kernel(
+        backward_kernel, "backward", matrices, pair, (weight,), parts, outs, (1,), buffers,
+        (6, 2, 3, 3),
+    )
+
+
+def middle(matrices, pair34, pair12, weight34, weight12, parts12):
+    ahead = forward_outs(matrices, weight34)
+    back, buffers = backward_outs(matrices, weight12)
+    result = row_kernel(
+        middle_kernel, "middle", matrices, (*pair34, *pair12), (weight34, weight12), parts12,
+        ahead + back, (len(ahead) + 1,), ahead + buffers, (6, 2, 2, 3, 5, 3),
+    )
+    return result[: len(ahead)], result[len(ahead) :]
 
 
 def weight_grads(wide, narrow, h, received=None):
@@ -510,14 +563,14 @@
     g_near = to_near(g_own)
     g_far = to_far(after(g_own, x_last, g_near))
     g_last = to_far(after(g_near, x_last))
-    dx12, route12, gate12, up12 = backward(
-        matrices, after((g_own, g_near), x_last), weight12, hidden12, *slopes12
-    )
-    x_far, x_last = after((x_far, x_last), dx12)
-    mixed34, hidden34, weighted34, *slopes34 = forward(matrices, (x_far, x_last), weight34)
+    ahead, back = middle(
+        matrices, (x_far, x_last), (g_own, g_near), weight34, weight12, (hidden12, *slopes12)
+    )
+    mixed34, hidden34, weighted34, *slopes34 = ahead
+    dx12, route12, gate12, up12 = back
     g_last = after(g_last, mixed34)
     dx34, route34, gate34, up34 = backward(
-        matrices, (g_far, g_last), weight34, hidden34, *slopes34
+        matrices, (g_far, g_last), weight34, (hidden34, *slopes34)
     )
 
     mixed_far = to_far(after(mixed34, g_far, g_last))

time: 206 us -> 202 us (0.981)
  Pallas kernels: 74.1 us -> 68.1 us
    pallas_call x4 -> x3, Pallas kernels: 52.4 us -> 46.3 us  [row_kernel(): pl.pallas_call(kernel, out_shape=outs, in_specs=specs(pl.ANY, len(matrice...]
  transfers between devices with their start and end apart: 25 -> 25, of which waited for: 11 -> 13; matrix products, arithmetic and copies ran while one was open for 8% -> 8% of each run, Pallas kernels for 37% -> 34%
where the time goes in v3:
time: 202 us; the launch traced here: 198 us
  waiting for transfers between devices  76.9 us (38%)
  Pallas kernels  68.1 us (34%)
  starting transfers between devices  31.5 us (16%)
  other arithmetic  12.2 us (6%)
  local copies, waits for them, and re-layouts  8.71 us (4%)
    ppermute x25, waiting for transfers between devices, exchange(): return lax.ppermute(value, ('dp', 'expert'), pairs)  76.9 us
    pallas_call x3, Pallas kernels, row_kernel(): pl.pallas_call(kernel, out_shape=outs, in_specs=specs(pl.ANY, len(matrice...  46.3 us
    ppermute x25, starting transfers between devices, exchange(): return lax.ppermute(value, ('dp', 'expert'), pairs)  31.5 us
    pallas_call x2, Pallas kernels, weight_grads(): pl.pallas_call(kernel, out_shape=outs, grid=(width // tile,), in_specs=in...  21.8 us
    convert_element_type x7, other arithmetic, add(): return total.astype(terms[0].dtype)  7.85 us
  transfers between devices with their start and end apart: 25, of which 13 were waited for; matrix products, arithmetic and copies ran while one was open for 8% of the time, Pallas kernels for 34%

profile of v3, /device:TPU:0, one launch (start us, length us, event | category | flops | bytes accessed | tf_op | source)
XLA Modules:
  0.0 198.5 jit_solution(4152183023949116696)
XLA Ops:
  0.7 0.8 compare_select_fusion
  1.5 0.8 select_reduce_fusion
  2.4 0.1 reshape.153
  2.4 0.6 gather_fusion.1
  3.1 0.1 stack_reshape.11
  3.1 0.1 stack_reshape.10
  3.4 0.6 gather_fusion
  4.1 0.2 copy-done.8
  4.4 4.0 %collective-permute-start.6 = (bf16[64,2048]{1,0:T(8,128)(2,1)S(1)}, bf16[64,2048]{1,0:T(8,128)(2,1)S(1)}, u32[]{:S(2)}, u32[]{:S(2)}) collective-permute-start(bf16[64,2048]{1,0:T(8,128)(2,1)S(1)} %copy-done.8), channel_id=1, source_target_pairs={{0,4},{1,5},{2,6},{3,7},{4,0},{5,1},{6,2},{7,3},{8,12},{9,13},{10,... | collective-permute-start | bytes 786440 | tf_op jit(solution)/shard_map/ppermute | solution.py:495
  8.4 1.5 collective-permute-start.4
  9.9 1.5 collective-permute-start.3
  11.4 8.9 %collective-permute-done.6 = bf16[64,2048]{1,0:T(8,128)(2,1)S(1)} collective-permute-done((bf16[64,2048]{1,0:T(8,128)(2,1)S(1)}, bf16[64,2048]{1,0:T(8,128)(2,1)S(1)}, u32[]{:S(2)}, u32[]{:S(2)}) %collective-permute-start.6) | collective-permute-done | bytes 262176 | tf_op jit(solution)/shard_map/ppermute | solution.py:495
  20.4 0.8 collective-permute-start.7
  21.2 0.5 collective-permute-start.1
  21.7 11.9 %collective-permute-done.7 = bf16[128,2048]{1,0:T(8,128)(2,1)} collective-permute-done((bf16[128,2048]{1,0:T(8,128)(2,1)S(1)}, bf16[128,2048]{1,0:T(8,128)(2,1)}, u32[]{:S(2)}, u32[]{:S(2)}) %collective-permute-start.7) | collective-permute-done | bytes 524320 | tf_op jit(solution)/shard_map/ppermute | solution.py:495
  33.6 1.1 pad_maximum_fusion.1.cot_first.refs_4_
  34.8 1.0 collective-permute-done.4.x_first.refs_2_
  35.7 0.8 slice_bitcast_fusion.2
  36.6 0.7 collective-permute-start.8
  37.3 1.5 collective-permute-start.5
  38.8 0.8 slice_bitcast_fusion.1
  39.8 0.9 copy.52.weight.weight12
  40.7 11.2 %forward.1 = (bf16[512,2048]{1,0:T(8,128)(2,1)}, bf16[512,768]{1,0:T(8,128)(2,1)}, bf16[512,768]{1,0:T(8,128)(2,1)}, f32[512,768]{1,0:T(8,128)}, f32[512,768]{1,0:T(8,128)}) custom-call(bf16[1,352,2048]{2,1,0:T(8,128)(2,1)} %gate.5, bf16[1,352,2048]{2,1,0:T(8,128)(2,1)} %collective-permute-done.gate_other, bf16[1,352,2048]{2,1,0:T(8,128)(2,1)} %up.5, ...), custom_call_target="tpu_custom_call" | custom-call | flops 5000000000 | bytes 20000000 | tf_op jit(solution)/shard_map/forward/pallas_call | solution.py:376
  51.8 10.6 %collective-permute-done.5.x_second.refs_3_ = bf16[272,2048]{1,0:T(8,128)(2,1)} collective-permute-done((bf16[272,2048]{1,0:T(8,128)(2,1)}, bf16[272,2048]{1,0:T(8,128)(2,1)}, u32[]{:S(2)}, u32[]{:S(2)}) %collective-permute-start.5) | collective-permute-done | bytes 1114144 | tf_op jit(solution)/shard_map/ppermute | solution.py:495
  62.5 1.8 collective-permute-start.9
  64.3 0.3 collective-permute-start.10
  64.6 0.8 slice_bitcast_fusion
  65.5 0.9 copy.53.weight34.weight
  66.4 20.1 %middle.1 = (bf16[512,2048]{1,0:T(8,128)(2,1)}, bf16[512,768]{1,0:T(8,128)(2,1)}, bf16[512,768]{1,0:T(8,128)(2,1)}, f32[512,768]{1,0:T(8,128)}, f32[512,768]{1,0...) custom-call(bf16[1,352,2048]{2,1,0:T(8,128)(2,1)} %gate.5, ...), custom_call_target="tpu_custom_call" | custom-call | flops 5000000000 | bytes 20000000 | tf_op jit(solution)/shard_map/middle/pallas_call | solution.py:376
  86.5 2.2 %collective-permute-done.10.cot_second.refs_7_ = bf16[256,2048]{1,0:T(8,128)(2,1)} collective-permute-done((bf16[256,2048]{1,0:T(8,128)(2,1)}, bf16[256,2048]{1,0:T(8,128)(2,1)}, u32[]{:S(2)}, u32[]{:S(2)}) %collective-permute-start.10) | collective-permute-done | bytes 1048608 | tf_op jit(solution)/shard_map/ppermute | solution.py:495
  88.7 1.8 collective-permute-start.11
  90.4 15.0 %backward.1 = (bf16[512,2048]{1,0:T(8,128)(2,1)}, f32[512,1]{1,0:T(8,128)}, bf16[512,768]{1,0:T(8,128)(2,1)}, bf16[512,768]{1,0:T(8,128)(2,1)}) custom-call(bf16[1,352,2048]{2,1,0:T(8,128)(2,1)} %gate.5, bf16[1,352,2048]{2,1,0:T(8,128)(2,1)} %collective-permute-done.gate_other, bf16[1,352,2048]{2,1,0:T(8,128)(2,1)} %up.5, ...), custom_call_target="tpu_custom_call" | custom-call | flops 5000000000 | bytes 20000000 | tf_op jit(solution)/shard_map/backward/pallas_call | solution.py:376
  105.4 0.3 collective-permute-start.14
  105.8 9.1 %collective-permute-done.11 = bf16[512,2048]{1,0:T(8,128)(2,1)S(1)} collective-permute-done((bf16[512,2048]{1,0:T(8,128)(2,1)}, bf16[512,2048]{1,0:T(8,128)(2,1)S(1)}, u32[]{:S(2)}, u32[]{:S(2)}) %collective-permute-start.11) | collective-permute-done | bytes 2097184 | tf_op jit(solution)/shard_map/ppermute | solution.py:495
  114.9 0.4 add_convert_fusion.1
  115.3 1.0 collective-permute-start.12
  116.3 10.8 %other_grads.1 = bf16[3,352,2048]{2,1,0:T(8,128)(2,1)} custom-call(bf16[272,2048]{1,0:T(8,128)(2,1)} %copy-done.6, bf16[272,2048]{1,0:T(8,128)(2,1)} %collective-permute-done.3.x_second.refs_1_, bf16[272,2048]{1,0:T(8,128)(2,1)} %collective-permute-done.4.x_first.refs_2_, bf16[272,2048]{1,0:T(8,128)(2,1)} %collective-permute-done.5.x_second.refs_3_, ...), custom_call_target="tpu_custom_call" | custom-call | flops 5000000000 | bytes 20000000 | tf_op jit(solution)/shard_map/other_grads/pallas_call | solution.py:449
  127.3 0.1 copy.56
  127.4 1.1 copy.57
  128.6 1.8 collective-permute-start.21
  130.3 1.1 slice.279
  131.4 0.8 collective-permute-done.21
  132.2 9.4 %collective-permute-done.12 = bf16[256,2048]{1,0:T(8,128)(2,1)} collective-permute-done((bf16[256,2048]{1,0:T(8,128)(2,1)S(1)}, bf16[256,2048]{1,0:T(8,128)(2,1)}, u32[]{:S(2)}, u32[]{:S(2)}) %collective-permute-start.12) | collective-permute-done | bytes 1048608 | tf_op jit(solution)/shard_map/ppermute | solution.py:495
  141.6 1.6 add_convert_fusion.2
  143.2 5.4 %collective-permute-done.14 = bf16[512,2048]{1,0:T(8,128)(2,1)S(1)} collective-permute-done((bf16[512,2048]{1,0:T(8,128)(2,1)}, bf16[512,2048]{1,0:T(8,128)(2,1)S(1)}, u32[]{:S(2)}, u32[]{:S(2)}) %collective-permute-start.14) | collective-permute-done | bytes 2097184 | tf_op jit(solution)/shard_map/ppermute | solution.py:495
  148.6 0.4 add_convert_fusion
  149.0 1.0 collective-permute-start.17
  150.0 3.3 %collective-permute-start.22 = (f32[4,64]{1,0:T(4,128)S(1)}, f32[4,64]{1,0:T(4,128)S(1)}, u32[]{:S(2)}, u32[]{:S(2)}) collective-permute-start(f32[4,64]{1,0:T(4,128)S(1)} %bitcast.58), channel_id=1, source_target_pairs={{0,4},{1,5},{2,6},{3,7},{4,0},{5,1},{6,2},{7,3},{8,12},{9,13},{10,... | collective-permute-start | bytes 3080 | tf_op jit(solution)/shard_map/ppermute | solution.py:495
  153.4 1.7 collective-permute-start.13
  155.1 1.6 collective-permute-start.23
  156.7 8.5 %collective-permute-done.13 = bf16[2,64,2048]{2,1,0:T(8,128)(2,1)S(1)} collective-permute-done((bf16[2,64,2048]{2,1,0:T(8,128)(2,1)S(1)}, bf16[2,64,2048]{2,1,0:T(8,128)(2,1)S(1)}, u32[]{:S(2)}, u32[]{:S(2)}) %collective-permute-start.13) | collective-permute-done | bytes 524320 | tf_op jit(solution)/shard_map/ppermute | solution.py:495
  165.2 1.2 fusion
  166.5 0.4 collective-permute-start.15
  166.9 1.6 collective-permute-start.24
  168.4 0.4 add_convert_fusion.6
  168.8 2.7 %collective-permute-start.18 = (bf16[64,2048]{1,0:T(8,128)(2,1)S(1)}, bf16[64,2048]{1,0:T(8,128)(2,1)S(1)}, u32[]{:S(2)}, u32[]{:S(2)}) collective-permute-start(bf16[64,2048]{1,0:T(8,128)(2,1)S(1)} %get-tuple-element.96), channel_id=1, source_target_pairs={{0,4},{1,5},{2,6},{3,7},{4,0},{5,1},{6,2},{7,3},{8,12},{9,13},{10,... | collective-permute-start | bytes 786440 | tf_op jit(solution)/shard_map/ppermute | solution.py:495
  171.5 1.5 collective-permute-start.20
  173.0 0.3 collective-permute-start.19
  173.3 1.4 select_add_fusion
  174.6 10.9 %own_grads.1 = (bf16[1,352,2048]{2,1,0:T(8,128)(2,1)}, bf16[1,352,2048]{2,1,0:T(8,128)(2,1)}, bf16[1,352,2048]{2,1,0:T(8,128)(2,1)}) custom-call(bf16[272,2048]{1,0:T(8,128)(2,1)} %copy-done.6, bf16[272,2048]{1,0:T(8,128)(2,1)} %collective-permute-done.3.x_second.refs_1_, bf16[272,2048]{1,0:T(8,128)(2,1)} %collective-permute-done.4.x_first.refs_2_, ...), custom_call_target="tpu_custom_call" | custom-call | flops 5000000000 | bytes 20000000 | tf_op jit(solution)/shard_map/own_grads/pallas_call | solution.py:449
  185.6 5.4 %collective-permute-done.15 = bf16[64,2048]{1,0:T(8,128)(2,1)S(1)} collective-permute-done((bf16[64,2048]{1,0:T(8,128)(2,1)S(1)}, bf16[64,2048]{1,0:T(8,128)(2,1)S(1)}, u32[]{:S(2)}, u32[]{:S(2)}) %collective-permute-start.15) | collective-permute-done | bytes 262176 | tf_op jit(solution)/shard_map/ppermute | solution.py:495
  191.0 2.0 fusion.2
  192.9 3.6 %collective-permute-done.18 = bf16[64,2048]{1,0:T(8,128)(2,1)S(1)} collective-permute-done((bf16[64,2048]{1,0:T(8,128)(2,1)S(1)}, bf16[64,2048]{1,0:T(8,128)(2,1)S(1)}, u32[]{:S(2)}, u32[]{:S(2)}) %collective-permute-start.18) | collective-permute-done | bytes 262176 | tf_op jit(solution)/shard_map/ppermute | solution.py:495
  196.6 1.9 add_convert_fusion.3
  (79 shorter events, 0.9 us)
Async XLA Ops:
  0.6 2.8 %copy-start = (bf16[512,2048]{1,0:T(8,128)(2,1)S(1)}, bf16[512,2048]{1,0:T(8,128)(2,1)}, u32[]{:S(2)}) copy-start(bf16[512,2048]{1,0:T(8,128)(2,1)} %param.8) | copy-start | bytes 6291460
  3.4 1.0 copy-start.8
  4.4 36.3 %copy-start.6 = (bf16[272,2048]{1,0:T(8,128)(2,1)}, bf16[272,2048]{1,0:T(8,128)(2,1)S(1)}, u32[]{:S(2)}) copy-start(bf16[272,2048]{1,0:T(8,128)(2,1)S(1)} %pad_maximum_fusion.x_first.refs_0_) | copy-start | bytes 3342340
  4.4 16.0 %collective-permute-start.6 = (bf16[64,2048]{1,0:T(8,128)(2,1)S(1)}, bf16[64,2048]{1,0:T(8,128)(2,1)S(1)}, u32[]{:S(2)}, u32[]{:S(2)}) collective-permute-start(bf16[64,2048]{1,0:T(8,128)(2,1)S(1)} %copy-done.8), channel_id=1, source_target_pairs={{0,4},{1,5},{2,6},{3,7},{4,0},{5,1},{6,2},{7,3},{8,12},{9,13},{10,... | collective-permute-start | bytes 786440 | tf_op jit(solution)/shard_map/ppermute | solution.py:495
  8.4 27.3 %collective-permute-start.4 = (bf16[272,2048]{1,0:T(8,128)(2,1)S(1)}, bf16[272,2048]{1,0:T(8,128)(2,1)}, u32[]{:S(2)}, u32[]{:S(2)}) collective-permute-start(bf16[272,2048]{1,0:T(8,128)(2,1)S(1)} %pad_maximum_fusion.x_first.refs_0_), channel_id=1, source_target_pairs={{0,16},{1,9},{2,18},{3,11},{4,20},{5,13},{6,22},{7,15},{8,24},{9,1... | collective-permute-start | bytes 3342344 | tf_op jit(solution)/shard_map/ppermute | solution.py:495
  9.9 25.8 %collective-permute-start.3 = (bf16[272,2048]{1,0:T(8,128)(2,1)S(1)}, bf16[272,2048]{1,0:T(8,128)(2,1)}, u32[]{:S(2)}, u32[]{:S(2)}) collective-permute-start(bf16[272,2048]{1,0:T(8,128)(2,1)S(1)} %pad_maximum_fusion.x_first.refs_0_), channel_id=1, source_target_pairs={{0,8},{1,17},{2,10},{3,19},{4,12},{5,21},{6,14},{7,23},{8,0},{9,25... | collective-permute-start | bytes 3342344 | tf_op jit(solution)/shard_map/ppermute | solution.py:495
  20.4 13.3 %collective-permute-start.7 = (bf16[128,2048]{1,0:T(8,128)(2,1)S(1)}, bf16[128,2048]{1,0:T(8,128)(2,1)}, u32[]{:S(2)}, u32[]{:S(2)}) collective-permute-start(bf16[128,2048]{1,0:T(8,128)(2,1)S(1)} %pad_maximum_fusion.2), channel_id=1, source_target_pairs={{0,2},{1,3},{2,0},{3,1},{4,6},{5,7},{6,4},{7,5},{8,10},{9,11},{10,... | collective-permute-start | bytes 1572872 | tf_op jit(solution)/shard_map/ppermute | solution.py:495
  21.1 19.5 %collective-permute-start = (bf16[1,352,2048]{2,1,0:T(8,128)(2,1)}, bf16[1,352,2048]{2,1,0:T(8,128)(2,1)}, u32[]{:S(2)}, u32[]{:S(2)}) collective-permute-start(bf16[1,352,2048]{2,1,0:T(8,128)(2,1)} %gate.5), channel_id=1, source_target_pairs={{0,1},{1,0},{2,3},{3,2},{4,5},{5,4},{6,7},{7,6},{8,9},{9,8},{10,11... | collective-permute-start | bytes 4325384 | tf_op jit(solution)/shard_map/ppermute | solution.py:495
  21.2 19.5 %collective-permute-start.1 = (bf16[1,352,2048]{2,1,0:T(8,128)(2,1)}, bf16[1,352,2048]{2,1,0:T(8,128)(2,1)}, u32[]{:S(2)}, u32[]{:S(2)}) collective-permute-start(bf16[1,352,2048]{2,1,0:T(8,128)(2,1)} %up.5), channel_id=1, source_target_pairs={{0,1},{1,0},{2,3},{3,2},{4,5},{5,4},{6,7},{7,6},{8,9},{9,8},{10,11... | collective-permute-start | bytes 4325384 | tf_op jit(solution)/shard_map/ppermute | solution.py:495
  33.6 7.0 %collective-permute-start.2 = (bf16[1,352,2048]{2,1,0:T(8,128)(2,1)}, bf16[1,352,2048]{2,1,0:T(8,128)(2,1)}, u32[]{:S(2)}, u32[]{:S(2)}) collective-permute-start(bf16[1,352,2048]{2,1,0:T(8,128)(2,1)} %down.5), channel_id=1, source_target_pairs={{0,1},{1,0},{2,3},{3,2},{4,5},{5,4},{6,7},{7,6},{8,9},{9,8},{10,11... | collective-permute-start | bytes 4325384 | tf_op jit(solution)/shard_map/ppermute | solution.py:495
  34.8 27.8 %copy-start.7 = (bf16[256,2048]{1,0:T(8,128)(2,1)}, bf16[256,2048]{1,0:T(8,128)(2,1)S(1)}, u32[]{:S(2)}) copy-start(bf16[256,2048]{1,0:T(8,128)(2,1)S(1)} %pad_maximum_fusion.1.cot_first.refs_4_) | copy-start | bytes 3145732
  36.6 25.9 %collective-permute-start.8 = (bf16[256,2048]{1,0:T(8,128)(2,1)S(1)}, bf16[256,2048]{1,0:T(8,128)(2,1)}, u32[]{:S(2)}, u32[]{:S(2)}) collective-permute-start(bf16[256,2048]{1,0:T(8,128)(2,1)S(1)} %pad_maximum_fusion.1.cot_first.refs_4_), channel_id=1, source_target_pairs={{0,8},{1,17},{2,10},{3,19},{4,12},{5,21},{6,14},{7,23},{8,0},{9,25... | collective-permute-start | bytes 3145736 | tf_op jit(solution)/shard_map/ppermute | solution.py:495
  37.3 25.1 %collective-permute-start.5 = (bf16[272,2048]{1,0:T(8,128)(2,1)}, bf16[272,2048]{1,0:T(8,128)(2,1)}, u32[]{:S(2)}, u32[]{:S(2)}) collective-permute-start(bf16[272,2048]{1,0:T(8,128)(2,1)} %collective-permute-done.3.x_second.refs_1_), channel_id=1, source_target_pairs={{0,16},{1,9},{2,18},{3,11},{4,20},{5,13},{6,22},{7,15},{8,24},{9,1... | collective-permute-start | bytes 3342344 | tf_op jit(solution)/shard_map/ppermute | solution.py:495
  62.5 26.1 %collective-permute-start.9 = (bf16[256,2048]{1,0:T(8,128)(2,1)S(1)}, bf16[256,2048]{1,0:T(8,128)(2,1)}, u32[]{:S(2)}, u32[]{:S(2)}) collective-permute-start(bf16[256,2048]{1,0:T(8,128)(2,1)S(1)} %pad_maximum_fusion.1.cot_first.refs_4_), channel_id=1, source_target_pairs={{0,16},{1,9},{2,18},{3,11},{4,20},{5,13},{6,22},{7,15},{8,24},{9,1... | collective-permute-start | bytes 3145736 | tf_op jit(solution)/shard_map/ppermute | solution.py:495
  64.3 24.4 %collective-permute-start.10 = (bf16[256,2048]{1,0:T(8,128)(2,1)}, bf16[256,2048]{1,0:T(8,128)(2,1)}, u32[]{:S(2)}, u32[]{:S(2)}) collective-permute-start(bf16[256,2048]{1,0:T(8,128)(2,1)} %collective-permute-done.8.cot_second.refs_5_), channel_id=1, source_target_pairs={{0,16},{1,9},{2,18},{3,11},{4,20},{5,13},{6,22},{7,15},{8,24},{9,1... | collective-permute-start | bytes 3145736 | tf_op jit(solution)/shard_map/ppermute | solution.py:495
  88.7 26.2 %collective-permute-start.11 = (bf16[512,2048]{1,0:T(8,128)(2,1)}, bf16[512,2048]{1,0:T(8,128)(2,1)S(1)}, u32[]{:S(2)}, u32[]{:S(2)}) collective-permute-start(bf16[512,2048]{1,0:T(8,128)(2,1)} %get-tuple-element.61), channel_id=1, source_target_pairs={{0,16},{1,9},{2,18},{3,11},{4,20},{5,13},{6,22},{7,15},{8,24},{9,1... | collective-permute-start | bytes 6291464 | tf_op jit(solution)/shard_map/ppermute | solution.py:495
  90.4 24.5 %copy-start.4 = (bf16[512,2048]{1,0:T(8,128)(2,1)S(1)}, bf16[512,2048]{1,0:T(8,128)(2,1)}, u32[]{:S(2)}) copy-start(bf16[512,2048]{1,0:T(8,128)(2,1)} %get-tuple-element.49) | copy-start | bytes 6291460
  105.4 43.2 %collective-permute-start.14 = (bf16[512,2048]{1,0:T(8,128)(2,1)}, bf16[512,2048]{1,0:T(8,128)(2,1)S(1)}, u32[]{:S(2)}, u32[]{:S(2)}) collective-permute-start(bf16[512,2048]{1,0:T(8,128)(2,1)} %get-tuple-element.65), channel_id=1, source_target_pairs={{0,16},{1,9},{2,18},{3,11},{4,20},{5,13},{6,22},{7,15},{8,24},{9,1... | collective-permute-start | bytes 6291464 | tf_op jit(solution)/shard_map/ppermute | solution.py:495
  114.9 12.2 %copy-start.5 = (bf16[512,2048]{1,0:T(8,128)(2,1)}, bf16[512,2048]{1,0:T(8,128)(2,1)S(1)}, u32[]{:S(2)}) copy-start(bf16[512,2048]{1,0:T(8,128)(2,1)S(1)} %collective-permute-done.11) | copy-start | bytes 6291460
  115.3 11.9 %copy-start.9 = (f32[512,1]{1,0:T(8,128)S(1)}, f32[512,1]{1,0:T(8,128)}, u32[]{:S(2)}) copy-start(f32[512,1]{1,0:T(8,128)} %get-tuple-element.87) | copy-start | bytes 6148
  115.3 26.3 %collective-permute-start.12 = (bf16[256,2048]{1,0:T(8,128)(2,1)S(1)}, bf16[256,2048]{1,0:T(8,128)(2,1)}, u32[]{:S(2)}, u32[]{:S(2)}) collective-permute-start(bf16[256,2048]{1,0:T(8,128)(2,1)S(1)} %add_convert_fusion.1), channel_id=1, source_target_pairs={{0,8},{1,17},{2,10},{3,19},{4,12},{5,21},{6,14},{7,23},{8,0},{9,25... | collective-permute-start | bytes 3145736 | tf_op jit(solution)/shard_map/ppermute | solution.py:495
  127.2 47.5 %collective-permute-start.16 = (bf16[3,352,2048]{2,1,0:T(8,128)(2,1)}, bf16[3,352,2048]{2,1,0:T(8,128)(2,1)}, u32[]{:S(2)}, u32[]{:S(2)}) collective-permute-start(bf16[3,352,2048]{2,1,0:T(8,128)(2,1)} %other_grads.1), channel_id=1, source_target_pairs={{0,1},{1,0},{2,3},{3,2},{4,5},{5,4},{6,7},{7,6},{8,9},{9,8},{10,11... | collective-permute-start | bytes 12976136 | tf_op jit(solution)/shard_map/ppermute | solution.py:495
  128.6 3.7 %collective-permute-start.21 = (f32[4,2,64]{2,0,1:T(4,128)S(1)}, f32[4,2,64]{2,0,1:T(4,128)S(1)}, u32[]{:S(2)}, u32[]{:S(2)}) collective-permute-start(f32[4,2,64]{2,0,1:T(4,128)S(1)} %copy.62), channel_id=1, source_target_pairs={{0,2},{1,3},{2,0},{3,1},{4,6},{5,7},{6,4},{7,5},{8,10},{9,11},{10,... | collective-permute-start | bytes 6152 | tf_op jit(solution)/shard_map/ppermute | solution.py:495
  130.3 18.3 %copy-start.3 = (bf16[512,2048]{1,0:T(8,128)(2,1)S(1)}, bf16[512,2048]{1,0:T(8,128)(2,1)}, u32[]{:S(2)}) copy-start(bf16[512,2048]{1,0:T(8,128)(2,1)} %get-tuple-element.67) | copy-start | bytes 6291460
  148.6 19.8 %copy-start.2 = (bf16[512,2048]{1,0:T(8,128)(2,1)}, bf16[512,2048]{1,0:T(8,128)(2,1)S(1)}, u32[]{:S(2)}) copy-start(bf16[512,2048]{1,0:T(8,128)(2,1)S(1)} %collective-permute-done.14) | copy-start | bytes 6291460
  149.0 17.8 %collective-permute-start.17 = (bf16[256,2048]{1,0:T(8,128)(2,1)S(1)}, bf16[256,2048]{1,0:T(8,128)(2,1)S(1)}, u32[]{:S(2)}, u32[]{:S(2)}) collective-permute-start(bf16[256,2048]{1,0:T(8,128)(2,1)S(1)} %add_convert_fusion), channel_id=1, source_target_pairs={{0,8},{1,17},{2,10},{3,19},{4,12},{5,21},{6,14},{7,23},{8,0},{9,25... | collective-permute-start | bytes 3145736 | tf_op jit(solution)/shard_map/ppermute | solution.py:495
  150.0 5.1 %collective-permute-start.22 = (f32[4,64]{1,0:T(4,128)S(1)}, f32[4,64]{1,0:T(4,128)S(1)}, u32[]{:S(2)}, u32[]{:S(2)}) collective-permute-start(f32[4,64]{1,0:T(4,128)S(1)} %bitcast.58), channel_id=1, source_target_pairs={{0,4},{1,5},{2,6},{3,7},{4,0},{5,1},{6,2},{7,3},{8,12},{9,13},{10,... | collective-permute-start | bytes 3080 | tf_op jit(solution)/shard_map/ppermute | solution.py:495
  153.4 11.9 %collective-permute-start.13 = (bf16[2,64,2048]{2,1,0:T(8,128)(2,1)S(1)}, bf16[2,64,2048]{2,1,0:T(8,128)(2,1)S(1)}, u32[]{:S(2)}, u32[]{:S(2)}) collective-permute-start(bf16[2,64,2048]{2,1,0:T(8,128)(2,1)S(1)} %bitcast.45), channel_id=1, source_target_pairs={{0,2},{1,3},{2,0},{3,1},{4,6},{5,7},{6,4},{7,5},{8,10},{9,11},{10,... | collective-permute-start | bytes 1572872 | tf_op jit(solution)/shard_map/ppermute | solution.py:495
  155.1 11.7 %collective-permute-start.23 = (f32[2,2,64]{2,0,1:T(2,128)S(1)}, f32[2,2,64]{2,0,1:T(2,128)S(1)}, u32[]{:S(2)}, u32[]{:S(2)}) collective-permute-start(f32[2,2,64]{2,0,1:T(2,128)S(1)} %fusion.10), channel_id=1, source_target_pairs={{0,16},{1,9},{2,18},{3,11},{4,20},{5,13},{6,22},{7,15},{8,24},{9,1... | collective-permute-start | bytes 3080 | tf_op jit(solution)/shard_map/ppermute | solution.py:495
  166.5 24.5 %collective-permute-start.15 = (bf16[64,2048]{1,0:T(8,128)(2,1)S(1)}, bf16[64,2048]{1,0:T(8,128)(2,1)S(1)}, u32[]{:S(2)}, u32[]{:S(2)}) collective-permute-start(bf16[64,2048]{1,0:T(8,128)(2,1)S(1)} %fusion), channel_id=1, source_target_pairs={{0,4},{1,5},{2,6},{3,7},{4,0},{5,1},{6,2},{7,3},{8,12},{9,13},{10,... | collective-permute-start | bytes 786440 | tf_op jit(solution)/shard_map/ppermute | solution.py:495
  166.9 6.1 %collective-permute-start.24 = (f32[2,2,64]{2,0,1:T(2,128)S(1)}, f32[2,2,64]{2,0,1:T(2,128)S(1)}, u32[]{:S(2)}, u32[]{:S(2)}) collective-permute-start(f32[2,2,64]{2,0,1:T(2,128)S(1)} %fusion.11), channel_id=1, source_target_pairs={{0,8},{1,17},{2,10},{3,19},{4,12},{5,21},{6,14},{7,23},{8,0},{9,25... | collective-permute-start | bytes 3080 | tf_op jit(solution)/shard_map/ppermute | solution.py:495
  168.8 27.7 %collective-permute-start.18 = (bf16[64,2048]{1,0:T(8,128)(2,1)S(1)}, bf16[64,2048]{1,0:T(8,128)(2,1)S(1)}, u32[]{:S(2)}, u32[]{:S(2)}) collective-permute-start(bf16[64,2048]{1,0:T(8,128)(2,1)S(1)} %get-tuple-element.96), channel_id=1, source_target_pairs={{0,4},{1,5},{2,6},{3,7},{4,0},{5,1},{6,2},{7,3},{8,12},{9,13},{10,... | collective-permute-start | bytes 786440 | tf_op jit(solution)/shard_map/ppermute | solution.py:495
  171.5 25.0 %collective-permute-start.20 = (bf16[64,2048]{1,0:T(8,128)(2,1)S(1)}, bf16[64,2048]{1,0:T(8,128)(2,1)S(1)}, u32[]{:S(2)}, u32[]{:S(2)}) collective-permute-start(bf16[64,2048]{1,0:T(8,128)(2,1)S(1)} %get-tuple-element.97), channel_id=1, source_target_pairs={{0,6},{1,7},{2,4},{3,5},{4,2},{5,3},{6,0},{7,1},{8,14},{9,15},{10,... | collective-permute-start | bytes 786440 | tf_op jit(solution)/shard_map/ppermute | solution.py:495
  173.0 23.6 %collective-permute-start.19 = (bf16[64,2048]{1,0:T(8,128)(2,1)S(1)}, bf16[64,2048]{1,0:T(8,128)(2,1)S(1)}, u32[]{:S(2)}, u32[]{:S(2)}) collective-permute-start(bf16[64,2048]{1,0:T(8,128)(2,1)S(1)} %get-tuple-element.98), channel_id=1, source_target_pairs={{0,2},{1,3},{2,0},{3,1},{4,6},{5,7},{6,4},{7,5},{8,10},{9,11},{10,... | collective-permute-start | bytes 786440 | tf_op jit(solution)/shard_map/ppermute | solution.py:495
  174.6 23.8 %copy-start.1 = (bf16[512,2048]{1,0:T(8,128)(2,1)S(1)}, bf16[512,2048]{1,0:T(8,128)(2,1)}, u32[]{:S(2)}) copy-start(bf16[512,2048]{1,0:T(8,128)(2,1)} %param.8) | copy-start | bytes 6291460

commit v4 on v3

--- a/solution.py
+++ b/solution.py
@@ -214,12 +214,14 @@
         to_up[:, there] = silu_value
 
 
-def backward_units(rows, weight, down, hidden, to_gate, to_up, d_pre, route_out):
+def backward_units(rows, weight, down, parts, hidden, to_gate, to_up, d_pre, route_out):
     both = hidden.shape[1]
     route = None
     for first in range(0, both, UNIT_TILE):
         there = pl.ds(first, UNIT_TILE)
         plain = dot_rows(rows[...], down[there])
+        if first == 0:
+            wait(parts)
         term = jnp.sum(plain * hidden[:, there].astype(jnp.float32), axis=1, keepdims=True)
         route = term if route is None else route + term
         d_hidden = plain * weight[...]
@@ -272,8 +274,8 @@
     d_gate, d_up = both_halves(d_pre)
     stores = copies_between(((dx, dx_out), (d_gate, d_gate_out), (d_up, d_up_out)), out_sems)
     start(rows + loads[4:] + parts + loads[:4])
-    wait(rows + loads[4:] + parts)
-    backward_units(row_buf, weight, down_buf, *kept, d_pre, route_out)
+    wait(rows + loads[4:])
+    backward_units(row_buf, weight, down_buf, parts, *kept, d_pre, route_out)
     start(stores[1:])
     wait(loads[:4])
     dot_columns(dx, d_pre, pre_buf)
@@ -310,8 +312,8 @@
     wait(loads[4:])
     dot_columns(mixed, weighted34, down_buf)
     start(stores[:1])
-    wait(cots + parts)
-    backward_units(cot_buf, weight12, down_buf, *kept12, d_pre, route_out)
+    wait(cots)
+    backward_units(cot_buf, weight12, down_buf, parts, *kept12, d_pre, route_out)
     start(back[1:])
     dot_columns(dx, d_pre, pre_buf)
     start(back[:1])
@@ -577,23 +579,26 @@
     mixed_part = add(mixed12[half:], after(mixed_far, dx34)[half:])
     mixed_near = to_near(mixed_part)
 
-    mixed_terms = in_blocks((mixed12[:half], mixed_far[:half], mixed_near))
-    mixed_pair = add(*[term[2:] for term in mixed_terms])
-    dx_far = to_far(dx34)
-    dx_part = add(dx12[half:], after(dx_far, mixed_pair)[half:])
-    dx_near = to_near(dx_part)
-    mixed_pair = after(to_level(mixed_pair, 1), dx_part)
-    mixed_last = to_level(add(*[term[1] for term in mixed_terms], mixed_pair[1]), 2)
-
     h = w_gate.shape[1]
     wide = (x_own, x_near, x_far, x_last, g_own, g_near, g_far, g_last)
     narrow = after((gate12, gate34, up12, up34, weighted12, weighted34), mixed_far)
-    received = to_core(weight_grads(wide, narrow, h))
-    grads = weight_grads(wide, narrow, h, received)
+    for_other = weight_grads(wide, narrow, h)
+    grads = weight_grads(wide, narrow, h, to_core(for_other))
+    mixed_near = after(mixed_near, for_other)
+
+
+    mixed_terms = in_blocks((mixed12[:half], mixed_far[:half], mixed_near))
+    mixed_pair = add(*[term[2:] for term in mixed_terms])
+    mixed_pair = to_level(mixed_pair, 1)
+    mixed_last = to_level(add(*[term[1] for term in mixed_terms], mixed_pair[1]), 2)
+    dx_far = after(to_far(after(dx34, mixed_near)), mixed_pair)
+    dx_part = add(dx12[half:], dx_far[half:])
+    dx_near = to_near(dx_part)
+    dx_near = after(dx_near, mixed_last)
 
     route = jnp.concatenate([route12, route34]).reshape(dp_count, levels, block)
     pair = after(to_level(route[:, 2:], 1), mixed_part)
-    other_group = after(to_level(route[:, 1] + pair[:, 1], 2), mixed_near)
+    other_group = after(to_level(route[:, 1] + pair[:, 1], 2), dx_near)
     route = jnp.stack([route[:, 0] + pair[:, 0], other_group], axis=1)
     route_far = after(to_far(route[2:]), dx_near)
     route_near = to_near(jnp.stack([route[1], route_far[1]]))

time: 202 us -> 202 us (level); the launches traced: 198 us -> 201 us
  other arithmetic: 12.2 us -> 14.7 us
    convert_element_type x7, other arithmetic: 7.85 us -> 10.4 us  [add(): return total.astype(terms[0].dtype)]
  transfers between devices with their start and end apart: 25 -> 25, of which waited for: 13 -> 13; matrix products, arithmetic and copies ran while one was open for 8% -> 9% of each run, Pallas kernels for 34% -> 34%
where the time goes in v4:
time: 202 us; the launch traced here: 201 us
  waiting for transfers between devices  77.3 us (38%)
  Pallas kernels  68.3 us (34%)
  starting transfers between devices  31.4 us (16%)
  other arithmetic  14.7 us (7%)
  local copies, waits for them, and re-layouts  8.55 us (4%)
    ppermute x25, waiting for transfers between devices, exchange(): return lax.ppermute(value, ('dp', 'expert'), pairs)  77.3 us
    pallas_call x3, Pallas kernels, row_kernel(): pl.pallas_call(kernel, out_shape=outs, in_specs=specs(pl.ANY, len(matrice...  46.5 us
    ppermute x25, starting transfers between devices, exchange(): return lax.ppermute(value, ('dp', 'expert'), pairs)  31.4 us
    pallas_call x2, Pallas kernels, weight_grads(): pl.pallas_call(kernel, out_shape=outs, grid=(width // tile,), in_specs=in...  21.8 us
    convert_element_type x7, other arithmetic, add(): return total.astype(terms[0].dtype)  10.4 us
  transfers between devices with their start and end apart: 25, of which 13 were waited for; matrix products, arithmetic and copies ran while one was open for 9% of the time, Pallas kernels for 34%

profile of v4, /device:TPU:0, one launch (start us, length us, event | category | flops | bytes accessed | tf_op | source)
XLA Modules:
  0.0 201.3 jit_solution(3057911329635894267)
XLA Ops:
  0.7 0.8 compare_select_fusion
  1.5 0.8 select_reduce_fusion
  2.4 0.1 reshape.153
  2.4 0.6 gather_fusion.1
  3.1 0.1 stack_reshape.11
  3.1 0.1 stack_reshape.10
  3.4 0.6 gather_fusion
  4.1 0.2 copy-done.7
  4.4 4.0 %collective-permute-start.6 = (bf16[64,2048]{1,0:T(8,128)(2,1)S(1)}, bf16[64,2048]{1,0:T(8,128)(2,1)S(1)}, u32[]{:S(2)}, u32[]{:S(2)}) collective-permute-start(bf16[64,2048]{1,0:T(8,128)(2,1)S(1)} %copy-done.7), channel_id=1, source_target_pairs={{0,4},{1,5},{2,6},{3,7},{4,0},{5,1},{6,2},{7,3},{8,12},{9,13},{10,... | collective-permute-start | bytes 786440 | tf_op jit(solution)/shard_map/ppermute | solution.py:497
  8.4 1.5 collective-permute-start.4
  9.9 1.5 collective-permute-start.3
  11.4 8.9 %collective-permute-done.6 = bf16[64,2048]{1,0:T(8,128)(2,1)S(1)} collective-permute-done((bf16[64,2048]{1,0:T(8,128)(2,1)S(1)}, bf16[64,2048]{1,0:T(8,128)(2,1)S(1)}, u32[]{:S(2)}, u32[]{:S(2)}) %collective-permute-start.6) | collective-permute-done | bytes 262176 | tf_op jit(solution)/shard_map/ppermute | solution.py:497
  20.4 0.8 collective-permute-start.7
  21.2 0.5 collective-permute-start.1
  21.7 11.9 %collective-permute-done.7 = bf16[128,2048]{1,0:T(8,128)(2,1)} collective-permute-done((bf16[128,2048]{1,0:T(8,128)(2,1)S(1)}, bf16[128,2048]{1,0:T(8,128)(2,1)}, u32[]{:S(2)}, u32[]{:S(2)}) %collective-permute-start.7) | collective-permute-done | bytes 524320 | tf_op jit(solution)/shard_map/ppermute | solution.py:497
  33.6 1.1 pad_maximum_fusion.1.cot_first.refs_4_
  34.8 1.0 collective-permute-done.4.x_first.refs_2_
  35.7 0.8 slice_bitcast_fusion.4
  36.6 0.7 collective-permute-start.8
  37.3 1.5 collective-permute-start.5
  38.8 0.8 slice_bitcast_fusion.3
  39.8 0.9 copy.52.weight.weight12
  40.7 11.2 %forward.1 = (bf16[512,2048]{1,0:T(8,128)(2,1)}, bf16[512,768]{1,0:T(8,128)(2,1)}, bf16[512,768]{1,0:T(8,128)(2,1)}, f32[512,768]{1,0:T(8,128)}, f32[512,768]{1,0:T(8,128)}) custom-call(bf16[1,352,2048]{2,1,0:T(8,128)(2,1)} %gate.5, bf16[1,352,2048]{2,1,0:T(8,128)(2,1)} %collective-permute-done.gate_other, bf16[1,352,2048]{2,1,0:T(8,128)(2,1)} %up.5, ...), custom_call_target="tpu_custom_call" | custom-call | flops 5000000000 | bytes 20000000 | tf_op jit(solution)/shard_map/forward/pallas_call | solution.py:378
  51.9 10.6 %collective-permute-done.5.x_second.refs_3_ = bf16[272,2048]{1,0:T(8,128)(2,1)} collective-permute-done((bf16[272,2048]{1,0:T(8,128)(2,1)}, bf16[272,2048]{1,0:T(8,128)(2,1)}, u32[]{:S(2)}, u32[]{:S(2)}) %collective-permute-start.5) | collective-permute-done | bytes 1114144 | tf_op jit(solution)/shard_map/ppermute | solution.py:497
  62.5 1.8 collective-permute-start.9
  64.3 0.3 collective-permute-start.10
  64.6 0.8 slice_bitcast_fusion.2
  65.5 0.9 copy.53.weight34.weight
  66.4 20.6 %middle.1 = (bf16[512,2048]{1,0:T(8,128)(2,1)}, bf16[512,768]{1,0:T(8,128)(2,1)}, bf16[512,768]{1,0:T(8,128)(2,1)}, f32[512,768]{1,0:T(8,128)}, f32[512,768]{1,0...) custom-call(bf16[1,352,2048]{2,1,0:T(8,128)(2,1)} %gate.5, ...), custom_call_target="tpu_custom_call" | custom-call | flops 5000000000 | bytes 20000000 | tf_op jit(solution)/shard_map/middle/pallas_call | solution.py:378
  86.9 1.7 collective-permute-done.10.cot_second.refs_7_
  88.7 1.8 collective-permute-start.11
  90.4 14.7 %backward.1 = (bf16[512,2048]{1,0:T(8,128)(2,1)}, f32[512,1]{1,0:T(8,128)}, bf16[512,768]{1,0:T(8,128)(2,1)}, bf16[512,768]{1,0:T(8,128)(2,1)}) custom-call(bf16[1,352,2048]{2,1,0:T(8,128)(2,1)} %gate.5, bf16[1,352,2048]{2,1,0:T(8,128)(2,1)} %collective-permute-done.gate_other, bf16[1,352,2048]{2,1,0:T(8,128)(2,1)} %up.5, ...), custom_call_target="tpu_custom_call" | custom-call | flops 5000000000 | bytes 20000000 | tf_op jit(solution)/shard_map/backward/pallas_call | solution.py:378
  105.2 9.7 %collective-permute-done.11 = bf16[512,2048]{1,0:T(8,128)(2,1)S(1)} collective-permute-done((bf16[512,2048]{1,0:T(8,128)(2,1)}, bf16[512,2048]{1,0:T(8,128)(2,1)S(1)}, u32[]{:S(2)}, u32[]{:S(2)}) %collective-permute-start.11) | collective-permute-done | bytes 2097184 | tf_op jit(solution)/shard_map/ppermute | solution.py:497
  114.9 0.4 add_convert_fusion.1
  115.3 1.0 collective-permute-start.12
  116.3 10.8 %other_grads.1 = bf16[3,352,2048]{2,1,0:T(8,128)(2,1)} custom-call(bf16[272,2048]{1,0:T(8,128)(2,1)} %copy-done.5, bf16[272,2048]{1,0:T(8,128)(2,1)} %collective-permute-done.3.x_second.refs_1_, bf16[272,2048]{1,0:T(8,128)(2,1)} %collective-permute-done.4.x_first.refs_2_, bf16[272,2048]{1,0:T(8,128)(2,1)} %collective-permute-done.5.x_second.refs_3_, ...), custom_call_target="tpu_custom_call" | custom-call | flops 5000000000 | bytes 20000000 | tf_op jit(solution)/shard_map/other_grads/pallas_call | solution.py:451
  127.2 3.0 %collective-permute-done.12 = bf16[256,2048]{1,0:T(8,128)(2,1)S(1)} collective-permute-done((bf16[256,2048]{1,0:T(8,128)(2,1)S(1)}, bf16[256,2048]{1,0:T(8,128)(2,1)S(1)}, u32[]{:S(2)}, u32[]{:S(2)}) %collective-permute-start.12) | collective-permute-done | bytes 1048608 | tf_op jit(solution)/shard_map/ppermute | solution.py:497
  130.2 1.8 collective-permute-start.16
  131.9 1.0 add_convert_fusion.2
  133.0 1.6 collective-permute-start.13
  134.6 0.1 copy.56
  134.7 1.1 copy.57
  135.9 0.5 collective-permute-start.21
  136.4 1.0 slice.277
  137.3 10.3 %collective-permute-done.21 = f32[4,2,64]{2,0,1:T(4,128)S(1)} collective-permute-done((f32[4,2,64]{2,0,1:T(4,128)S(1)}, f32[4,2,64]{2,0,1:T(4,128)S(1)}, u32[]{:S(2)}, u32[]{:S(2)}) %collective-permute-start.21) | collective-permute-done | bytes 2080 | tf_op jit(solution)/shard_map/ppermute | solution.py:497
  147.7 8.8 %collective-permute-done.16 = bf16[512,2048]{1,0:T(8,128)(2,1)S(1)} collective-permute-done((bf16[512,2048]{1,0:T(8,128)(2,1)}, bf16[512,2048]{1,0:T(8,128)(2,1)S(1)}, u32[]{:S(2)}, u32[]{:S(2)}) %collective-permute-start.16) | collective-permute-done | bytes 2097184 | tf_op jit(solution)/shard_map/ppermute | solution.py:497
  156.4 2.4 %add_convert_fusion = bf16[256,2048]{1,0:T(8,128)(2,1)S(1)} fusion(bf16[512,2048]{1,0:T(8,128)(2,1)S(1)} %collective-permute-done.16, bf16[512,2048]{1,0:T(8,128)(2,1)} %get-tuple-element.86), kind=kLoop, calls=%fused_computation.2 | loop fusion | flops 2097152 | bytes 3145728 | tf_op jit(solution)/shard_map/convert_element_type | solution.py:515
  158.8 1.0 collective-permute-start.17
  159.8 1.2 fusion
  161.1 3.4 %collective-permute-start.14 = (bf16[64,2048]{1,0:T(8,128)(2,1)S(1)}, bf16[64,2048]{1,0:T(8,128)(2,1)S(1)}, u32[]{:S(2)}, u32[]{:S(2)}) collective-permute-start(bf16[64,2048]{1,0:T(8,128)(2,1)S(1)} %fusion), channel_id=1, source_target_pairs={{0,4},{1,5},{2,6},{3,7},{4,0},{5,1},{6,2},{7,3},{8,12},{9,13},{10,... | collective-permute-start | bytes 786440 | tf_op jit(solution)/shard_map/ppermute | solution.py:497
  164.5 0.1 collective-permute-start.22
  164.6 8.6 %collective-permute-done.14 = bf16[64,2048]{1,0:T(8,128)(2,1)S(1)} collective-permute-done((bf16[64,2048]{1,0:T(8,128)(2,1)S(1)}, bf16[64,2048]{1,0:T(8,128)(2,1)S(1)}, u32[]{:S(2)}, u32[]{:S(2)}) %collective-permute-start.14) | collective-permute-done | bytes 262176 | tf_op jit(solution)/shard_map/ppermute | solution.py:497
  173.2 0.5 collective-permute-done.17
  173.7 1.8 collective-permute-start.23
  175.5 1.5 add_convert_fusion.6
  177.1 2.6 %collective-permute-start.18 = (bf16[64,2048]{1,0:T(8,128)(2,1)S(1)}, bf16[64,2048]{1,0:T(8,128)(2,1)S(1)}, u32[]{:S(2)}, u32[]{:S(2)}) collective-permute-start(bf16[64,2048]{1,0:T(8,128)(2,1)S(1)} %get-tuple-element.100), channel_id=1, source_target_pairs={{0,4},{1,5},{2,6},{3,7},{4,0},{5,1},{6,2},{7,3},{8,12},{9,13},{10,... | collective-permute-start | bytes 786440 | tf_op jit(solution)/shard_map/ppermute | solution.py:497
  179.7 1.4 collective-permute-start.20
  181.1 0.3 collective-permute-start.19
  181.4 1.6 collective-permute-start.24
  183.0 2.1 %collective-permute-done.24 = f32[2,2,64]{2,0,1:T(2,128)S(1)} collective-permute-done((f32[2,2,64]{2,0,1:T(2,128)S(1)}, f32[2,2,64]{2,0,1:T(2,128)S(1)}, u32[]{:S(2)}, u32[]{:S(2)}) %collective-permute-start.24) | collective-permute-done | bytes 1056 | tf_op jit(solution)/shard_map/ppermute | solution.py:497
  185.1 1.4 select_add_fusion
  186.4 10.9 %own_grads.1 = (bf16[1,352,2048]{2,1,0:T(8,128)(2,1)}, bf16[1,352,2048]{2,1,0:T(8,128)(2,1)}, bf16[1,352,2048]{2,1,0:T(8,128)(2,1)}) custom-call(bf16[272,2048]{1,0:T(8,128)(2,1)} %copy-done.5, bf16[272,2048]{1,0:T(8,128)(2,1)} %collective-permute-done.3.x_second.refs_1_, bf16[272,2048]{1,0:T(8,128)(2,1)} %collective-permute-done.4.x_first.refs_2_, ...), custom_call_target="tpu_custom_call" | custom-call | flops 5000000000 | bytes 20000000 | tf_op jit(solution)/shard_map/own_grads/pallas_call | solution.py:451
  197.4 2.0 fusion.2
  199.4 1.9 add_convert_fusion.3
  (77 shorter events, 0.9 us)
Async XLA Ops:
  0.6 2.8 %copy-start = (bf16[512,2048]{1,0:T(8,128)(2,1)S(1)}, bf16[512,2048]{1,0:T(8,128)(2,1)}, u32[]{:S(2)}) copy-start(bf16[512,2048]{1,0:T(8,128)(2,1)} %param.8) | copy-start | bytes 6291460
  3.4 1.0 copy-start.7
  4.4 36.3 %copy-start.5 = (bf16[272,2048]{1,0:T(8,128)(2,1)}, bf16[272,2048]{1,0:T(8,128)(2,1)S(1)}, u32[]{:S(2)}) copy-start(bf16[272,2048]{1,0:T(8,128)(2,1)S(1)} %pad_maximum_fusion.x_first.refs_0_) | copy-start | bytes 3342340
  4.4 16.0 %collective-permute-start.6 = (bf16[64,2048]{1,0:T(8,128)(2,1)S(1)}, bf16[64,2048]{1,0:T(8,128)(2,1)S(1)}, u32[]{:S(2)}, u32[]{:S(2)}) collective-permute-start(bf16[64,2048]{1,0:T(8,128)(2,1)S(1)} %copy-done.7), channel_id=1, source_target_pairs={{0,4},{1,5},{2,6},{3,7},{4,0},{5,1},{6,2},{7,3},{8,12},{9,13},{10,... | collective-permute-start | bytes 786440 | tf_op jit(solution)/shard_map/ppermute | solution.py:497
  8.4 27.3 %collective-permute-start.4 = (bf16[272,2048]{1,0:T(8,128)(2,1)S(1)}, bf16[272,2048]{1,0:T(8,128)(2,1)}, u32[]{:S(2)}, u32[]{:S(2)}) collective-permute-start(bf16[272,2048]{1,0:T(8,128)(2,1)S(1)} %pad_maximum_fusion.x_first.refs_0_), channel_id=1, source_target_pairs={{0,16},{1,9},{2,18},{3,11},{4,20},{5,13},{6,22},{7,15},{8,24},{9,1... | collective-permute-start | bytes 3342344 | tf_op jit(solution)/shard_map/ppermute | solution.py:497
  9.9 25.8 %collective-permute-start.3 = (bf16[272,2048]{1,0:T(8,128)(2,1)S(1)}, bf16[272,2048]{1,0:T(8,128)(2,1)}, u32[]{:S(2)}, u32[]{:S(2)}) collective-permute-start(bf16[272,2048]{1,0:T(8,128)(2,1)S(1)} %pad_maximum_fusion.x_first.refs_0_), channel_id=1, source_target_pairs={{0,8},{1,17},{2,10},{3,19},{4,12},{5,21},{6,14},{7,23},{8,0},{9,25... | collective-permute-start | bytes 3342344 | tf_op jit(solution)/shard_map/ppermute | solution.py:497
  20.4 13.3 %collective-permute-start.7 = (bf16[128,2048]{1,0:T(8,128)(2,1)S(1)}, bf16[128,2048]{1,0:T(8,128)(2,1)}, u32[]{:S(2)}, u32[]{:S(2)}) collective-permute-start(bf16[128,2048]{1,0:T(8,128)(2,1)S(1)} %pad_maximum_fusion.2), channel_id=1, source_target_pairs={{0,2},{1,3},{2,0},{3,1},{4,6},{5,7},{6,4},{7,5},{8,10},{9,11},{10,... | collective-permute-start | bytes 1572872 | tf_op jit(solution)/shard_map/ppermute | solution.py:497
  21.1 19.5 %collective-permute-start = (bf16[1,352,2048]{2,1,0:T(8,128)(2,1)}, bf16[1,352,2048]{2,1,0:T(8,128)(2,1)}, u32[]{:S(2)}, u32[]{:S(2)}) collective-permute-start(bf16[1,352,2048]{2,1,0:T(8,128)(2,1)} %gate.5), channel_id=1, source_target_pairs={{0,1},{1,0},{2,3},{3,2},{4,5},{5,4},{6,7},{7,6},{8,9},{9,8},{10,11... | collective-permute-start | bytes 4325384 | tf_op jit(solution)/shard_map/ppermute | solution.py:497
  21.2 19.5 %collective-permute-start.1 = (bf16[1,352,2048]{2,1,0:T(8,128)(2,1)}, bf16[1,352,2048]{2,1,0:T(8,128)(2,1)}, u32[]{:S(2)}, u32[]{:S(2)}) collective-permute-start(bf16[1,352,2048]{2,1,0:T(8,128)(2,1)} %up.5), channel_id=1, source_target_pairs={{0,1},{1,0},{2,3},{3,2},{4,5},{5,4},{6,7},{7,6},{8,9},{9,8},{10,11... | collective-permute-start | bytes 4325384 | tf_op jit(solution)/shard_map/ppermute | solution.py:497
  33.6 7.0 %collective-permute-start.2 = (bf16[1,352,2048]{2,1,0:T(8,128)(2,1)}, bf16[1,352,2048]{2,1,0:T(8,128)(2,1)}, u32[]{:S(2)}, u32[]{:S(2)}) collective-permute-start(bf16[1,352,2048]{2,1,0:T(8,128)(2,1)} %down.5), channel_id=1, source_target_pairs={{0,1},{1,0},{2,3},{3,2},{4,5},{5,4},{6,7},{7,6},{8,9},{9,8},{10,11... | collective-permute-start | bytes 4325384 | tf_op jit(solution)/shard_map/ppermute | solution.py:497
  34.8 27.8 %copy-start.6 = (bf16[256,2048]{1,0:T(8,128)(2,1)}, bf16[256,2048]{1,0:T(8,128)(2,1)S(1)}, u32[]{:S(2)}) copy-start(bf16[256,2048]{1,0:T(8,128)(2,1)S(1)} %pad_maximum_fusion.1.cot_first.refs_4_) | copy-start | bytes 3145732
  36.6 25.9 %collective-permute-start.8 = (bf16[256,2048]{1,0:T(8,128)(2,1)S(1)}, bf16[256,2048]{1,0:T(8,128)(2,1)}, u32[]{:S(2)}, u32[]{:S(2)}) collective-permute-start(bf16[256,2048]{1,0:T(8,128)(2,1)S(1)} %pad_maximum_fusion.1.cot_first.refs_4_), channel_id=1, source_target_pairs={{0,8},{1,17},{2,10},{3,19},{4,12},{5,21},{6,14},{7,23},{8,0},{9,25... | collective-permute-start | bytes 3145736 | tf_op jit(solution)/shard_map/ppermute | solution.py:497
  37.3 25.1 %collective-permute-start.5 = (bf16[272,2048]{1,0:T(8,128)(2,1)}, bf16[272,2048]{1,0:T(8,128)(2,1)}, u32[]{:S(2)}, u32[]{:S(2)}) collective-permute-start(bf16[272,2048]{1,0:T(8,128)(2,1)} %collective-permute-done.3.x_second.refs_1_), channel_id=1, source_target_pairs={{0,16},{1,9},{2,18},{3,11},{4,20},{5,13},{6,22},{7,15},{8,24},{9,1... | collective-permute-start | bytes 3342344 | tf_op jit(solution)/shard_map/ppermute | solution.py:497
  62.5 26.1 %collective-permute-start.9 = (bf16[256,2048]{1,0:T(8,128)(2,1)S(1)}, bf16[256,2048]{1,0:T(8,128)(2,1)}, u32[]{:S(2)}, u32[]{:S(2)}) collective-permute-start(bf16[256,2048]{1,0:T(8,128)(2,1)S(1)} %pad_maximum_fusion.1.cot_first.refs_4_), channel_id=1, source_target_pairs={{0,16},{1,9},{2,18},{3,11},{4,20},{5,13},{6,22},{7,15},{8,24},{9,1... | collective-permute-start | bytes 3145736 | tf_op jit(solution)/shard_map/ppermute | solution.py:497
  64.3 24.4 %collective-permute-start.10 = (bf16[256,2048]{1,0:T(8,128)(2,1)}, bf16[256,2048]{1,0:T(8,128)(2,1)}, u32[]{:S(2)}, u32[]{:S(2)}) collective-permute-start(bf16[256,2048]{1,0:T(8,128)(2,1)} %collective-permute-done.8.cot_second.refs_5_), channel_id=1, source_target_pairs={{0,16},{1,9},{2,18},{3,11},{4,20},{5,13},{6,22},{7,15},{8,24},{9,1... | collective-permute-start | bytes 3145736 | tf_op jit(solution)/shard_map/ppermute | solution.py:497
  88.7 26.2 %collective-permute-start.11 = (bf16[512,2048]{1,0:T(8,128)(2,1)}, bf16[512,2048]{1,0:T(8,128)(2,1)S(1)}, u32[]{:S(2)}, u32[]{:S(2)}) collective-permute-start(bf16[512,2048]{1,0:T(8,128)(2,1)} %get-tuple-element.63), channel_id=1, source_target_pairs={{0,16},{1,9},{2,18},{3,11},{4,20},{5,13},{6,22},{7,15},{8,24},{9,1... | collective-permute-start | bytes 6291464 | tf_op jit(solution)/shard_map/ppermute | solution.py:497
  90.4 24.5 %copy-start.3 = (bf16[512,2048]{1,0:T(8,128)(2,1)S(1)}, bf16[512,2048]{1,0:T(8,128)(2,1)}, u32[]{:S(2)}) copy-start(bf16[512,2048]{1,0:T(8,128)(2,1)} %get-tuple-element.51) | copy-start | bytes 6291460
  114.9 17.0 %copy-start.4 = (bf16[512,2048]{1,0:T(8,128)(2,1)}, bf16[512,2048]{1,0:T(8,128)(2,1)S(1)}, u32[]{:S(2)}) copy-start(bf16[512,2048]{1,0:T(8,128)(2,1)S(1)} %collective-permute-done.11) | copy-start | bytes 6291460
  115.3 14.9 %collective-permute-start.12 = (bf16[256,2048]{1,0:T(8,128)(2,1)S(1)}, bf16[256,2048]{1,0:T(8,128)(2,1)S(1)}, u32[]{:S(2)}, u32[]{:S(2)}) collective-permute-start(bf16[256,2048]{1,0:T(8,128)(2,1)S(1)} %add_convert_fusion.1), channel_id=1, source_target_pairs={{0,8},{1,17},{2,10},{3,19},{4,12},{5,21},{6,14},{7,23},{8,0},{9,25... | collective-permute-start | bytes 3145736 | tf_op jit(solution)/shard_map/ppermute | solution.py:497
  127.2 7.4 %copy-start.8 = (f32[512,1]{1,0:T(8,128)S(1)}, f32[512,1]{1,0:T(8,128)}, u32[]{:S(2)}) copy-start(f32[512,1]{1,0:T(8,128)} %get-tuple-element.91) | copy-start | bytes 6148
  130.2 26.2 %collective-permute-start.16 = (bf16[512,2048]{1,0:T(8,128)(2,1)}, bf16[512,2048]{1,0:T(8,128)(2,1)S(1)}, u32[]{:S(2)}, u32[]{:S(2)}) collective-permute-start(bf16[512,2048]{1,0:T(8,128)(2,1)} %get-tuple-element.88), channel_id=1, source_target_pairs={{0,16},{1,9},{2,18},{3,11},{4,20},{5,13},{6,22},{7,15},{8,24},{9,1... | collective-permute-start | bytes 6291464 | tf_op jit(solution)/shard_map/ppermute | solution.py:497
  131.9 54.5 %collective-permute-start.15 = (bf16[3,352,2048]{2,1,0:T(8,128)(2,1)}, bf16[3,352,2048]{2,1,0:T(8,128)(2,1)}, u32[]{:S(2)}, u32[]{:S(2)}) collective-permute-start(bf16[3,352,2048]{2,1,0:T(8,128)(2,1)} %other_grads.1), channel_id=1, source_target_pairs={{0,1},{1,0},{2,3},{3,2},{4,5},{5,4},{6,7},{7,6},{8,9},{9,8},{10,11... | collective-permute-start | bytes 12976136 | tf_op jit(solution)/shard_map/ppermute | solution.py:497
  133.0 14.7 %collective-permute-start.13 = (bf16[2,64,2048]{2,1,0:T(8,128)(2,1)}, bf16[2,64,2048]{2,1,0:T(8,128)(2,1)}, u32[]{:S(2)}, u32[]{:S(2)}) collective-permute-start(bf16[2,64,2048]{2,1,0:T(8,128)(2,1)} %bitcast.7), channel_id=1, source_target_pairs={{0,2},{1,3},{2,0},{3,1},{4,6},{5,7},{6,4},{7,5},{8,10},{9,11},{10,... | collective-permute-start | bytes 1572872 | tf_op jit(solution)/shard_map/ppermute | solution.py:497
  135.9 11.8 %collective-permute-start.21 = (f32[4,2,64]{2,0,1:T(4,128)S(1)}, f32[4,2,64]{2,0,1:T(4,128)S(1)}, u32[]{:S(2)}, u32[]{:S(2)}) collective-permute-start(f32[4,2,64]{2,0,1:T(4,128)S(1)} %copy.62), channel_id=1, source_target_pairs={{0,2},{1,3},{2,0},{3,1},{4,6},{5,7},{6,4},{7,5},{8,10},{9,11},{10,... | collective-permute-start | bytes 6152 | tf_op jit(solution)/shard_map/ppermute | solution.py:497
  156.4 19.1 %copy-start.2 = (bf16[512,2048]{1,0:T(8,128)(2,1)}, bf16[512,2048]{1,0:T(8,128)(2,1)S(1)}, u32[]{:S(2)}) copy-start(bf16[512,2048]{1,0:T(8,128)(2,1)S(1)} %collective-permute-done.16) | copy-start | bytes 6291460
  158.8 14.9 %collective-permute-start.17 = (bf16[256,2048]{1,0:T(8,128)(2,1)S(1)}, bf16[256,2048]{1,0:T(8,128)(2,1)S(1)}, u32[]{:S(2)}, u32[]{:S(2)}) collective-permute-start(bf16[256,2048]{1,0:T(8,128)(2,1)S(1)} %add_convert_fusion), channel_id=1, source_target_pairs={{0,8},{1,17},{2,10},{3,19},{4,12},{5,21},{6,14},{7,23},{8,0},{9,25... | collective-permute-start | bytes 3145736 | tf_op jit(solution)/shard_map/ppermute | solution.py:497
  161.1 12.2 %collective-permute-start.14 = (bf16[64,2048]{1,0:T(8,128)(2,1)S(1)}, bf16[64,2048]{1,0:T(8,128)(2,1)S(1)}, u32[]{:S(2)}, u32[]{:S(2)}) collective-permute-start(bf16[64,2048]{1,0:T(8,128)(2,1)S(1)} %fusion), channel_id=1, source_target_pairs={{0,4},{1,5},{2,6},{3,7},{4,0},{5,1},{6,2},{7,3},{8,12},{9,13},{10,... | collective-permute-start | bytes 786440 | tf_op jit(solution)/shard_map/ppermute | solution.py:497
  164.5 9.2 %collective-permute-start.22 = (f32[4,64]{1,0:T(4,128)S(1)}, f32[4,64]{1,0:T(4,128)S(1)}, u32[]{:S(2)}, u32[]{:S(2)}) collective-permute-start(f32[4,64]{1,0:T(4,128)S(1)} %bitcast.61), channel_id=1, source_target_pairs={{0,4},{1,5},{2,6},{3,7},{4,0},{5,1},{6,2},{7,3},{8,12},{9,13},{10,... | collective-permute-start | bytes 3080 | tf_op jit(solution)/shard_map/ppermute | solution.py:497
  173.7 7.7 %collective-permute-start.23 = (f32[2,2,64]{2,0,1:T(2,128)S(1)}, f32[2,2,64]{2,0,1:T(2,128)S(1)}, u32[]{:S(2)}, u32[]{:S(2)}) collective-permute-start(f32[2,2,64]{2,0,1:T(2,128)S(1)} %fusion.10), channel_id=1, source_target_pairs={{0,16},{1,9},{2,18},{3,11},{4,20},{5,13},{6,22},{7,15},{8,24},{9,1... | collective-permute-start | bytes 3080 | tf_op jit(solution)/shard_map/ppermute | solution.py:497
  177.1 22.3 %collective-permute-start.18 = (bf16[64,2048]{1,0:T(8,128)(2,1)S(1)}, bf16[64,2048]{1,0:T(8,128)(2,1)S(1)}, u32[]{:S(2)}, u32[]{:S(2)}) collective-permute-start(bf16[64,2048]{1,0:T(8,128)(2,1)S(1)} %get-tuple-element.100), channel_id=1, source_target_pairs={{0,4},{1,5},{2,6},{3,7},{4,0},{5,1},{6,2},{7,3},{8,12},{9,13},{10,... | collective-permute-start | bytes 786440 | tf_op jit(solution)/shard_map/ppermute | solution.py:497
  179.7 19.7 %collective-permute-start.20 = (bf16[64,2048]{1,0:T(8,128)(2,1)S(1)}, bf16[64,2048]{1,0:T(8,128)(2,1)S(1)}, u32[]{:S(2)}, u32[]{:S(2)}) collective-permute-start(bf16[64,2048]{1,0:T(8,128)(2,1)S(1)} %get-tuple-element.101), channel_id=1, source_target_pairs={{0,6},{1,7},{2,4},{3,5},{4,2},{5,3},{6,0},{7,1},{8,14},{9,15},{10,... | collective-permute-start | bytes 786440 | tf_op jit(solution)/shard_map/ppermute | solution.py:497
  181.1 18.3 %collective-permute-start.19 = (bf16[64,2048]{1,0:T(8,128)(2,1)S(1)}, bf16[64,2048]{1,0:T(8,128)(2,1)S(1)}, u32[]{:S(2)}, u32[]{:S(2)}) collective-permute-start(bf16[64,2048]{1,0:T(8,128)(2,1)S(1)} %get-tuple-element.102), channel_id=1, source_target_pairs={{0,2},{1,3},{2,0},{3,1},{4,6},{5,7},{6,4},{7,5},{8,10},{9,11},{10,... | collective-permute-start | bytes 786440 | tf_op jit(solution)/shard_map/ppermute | solution.py:497
  181.4 3.7 %collective-permute-start.24 = (f32[2,2,64]{2,0,1:T(2,128)S(1)}, f32[2,2,64]{2,0,1:T(2,128)S(1)}, u32[]{:S(2)}, u32[]{:S(2)}) collective-permute-start(f32[2,2,64]{2,0,1:T(2,128)S(1)} %fusion.11), channel_id=1, source_target_pairs={{0,8},{1,17},{2,10},{3,19},{4,12},{5,21},{6,14},{7,23},{8,0},{9,25... | collective-permute-start | bytes 3080 | tf_op jit(solution)/shard_map/ppermute | solution.py:497
  186.4 14.8 %copy-start.1 = (bf16[512,2048]{1,0:T(8,128)(2,1)S(1)}, bf16[512,2048]{1,0:T(8,128)(2,1)}, u32[]{:S(2)}) copy-start(bf16[512,2048]{1,0:T(8,128)(2,1)} %param.8) | copy-start | bytes 6291460
